TPU v7x, 128 devices: a whole 4x4x4 slice. The times are simulated.
128 devices in a mesh: row: 16 (over y, x), col: 8 (over z, core).
Axes of the slice: x: 4, y: 4, z: 4, core: 2. Of those that a mesh axis runs over, the one named last changes fastest.
Arguments:
- single: bfloat16 [6144, 768], P('row'), may hold values from -6 to 6
- pair_bias: bfloat16 [16, 6144, 6144], P(None, 'row', 'col'), may hold values from -8 to 304, as said below
- key_live: int32 [6144], P('col'), may hold values 0 or 1
- w_query: bfloat16 [768, 768], replicated, may hold values from -0.21875 to 0.21875
- w_key: bfloat16 [768, 768], replicated, may hold values from -0.21875 to 0.21875
- w_value: bfloat16 [768, 768], replicated, may hold values from -0.21875 to 0.21875
- w_gate: bfloat16 [768, 768], replicated, may hold values from -0.21875 to 0.21875
- w_out: bfloat16 [768, 768], replicated, may hold values from -0.21875 to 0.21875
- cotangent: bfloat16 [6144, 768], P('row'), may hold values from -6 to 6
Outputs:
- attended: bfloat16 [6144, 768], P('row')
- d_bias: bfloat16 [16, 6144, 6144], P(None, 'row', 'col')
- d_single: bfloat16 [6144, 768], P('row')
Inputs may be any that keep to these rules, and one draw needn't show every extreme that they name: `pair_bias`: per-head additive scores.
All inputs are finite; a program needn't handle non-finite values. No bound on the sum of `key_live` on one device may be relied on, other than what follows from the above.
Results may differ from a plain program's by a relative error of at most 0.034.
Values may be sent and summed in bfloat16 or wider, within the bound.
No kernel may reach another device: no remote copies, remote signals or barrier semaphores. Data moves between devices by JAX's collectives and lax.ppermute only.
A program may use at most 128 MiB of HBM per device.

v0:
```python
import math

import jax
import jax.numpy as jnp
from jax import lax
from jax.sharding import PartitionSpec as P


def broadcast(value, axis, source):
    kept = jnp.where(lax.axis_index(axis) == source, value, 0).astype(value.dtype)
    return lax.psum(kept, axis)


def dot_t(left, right):
    return lax.dot_general(
        left, right, (((1,), (1,)), ((), ())), preferred_element_type=jnp.float32
    )


def project(rows_in, weight):
    return jnp.dot(rows_in, weight, preferred_element_type=jnp.float32).astype(jnp.bfloat16)


def shards(single, pair_bias, key_live, w_query, w_key, w_value, w_gate, w_out, cotangent):
    rows = single.shape[0]
    width = single.shape[1]
    heads = pair_bias.shape[0]
    span = pair_bias.shape[2]
    head_size = width // heads
    scale = 1.0 / math.sqrt(head_size)
    row_index = lax.axis_index("row")
    col_index = lax.axis_index("col")
    ratio = lax.axis_size("row") // lax.axis_size("col")
    query = project(single, w_query)
    gate = jax.nn.sigmoid(jnp.dot(single, w_gate, preferred_element_type=jnp.float32))
    own_kv = jnp.concatenate([project(single, w_key), project(single, w_value)], axis=1)
    every_kv = lax.all_gather(own_kv, "row", axis=0, tiled=True)
    block_kv = lax.dynamic_slice_in_dim(every_kv, col_index * span, span, 0)
    keys = block_kv[:, :width]
    values = block_kv[:, width:]
    q_heads = query.reshape(rows, heads, head_size)
    k_heads = keys.reshape(span, heads, head_size)
    v_heads = values.reshape(span, heads, head_size)
    live = (key_live > 0)[None, None, :]
    scores = (
        jnp.einsum("ihd,jhd->hij", q_heads, k_heads, preferred_element_type=jnp.float32) * scale
    )
    scores = jnp.where(live, scores + pair_bias.astype(jnp.float32), -30000.0)
    local_top = jnp.max(scores, axis=-1)
    expo = jnp.exp(scores - local_top[..., None])
    local_total = jnp.sum(expo, axis=-1)
    local_out = jnp.einsum(
        "hij,jhd->ihd", expo.astype(jnp.bfloat16), v_heads, preferred_element_type=jnp.float32
    )
    local_out = local_out.reshape(rows, width)

    def rescale(out_flat, factor):
        return (out_flat.reshape(rows, heads, head_size) * factor.T[:, :, None]).reshape(
            rows, width
        )

    top = lax.pmax(local_top, "col")
    factor = jnp.exp(local_top - top)
    total, summed = (
        lax.psum((local_total * factor).astype(jnp.bfloat16), "col").astype(jnp.float32),
        lax.psum(rescale(local_out, factor).astype(jnp.bfloat16), "col").astype(jnp.float32),
    )
    heads_cat = rescale(summed, 1.0 / total)
    hidden = (heads_cat * gate).astype(jnp.bfloat16)
    attended = jnp.dot(hidden, w_out, preferred_element_type=jnp.float32).astype(jnp.bfloat16)
    d_hidden = dot_t(cotangent, w_out)
    d_heads = d_hidden * gate
    d_gate = (d_hidden * heads_cat * gate * (1.0 - gate)).astype(jnp.bfloat16)
    delta = jnp.sum((d_heads * heads_cat).reshape(rows, heads, head_size), axis=-1).T
    d_heads_b = d_heads.astype(jnp.bfloat16).reshape(rows, heads, head_size)
    prob = jnp.exp(scores - top[..., None]) / total[..., None]
    d_val = jnp.einsum(
        "hij,ihd->jhd", prob.astype(jnp.bfloat16), d_heads_b, preferred_element_type=jnp.float32
    )
    d_prob = jnp.einsum("ihd,jhd->hij", d_heads_b, v_heads, preferred_element_type=jnp.float32)
    d_score = (prob * (d_prob - delta[..., None])).astype(jnp.bfloat16)
    d_q = jnp.einsum("hij,jhd->ihd", d_score, k_heads, preferred_element_type=jnp.float32) * scale
    d_k = jnp.einsum("hij,ihd->jhd", d_score, q_heads, preferred_element_type=jnp.float32) * scale
    d_query = lax.psum(d_q.reshape(rows, width).astype(jnp.bfloat16), "col")
    d_kv = lax.psum(
        jnp.concatenate([d_k.reshape(span, width), d_val.reshape(span, width)], axis=1).astype(
            jnp.bfloat16
        ),
        "row",
    ).astype(jnp.float32)
    mine = lax.dynamic_slice_in_dim(d_kv, row_index % ratio * rows, rows, 0).astype(jnp.bfloat16)
    home = broadcast(mine, "col", row_index // ratio)
    d_single = dot_t(d_query, w_query) + dot_t(home[:, :width], w_key)
    d_single = d_single + dot_t(home[:, width:], w_value) + dot_t(d_gate, w_gate)
    return (attended, d_score, d_single.astype(jnp.bfloat16))


def solution(mesh):
    placed = (
        P("row", None),
        P(None, "row", "col"),
        P("col"),
        P(),
        P(),
        P(),
        P(),
        P(),
        P("row", None),
    )
    return jax.shard_map(
        shards,
        mesh=mesh,
        in_specs=placed,
        out_specs=(P("row", None), P(None, "row", "col"), P("row", None)),
        check_vma=False,
    )
```

profile of v0, /device:TPU:1, one launch (start us, length us, event | category | flops | bytes accessed | tf_op | source)
XLA Modules:
  0.0 463.1 jit_solution(4118811613400788482)
XLA Ops:
  7.2 2.2 convolution_convert_fusion.2
  10.1 1.1 pad_maximum_fusion.1
  11.3 1.2 copy-done.15
  13.8 122.7 %all-gather.2.cloned.1.call-done = bf16[6144,1536]{1,0:T(8,128)(2,1)} async-done(((bf16[384,1536]{1,0:T(8,128)(2,1)}), bf16[6144,1536]{1,0:T(8,128)(2,1)}) %all-gather.2.cloned.1.call-update) | async-done | bytes 18874384 | tf_op jit(solution)/shard_map/all_gather | solution.py:37
  136.5 3.2 fusion.30
  139.7 1.6 copy.24
  141.3 11.3 %fusion.31 = (f32[16,384]{1,0:T(8,128)S(1)}, f32[16,384,768]{2,1,0:T(8,128)}) fusion(bf16[16,384,768]{2,1,0:T(8,128)(2,1)} %param.10, bf16[384,16,48]{0,2,1:T(8,128)(2,1)S(1)} %bitcast.58, bf16[768,16,48]{0,2,1:T(8,128)(2,1)S(1)} %bitcast.55, pred[768]{0:T(1024)(128)(4,1)S(1)} %broadcast_compare_fusion), kind=kOutput, calls=%fused_computation.49 | convolution fusion | flops 476571648 | bytes 30106368 | tf_op jit(solution)/shard_map/ihd,jhd->hij/dot_general | solution.py:46
  152.6 23.5 %pmax.7 = f32[16,384]{1,0:T(8,128)} all-reduce(f32[16,384]{1,0:T(8,128)S(1)} %get-tuple-element.11), channel_id=1, replica_groups=mesh['row'=16,'col'=8] {'col'}, use_global_device_ids=true, to_apply=%region_1.2 | all-reduce | flops 6144 | bytes 49152 | tf_op jit(solution)/shard_map/pmax | solution.py:62
  176.1 8.9 %fusion = f32[16,384]{1,0:T(8,128)} fusion(f32[16,384,768]{2,1,0:T(8,128)} %get-tuple-element.12, f32[16,384]{1,0:T(8,128)} %copy-done.20), kind=kLoop, calls=%fused_computation.4 | loop fusion | flops 9431040 | bytes 18923520 | tf_op jit(solution)/shard_map/reduce_sum | solution.py:51
  186.6 8.0 %fusion.20 = bf16[384,16,48]{0,2,1:T(8,128)(2,1)S(1)} fusion(bf16[768,16,48]{0,2,1:T(8,128)(2,1)S(1)} %bitcast.60, f32[16,384,768]{2,1,0:T(8,128)} %get-tuple-element.12, f32[16,384]{1,0:T(8,128)} %copy-done.20, f32[384,16]{0,1:T(8,128)S(1)} %get-tuple-element.9), kind=kOutput, calls=%fused_computation.25 | convolution fusion | flops 463011840 | bytes 20692992 | tf_op jit(solution)/shard_map/hij,jhd->ihd/dot_general | solution.py:52
  195.8 2.0 fusion.12
  197.9 23.8 %psum.36 = bf16[16,384]{1,0:T(8,128)(2,1)S(1)} all-reduce(bf16[16,384]{1,0:T(8,128)(2,1)S(1)} %get-tuple-element.10), channel_id=1, replica_groups=mesh['row'=16,'col'=8] {'col'}, use_global_device_ids=true, to_apply=%region_4.5 | all-reduce | flops 6144 | bytes 24576 | tf_op jit(solution)/shard_map/psum | solution.py:65
  223.3 1.6 copy.26
  225.0 30.3 %all-reduce.5.cloned.1.call-done = bf16[384,768]{1,0:T(8,128)(2,1)} async-done(((bf16[384,768]{1,0:T(8,128)(2,1)}), bf16[384,768]{1,0:T(8,128)(2,1)}) %all-reduce.5.cloned.1.call-update) | async-done | bytes 589840 | tf_op jit(solution)/shard_map/psum | solution.py:66
  255.3 3.5 multiply_convert_fusion.6
  258.8 2.7 copy.28
  261.6 2.3 copy.27
  263.8 1.4 reduce_sum.19
  265.3 9.8 %fusion.7 = bf16[16,48,768]{2,1,0:T(8,128)(2,1)S(1)} fusion(bf16[384,16,48]{0,2,1:T(8,128)(2,1)} %bitcast.67, f32[16,384]{1,0:T(8,128)S(1)} %copy-done.23, f32[16,384,768]{2,1,0:T(8,128)} %get-tuple-element.12, f32[16,384]{1,0:T(8,128)S(1)} %copy-done.22), kind=kOutput, calls=%fused_computation.13 | convolution fusion | flops 467730432 | bytes 20692992 | tf_op jit(solution)/shard_map/hij,ihd->jhd/dot_general | solution.py:77
  275.5 1.2 slice-done.4
  277.1 7.5 %multiply_convert_fusion = bf16[16,384,768]{2,1,0:T(8,128)(2,1)} fusion(f32[16,384]{1,0:T(8,128)S(1)} %bitcast.69, bf16[384,16,48]{0,2,1:T(8,128)(2,1)S(1)} %bitcast.68, bf16[768,16,48]{0,2,1:T(8,128)(2,1)S(1)} %bitcast.61, f32[16,384]{1,0:T(8,128)S(1)} %copy-done.23, f32[16,384,768]{2,1,0:T(8,128)S(1)} %bitcast.54, f32[16,384]{1,0:T(8,128)S(1)} %copy-done.22), kind=kOutput, calls=%fused_computation | convolution fusion | flops 476577792 | bytes 30154752 | tf_op jit(solution)/shard_map/ihd,jhd->hij/dot_general | solution.py:80
  284.5 5.4 %multiply_convert_fusion.1 = bf16[16,48,768]{2,1,0:T(8,128)(2,1)S(1)} fusion(bf16[384,16,48]{0,2,1:T(8,128)(2,1)S(1)} %bitcast.59, bf16[16,384,768]{2,1,0:T(8,128)(2,1)} %multiply_convert_fusion), kind=kOutput, calls=%fused_computation.12 | convolution fusion | flops 454164480 | bytes 11206656 | tf_op jit(solution)/shard_map/hij,ihd->jhd/dot_general | solution.py:83
  290.0 1.6 pad_maximum_fusion
  291.7 1.2 copy-done.4
  292.9 7.2 %fusion.19 = bf16[16,48,384]{2,1,0:T(8,128)(2,1)} fusion(bf16[768,16,48]{0,2,1:T(8,128)(2,1)S(1)} %bitcast.56, bf16[16,384,768]{2,1,0:T(8,128)(2,1)} %multiply_convert_fusion), kind=kOutput, calls=%fused_computation.24 | convolution fusion | flops 453574656 | bytes 11206656 | tf_op jit(solution)/shard_map/hij,jhd->ihd/dot_general | solution.py:82
  300.1 83.3 %all-reduce.7.cloned.1.call-done = bf16[768,1536]{0,1:T(8,128)(2,1)} async-done(((bf16[768,1536]{0,1:T(8,128)(2,1)}), bf16[768,1536]{0,1:T(8,128)(2,1)}) %all-reduce.7.cloned.1.call-update) | async-done | bytes 2359312 | tf_op jit(solution)/shard_map/psum | solution.py:85
  383.4 2.6 fusion.24
  386.1 1.2 copy-done.2
  387.3 2.5 convolution_convert_fusion
  389.8 59.7 %all-reduce.9.cloned.1.call-done = (bf16[384,768]{0,1:T(8,128)(2,1)}, bf16[384,1536]{0,1:T(8,128)(2,1)}) async-done(((bf16[384,768]{0,1:T(8,128)(2,1)}, bf16[384,1536]{0,1:T(8,128)(2,1)}), (bf16[384,768]{0,1:T(8,128)(2,1)}, bf16[384,1536]{0,1:T(8,128)(2,1)})) %all-reduce.9.cloned.1.call-update) | async-done | bytes 1769488 | tf_op jit(solution)/shard_map/psum | solution.py:84
  449.6 2.3 fusion.32
  455.0 1.6 fusion.23
  (81 shorter events, 10.4 us)
Async XLA Ops:
  7.2 248.2 %copy-start = (bf16[768,768]{1,0:T(8,128)(2,1)S(1)}, bf16[768,768]{1,0:T(8,128)(2,1)}, u32[]{:S(2)}) copy-start(bf16[768,768]{1,0:T(8,128)(2,1)} %param.16) | copy-start | bytes 3538948
  7.2 2.3 copy-start.25
  7.2 2.3 copy-start.16
  7.2 129.3 %all-gather.2.cloned.1.call-start = ((), (), s32[]{:S(2)}) async-start(), calls=%async_computation | async-start | bytes 20054016 | tf_op jit(solution)/shard_map/all_gather | solution.py:37
  11.2 1.3 copy-start.15
  11.3 244.0 %all-reduce.5.cloned.1.call-start = ((), (), s32[]{:S(2)}) async-start(), calls=%async_computation.1 | async-start | bytes 1179648 | tf_op jit(solution)/shard_map/psum | solution.py:66
  13.5 127.9 %copy-start.7 = (bf16[384,768]{0,1:T(8,128)(2,1)}, bf16[384,768]{0,1:T(8,128)(2,1)S(1)}, u32[]{:S(2)}) copy-start(bf16[384,768]{0,1:T(8,128)(2,1)S(1)} %copy.23) | copy-start | bytes 1769476
  141.3 11.3 %copy-start.3 = (bf16[768,768]{0,1:T(8,128)(2,1)}, bf16[768,768]{0,1:T(8,128)(2,1)S(1)}, u32[]{:S(2)}) copy-start(bf16[768,768]{0,1:T(8,128)(2,1)S(1)} %copy.24) | copy-start | bytes 3538948
  152.6 23.5 %copy-start.20 = (f32[16,384]{1,0:T(8,128)}, f32[16,384]{1,0:T(8,128)S(1)}, u32[]{:S(2)}) copy-start(f32[16,384]{1,0:T(8,128)S(1)} %get-tuple-element.11) | copy-start | bytes 73732
  176.1 9.0 %copy-start.12 = (bf16[768,768]{1,0:T(8,128)(2,1)S(1)}, bf16[768,768]{1,0:T(8,128)(2,1)}, u32[]{:S(2)}) copy-start(bf16[768,768]{1,0:T(8,128)(2,1)} %get-tuple-element.5) | copy-start | bytes 3538948
  185.7 9.0 %copy-start.10 = (bf16[768,768]{0,1:T(8,128)(2,1)}, bf16[768,768]{0,1:T(8,128)(2,1)S(1)}, u32[]{:S(2)}) copy-start(bf16[768,768]{0,1:T(8,128)(2,1)S(1)} %copy.22) | copy-start | bytes 3538948
  195.8 187.6 %all-reduce.7.cloned.1.call-start = ((), (), s32[]{:S(2)}) async-start(), calls=%async_computation.2 | async-start | bytes 4718592 | tf_op jit(solution)/shard_map/psum | solution.py:85
  197.9 57.4 %copy-start.5 = (f32[384,768]{1,0:T(8,128)}, f32[384,768]{1,0:T(8,128)S(1)}, u32[]{:S(2)}) copy-start(f32[384,768]{1,0:T(8,128)S(1)} %fusion.12) | copy-start | bytes 3538948
  225.0 33.8 %copy-start.1 = (f32[384,768]{1,0:T(8,128)}, f32[384,768]{1,0:T(8,128)S(1)}, u32[]{:S(2)}) copy-start(f32[384,768]{1,0:T(8,128)S(1)} %copy.26) | copy-start | bytes 3538948
  261.6 3.6 copy-start.22
  261.6 3.6 copy-start.23
  261.6 13.5 %slice-start = ((s8[18874368]{0:T(1024)(128)(4,1)}), s8[2097152]{0:T(1024)(128)(4,1)S(1)}, s32[]{:S(2)}) async-start(s8[18874368]{0:T(1024)(128)(4,1)} %bitcast.53), calls=%async_computation.4 | async-start | bytes 4194304
  265.2 9.9 %slice-start.1 = ((s8[18874368]{0:T(1024)(128)(4,1)}), s8[4194304]{0:T(1024)(128)(4,1)S(1)}, s32[]{:S(2)}) async-start(s8[18874368]{0:T(1024)(128)(4,1)} %bitcast.53), calls=%async_computation.5 | async-start | bytes 8388608
  265.2 9.9 %slice-start.2 = ((s8[18874368]{0:T(1024)(128)(4,1)}), s8[4194304]{0:T(1024)(128)(4,1)S(1)}, s32[]{:S(2)}) async-start(s8[18874368]{0:T(1024)(128)(4,1)} %bitcast.53), calls=%async_computation.6 | async-start | bytes 8388608
  265.2 10.2 %slice-start.3 = ((s8[18874368]{0:T(1024)(128)(4,1)}), s8[4194304]{0:T(1024)(128)(4,1)S(1)}, s32[]{:S(2)}) async-start(s8[18874368]{0:T(1024)(128)(4,1)} %bitcast.53), calls=%async_computation.7 | async-start | bytes 8388608
  265.3 11.4 %slice-start.4 = ((s8[18874368]{0:T(1024)(128)(4,1)}), s8[4194304]{0:T(1024)(128)(4,1)S(1)}, s32[]{:S(2)}) async-start(s8[18874368]{0:T(1024)(128)(4,1)} %bitcast.53), calls=%async_computation.8 | async-start | bytes 8388608
  265.3 11.7 %copy-start.11 = (bf16[768,768]{0,1:T(8,128)(2,1)S(1)}, bf16[768,768]{0,1:T(8,128)(2,1)}, u32[]{:S(2)}) copy-start(bf16[768,768]{0,1:T(8,128)(2,1)} %copy-done.10) | copy-start | bytes 3538948
  265.3 11.8 %copy-start.21 = (bf16[384,768]{0,1:T(8,128)(2,1)S(1)}, bf16[384,768]{0,1:T(8,128)(2,1)}, u32[]{:S(2)}) copy-start(bf16[384,768]{0,1:T(8,128)(2,1)} %copy.27) | copy-start | bytes 1769476
  277.1 7.5 %copy-start.8 = (bf16[384,768]{0,1:T(8,128)(2,1)S(1)}, bf16[384,768]{0,1:T(8,128)(2,1)}, u32[]{:S(2)}) copy-start(bf16[384,768]{0,1:T(8,128)(2,1)} %copy-done.7) | copy-start | bytes 1769476
  291.6 158.0 %all-reduce.9.cloned.1.call-start = ((), (), s32[]{:S(2)}) async-start(), calls=%async_computation.3 | async-start | bytes 3538944 | tf_op jit(solution)/shard_map/psum | solution.py:84
  383.4 2.6 copy-start.6
  386.0 1.3 copy-start.2
  449.6 2.3 copy-start.17
  449.6 2.3 copy-start.19
  451.9 1.3 copy-start.18
  453.1 1.5 copy-start.13
  453.1 1.8 copy-start.14
  (4 other events, 4.2 us)
Sparse Core Ops, SparseCore 0:
  11.4 125.0 all-gather.1
  195.9 59.3 all-reduce.4
  291.7 91.6 all-reduce.6
  386.5 63.0 all-reduce.8
where the time goes:
time: 465 us; the launch traced here: 463 us
  waiting for transfers between devices  296 us (64%)
  matrix products  66.1 us (14%)
  blocking collectives  47.3 us (10%)
  local copies, waits for them, and re-layouts  22.1 us (5%)
  other arithmetic  17.1 us (4%)
  between operations  14.2 us (3%)
    all_gather x1, waiting for transfers between devices, shards(): every_kv = lax.all_gather(own_kv, 'row', axis=0, tiled=True)  123 us
    psum x1, waiting for transfers between devices, shards(): lax.psum(jnp.concatenate([d_k.reshape(span, width), d_val.reshape(span, w...  83.3 us
    psum x1, waiting for transfers between devices, shards(): d_query = lax.psum(d_q.reshape(rows, width).astype(jnp.bfloat16), 'col')  59.7 us
    psum x1, waiting for transfers between devices, shards(): lax.psum(rescale(local_out, factor).astype(jnp.bfloat16), 'col')  30.3 us
    psum x1, blocking collectives, shards(): lax.psum((local_total * factor).astype(jnp.bfloat16), 'col')  23.8 us
    pmax x1, blocking collectives, shards(): top = lax.pmax(local_top, 'col')  23.5 us
    dot_general x1, matrix products, shards(): jnp.einsum('ihd,jhd->hij', q_heads, k_heads, preferred_element_type=jnp.f...  11.3 us
    dot_general x1, matrix products, shards(): jnp.einsum('hij,ihd->jhd', prob.astype(jnp.bfloat16), d_heads_b, preferre...  9.82 us
  transfers between devices with their start and end apart: 4, of which 4 were waited for; matrix products, arithmetic and copies ran while one was open for 3% of the time, Pallas kernels for 0%

commit v1 on v0

v1 whole, which is shorter than its diff:
```python
import functools
import math

import jax
import jax.numpy as jnp
from jax import lax
from jax.experimental import pallas as pl
from jax.experimental.pallas import tpu as pltpu
from jax.sharding import PartitionSpec as P

HEADS = 16
HD = 48
SLOT = 64
PAIRS = HEADS // 2
WIDE = HEADS * SLOT
LOG2E = math.log2(math.e)
LN2 = math.log(2.0)
ROWS, COLS, SIDE = 16, 8, 4
VMEM = 56 * 1024 * 1024
F32, BF16 = jnp.float32, jnp.bfloat16


def nt(left, right):
    return lax.dot_general(left, right, (((1,), (1,)), ((), ())), preferred_element_type=F32)


def nn(left, right):
    return jnp.dot(left, right, preferred_element_type=F32)


def tn(left, right):
    return lax.dot_general(left, right, (((0,), (0,)), ((), ())), preferred_element_type=F32)


def lane_of(shape):
    return lax.broadcasted_iota(jnp.int32, shape, len(shape) - 1)


def along_x(k):
    return [(y * SIDE + x, y * SIDE + (x + k) % SIDE) for y in range(SIDE) for x in range(SIDE)]


def along_y(k):
    return [(y * SIDE + x, (y + k) % SIDE * SIDE + x) for y in range(SIDE) for x in range(SIDE)]


def along_col(k):
    return [(c, (c + k) % COLS) for c in range(COLS)]


def home_to_block():
    half = ROWS // 2
    return [
        (row * COLS + col, ((row % 2) * half + col) * COLS + row // 2)
        for row in range(ROWS)
        for col in range(COLS)
    ]


def params(**more):
    return pltpu.CompilerParams(vmem_limit_bytes=VMEM, **more)


def whole(count):
    return [pl.BlockSpec(memory_space=pltpu.VMEM)] * count


SCALAR = pl.BlockSpec(memory_space=pltpu.SMEM)


def place_kernel(at_ref, *refs):
    *pieces, out = refs
    size = pieces[0].shape[0]
    for k, piece in enumerate(pieces):
        out[pl.ds(pl.multiple_of(at_ref[k], size), size), :] = piece[...]


def place(pieces, at):
    rows = sum(p.shape[0] for p in pieces)
    return pl.pallas_call(
        place_kernel,
        out_shape=jax.ShapeDtypeStruct((rows, pieces[0].shape[1]), pieces[0].dtype),
        in_specs=[SCALAR] + whole(len(pieces)),
        out_specs=pl.BlockSpec(memory_space=pltpu.VMEM),
        compiler_params=params(),
    )(at, *pieces)


def project_kernel(at_ref, *refs):
    *pieces, wk_ref, wv_ref, k_ref, v_ref = refs
    size = pieces[0].shape[0]
    spare = lane_of((size, WIDE)) % SLOT >= HD
    for n, piece in enumerate(pieces):
        rows = pl.ds(pl.multiple_of(at_ref[n], size), size)
        k_ref[rows, :] = nn(piece[...], wk_ref[...]).astype(BF16)
        v_ref[rows, :] = jnp.where(spare, 1.0, nn(piece[...], wv_ref[...])).astype(BF16)


def project(pieces, at, wk, wv):
    span = sum(p.shape[0] for p in pieces)
    shape = jax.ShapeDtypeStruct((span, WIDE), BF16)
    return pl.pallas_call(
        project_kernel,
        out_shape=(shape, shape),
        in_specs=[SCALAR] + whole(len(pieces) + 2),
        out_specs=tuple(whole(2)),
        compiler_params=params(),
    )(at, *pieces, wk, wv)


def forward_kernel(bias_ref, q_ref, k_ref, v_ref, live_ref, dead_ref, row_ref, dh_ref, expo_ref, acc_ref, stats_ref):
    pair = pl.program_id(0)
    rows = q_ref.shape[0]
    lane = lane_of((rows, 2 * SLOT))
    keys = k_ref[...] * live_ref[...] + dead_ref[...]
    values = v_ref[...]
    halves = []
    for i in range(2):
        mine = lane // SLOT == i
        query = jnp.where(mine, q_ref[...], 0)
        scores = nt(query, keys) + bias_ref[i].astype(F32) * row_ref[0:1, :]
        top = jnp.max(scores, axis=-1, keepdims=True)
        expo = jnp.exp2(scores - top).astype(BF16)
        expo_ref[i] = expo
        out = nn(expo, values)
        inner = jnp.where(mine & (lane % SLOT < HD), out * dh_ref[...], 0.0)
        inner = jnp.sum(inner, axis=-1, keepdims=True)
        out = jnp.where(lane % SLOT == HD + 1, top, out)
        halves.append(jnp.where(lane % SLOT == HD + 2, inner, out))
    acc = jnp.where(lane < SLOT, halves[0], halves[1])
    acc_ref[...] = acc
    turned = acc.T
    for i in range(2):
        for stat in range(3):
            spot = i * SLOT + HD + stat
            stats_ref[pl.ds(stat * HEADS + 2 * pair + i, 1), :] = turned[spot : spot + 1, :]


def forward(bias, q, k, v, live, dead, row, dh):
    rows, span = bias.shape[1:]
    wide = lambda n: pl.BlockSpec((n, 2 * SLOT), lambda p: (0, p))
    still = lambda *s: pl.BlockSpec(s, lambda p: (0,) * len(s))
    tile = pl.BlockSpec((2, rows, span), lambda p: (p, 0, 0))
    return pl.pallas_call(
        forward_kernel,
        grid=(PAIRS,),
        out_shape=(
            jax.ShapeDtypeStruct((HEADS, rows, span), BF16),
            jax.ShapeDtypeStruct((rows, WIDE), F32),
            jax.ShapeDtypeStruct((3 * HEADS, rows), F32),
        ),
        in_specs=[tile, wide(rows), wide(span), wide(span), still(span, 2 * SLOT), still(span, 2 * SLOT), still(8, span), wide(rows)],
        out_specs=(tile, wide(rows), still(3 * HEADS, rows)),
        compiler_params=params(),
        cost_estimate=pl.CostEstimate(flops=4 * HEADS * rows * span * 256, bytes_accessed=4 * HEADS * rows * span, transcendentals=HEADS * rows * span),
    )(bias, q, k, v, live, dead, row, dh)


def combine_kernel(at_ref, *refs):
    stats, (acc_ref, dh_ref, dhf_ref), pieces = refs[:COLS], refs[COLS : COLS + 3], refs[COLS + 3 : -1]
    own_ref = refs[-1]
    rows = acc_ref.shape[0]
    tops = [s[HEADS : 2 * HEADS, :] for s in stats]
    top = functools.reduce(jnp.maximum, tops)
    total = jnp.zeros_like(top)
    inner = jnp.zeros_like(top)
    for s, t in zip(stats, tops):
        weight = jnp.exp2(t - top)
        total += weight * s[:HEADS, :]
        inner += weight * s[2 * HEADS :, :]
    factor = jnp.exp2(tops[0] - top) / total
    shift = -factor * (inner / total)
    both = jnp.concatenate([factor, shift, jnp.zeros((128 - 2 * HEADS, rows), F32)], axis=0).T
    source = lax.broadcasted_iota(jnp.int32, (128, WIDE), 0)
    lane = lane_of((128, WIDE))
    head, spot = lane // SLOT, lane % SLOT
    spread = jnp.zeros((rows, WIDE), F32)
    for part in range(3):
        rounded = both.astype(BF16)
        both = both - rounded.astype(F32)
        pick = (source == head) & (spot < HD) | (source == head + HEADS) & (spot == HD + part)
        spread += nn(rounded, pick.astype(BF16))
    dhf_ref[...] = (spread * dh_ref[...]).astype(BF16)
    own_ref[...] = jnp.where(lane_of((rows, WIDE)) % SLOT < HD, acc_ref[...] * spread, 0.0)
    size = rows // COLS
    for k, piece in enumerate(pieces):
        piece[...] = own_ref[pl.ds(pl.multiple_of(at_ref[k], size), size), :].astype(BF16)


def combine(at, stats, acc, dh):
    rows = acc.shape[0]
    return pl.pallas_call(
        combine_kernel,
        out_shape=[jax.ShapeDtypeStruct((rows, WIDE), BF16)] + [jax.ShapeDtypeStruct((rows // COLS, WIDE), BF16)] * COLS,
        in_specs=[SCALAR] + whole(COLS + 2),
        out_specs=whole(COLS + 1),
        scratch_shapes=[pltpu.VMEM((rows, WIDE), F32)],
        compiler_params=params(),
    )(at, *stats, acc, dh)


def backward_kernel(yat_ref, cat_ref, expo_ref, dhf_ref, q_ref, k_ref, v_ref, wq_ref, wk_ref, wv_ref, dbias_ref, *rest):
    kv_out, q_out, (kv_sum, q_sum) = rest[:SIDE], rest[SIDE : SIDE + COLS], rest[SIDE + COLS :]
    pair = pl.program_id(0)
    rows, span = expo_ref.shape[1:]
    lane = lane_of((rows, 2 * SLOT))
    keys, values = k_ref[...], v_ref[...]
    d_q, d_k, d_v = [], 0.0, 0.0
    for i in range(2):
        mine = lane // SLOT == i
        d_head = jnp.where(mine, dhf_ref[...], 0)
        query = jnp.where(mine & (lane % SLOT < HD), q_ref[...], 0)
        expo = expo_ref[i]
        d_score = (expo.astype(F32) * nt(d_head, values)).astype(BF16)
        dbias_ref[i] = d_score
        d_q.append(nn(d_score, keys))
        d_k += tn(d_score, query)
        d_v += tn(expo, d_head)
    d_q = (jnp.where(lane < SLOT, d_q[0], d_q[1]) * (1.0 / math.sqrt(HD))).astype(BF16)
    d_kv = jnp.concatenate([(d_k * LN2).astype(BF16), d_v.astype(BF16)], axis=1)
    w_kv = jnp.concatenate([wk_ref[...], wv_ref[...]], axis=1)
    to_kv, to_q = nt(d_kv, w_kv), nt(d_q, wq_ref[...])

    @pl.when(pair == 0)
    def _():
        kv_sum[...] = to_kv
        q_sum[...] = to_q

    @pl.when(pair > 0)
    def _():
        kv_sum[...] += to_kv
        q_sum[...] += to_q

    @pl.when(pair == PAIRS - 1)
    def _():
        for sums, at, outs in ((kv_sum, yat_ref, kv_out), (q_sum, cat_ref, q_out)):
            size = outs[0].shape[0]
            for n, out in enumerate(outs):
                out[...] = sums[pl.ds(pl.multiple_of(at[n], size), size), :].astype(BF16)


def backward(yat, cat, expo, dhf, q, k, v, wq, wk, wv):
    rows, span = expo.shape[1:]
    width = wq.shape[0]
    wide = lambda n: pl.BlockSpec((n, 2 * SLOT), lambda p: (0, p))
    still = lambda *s: pl.BlockSpec(s, lambda p: (0,) * len(s))
    tile = pl.BlockSpec((2, rows, span), lambda p: (p, 0, 0))
    return pl.pallas_call(
        backward_kernel,
        grid=(PAIRS,),
        out_shape=[jax.ShapeDtypeStruct(expo.shape, BF16)]
        + [jax.ShapeDtypeStruct((span // SIDE, width), BF16)] * SIDE
        + [jax.ShapeDtypeStruct((rows // COLS, width), BF16)] * COLS,
        in_specs=[SCALAR, SCALAR, tile, wide(rows), wide(rows), wide(span), wide(span), wide(width), wide(width), wide(width)],
        out_specs=[tile] + [still(span // SIDE, width)] * SIDE + [still(rows // COLS, width)] * COLS,
        scratch_shapes=[pltpu.VMEM((span, width), F32), pltpu.VMEM((rows, width), F32)],
        compiler_params=params(),
        cost_estimate=pl.CostEstimate(flops=8 * HEADS * rows * span * 256, bytes_accessed=4 * HEADS * rows * span, transcendentals=0),
    )(yat, cat, expo, dhf, q, k, v, wq, wk, wv)


def reduce_kernel(at_ref, *refs):
    terms, outs, total = refs[:SIDE], refs[SIDE:-1], refs[-1]
    total[...] = functools.reduce(jnp.add, [t[...].astype(F32) for t in terms])
    size = outs[0].shape[0]
    for n, out in enumerate(outs):
        out[...] = total[pl.ds(pl.multiple_of(at_ref[n], size), size), :].astype(BF16)


def reduce_split(at, terms):
    rows, width = terms[0].shape
    return pl.pallas_call(
        reduce_kernel,
        out_shape=[jax.ShapeDtypeStruct((rows // SIDE, width), BF16)] * SIDE,
        in_specs=[SCALAR] + whole(SIDE),
        out_specs=whole(SIDE),
        scratch_shapes=[pltpu.VMEM((rows, width), F32)],
        compiler_params=params(),
    )(at, *terms)


def finish_kernel(at_ref, *refs):
    pieces, (gate_ref, dh_ref, wo_ref, wg_ref, att_ref, dg_ref) = refs[:COLS], refs[COLS:]
    size = pieces[0].shape[0]
    rows = pl.ds(pl.multiple_of(at_ref[0], size), size)
    out = functools.reduce(jnp.add, [p[...].astype(F32) for p in pieces])
    gate = gate_ref[rows, :]
    att_ref[...] = nn((out * gate).astype(BF16), wo_ref[...]).astype(BF16)
    d_gate = (dh_ref[rows, :] * out * (1.0 - gate)).astype(BF16)
    dg_ref[...] = nt(d_gate, wg_ref[...])


def finish(at, pieces, gate, dh, wo, wg):
    size, width = pieces[0].shape[0], wo.shape[1]
    return pl.pallas_call(
        finish_kernel,
        out_shape=[jax.ShapeDtypeStruct((size, width), BF16), jax.ShapeDtypeStruct((size, width), F32)],
        in_specs=[SCALAR] + whole(COLS + 4),
        out_specs=whole(2),
        compiler_params=params(),
    )(at, *pieces, gate, dh, wo, wg)


def send(pieces, axis, way):
    return [pieces[0]] + [lax.ppermute(pieces[k], axis, way(k)) for k in range(1, len(pieces))]


def widen(weight):
    split = weight.reshape(weight.shape[0], HEADS, HD)
    return jnp.pad(split, ((0, 0), (0, 0), (0, SLOT - HD))).reshape(weight.shape[0], WIDE)


def shards(single, pair_bias, key_live, w_query, w_key, w_value, w_gate, w_out, cotangent):
    rows, width = single.shape
    span = pair_bias.shape[2]
    piece = rows // COLS
    row_index, col_index = lax.axis_index("row"), lax.axis_index("col")
    y, x = row_index // SIDE, row_index % SIDE
    steps4, steps8 = jnp.arange(SIDE), jnp.arange(COLS)
    x_from, x_to = (x - steps4) % SIDE * (span // ROWS), (x + steps4) % SIDE * (span // ROWS)
    y_from, y_to = (y - steps4) % SIDE * (span // SIDE), (y + steps4) % SIDE * (span // SIDE)
    c_from, c_to = (col_index - steps8) % COLS * piece, (col_index + steps8) % COLS * piece

    mine = lax.dynamic_slice_in_dim(single, col_index * piece, piece, 0)
    mine = lax.ppermute(mine, ("row", "col"), home_to_block())
    line = place(send([mine] * SIDE, "row", along_x), x_from)
    lines = send([line] * SIDE, "row", along_y)

    wq, wk, wv, wg = (widen(w) for w in (w_query, w_key, w_value, w_gate))
    wo = jnp.pad(w_out.reshape(HEADS, HD, width), ((0, 0), (0, SLOT - HD), (0, 0))).reshape(WIDE, width)
    spot = lane_of((1, WIDE)) % SLOT
    scale = LOG2E / math.sqrt(HD)
    q = jnp.where((spot >= HD) & (spot < HD + 3), 1.0, nn(single, wq) * scale).astype(BF16)
    gate = jax.nn.sigmoid(nn(single, wg))
    dh = jnp.where(spot >= HD, 1.0, nt(cotangent, wo) * gate)
    alive = key_live > 0
    row = jnp.broadcast_to(jnp.where(alive, LOG2E, 0.0).astype(F32)[None, :], (8, span))
    live = jnp.broadcast_to(alive[:, None], (span, 2 * SLOT)).astype(BF16)
    rest, fill = jnp.float32(-30000.0 * LOG2E), jnp.zeros((1, 2 * SLOT), F32)
    for n in range(3):
        part = rest.astype(BF16).astype(F32)
        rest = rest - part
        fill = jnp.where(spot[:, : 2 * SLOT] == HD + n, part, fill)
    dead = jnp.where(alive[:, None], 0.0, fill).astype(BF16)

    k, v = project(lines, y_from, wk, wv)
    expo, acc, stats = forward(pair_bias, q, k, v, live, dead, row, dh)
    all_stats = send([stats] * COLS, "col", along_col)
    dhf, *parts = combine(c_to, all_stats, acc, dh)
    parts = send(parts, "col", along_col)
    d_bias, *outs = backward(y_to, c_to, expo, dhf, q, k, v, wq, wk, wv)
    attended, from_gate = finish(c_to, parts, gate, dh, wo, wg)
    attended = place(send([attended] * COLS, "col", along_col), c_from)
    from_kv, from_q = outs[:SIDE], outs[SIDE:]
    from_kv = reduce_split(x_to, send(from_kv, "row", along_y))
    from_kv = send(from_kv, "row", along_x)
    from_kv = functools.reduce(jnp.add, [p.astype(F32) for p in from_kv]).astype(BF16)
    back = [(b, a) for a, b in home_to_block()]
    from_kv = lax.ppermute(from_kv, ("row", "col"), back)
    from_q = send(from_q, "col", along_col)
    d_single = functools.reduce(jnp.add, [p.astype(F32) for p in from_q])
    d_single = (d_single + from_kv.astype(F32) + from_gate).astype(BF16)
    d_single = place(send([d_single] * COLS, "col", along_col), c_from)
    return (attended, d_bias, d_single)


def solution(mesh):
    placed = (
        P("row", None),
        P(None, "row", "col"),
        P("col"),
        P(),
        P(),
        P(),
        P(),
        P(),
        P("row", None),
    )
    return jax.shard_map(
        shards,
        mesh=mesh,
        in_specs=placed,
        out_specs=(P("row", None), P(None, "row", "col"), P("row", None)),
        check_vma=False,
    )
```

time: 465 us -> 199 us (0.43)
  waiting for transfers between devices: 296 us -> 27.6 us
  starting transfers between devices: 0.16 us -> 73.9 us
  Pallas kernels: 0 us -> 59.2 us
  matrix products: 66.1 us -> 7.41 us
  blocking collectives: 47.3 us -> 0 us
  between operations: 14.2 us -> 1.25 us
  other arithmetic: 17.1 us -> 6.18 us
    psum x3 -> x0, waiting for transfers between devices: 173 us -> none  [the longest x1 83.3 us: shards(): lax.psum(jnp.concatenate([d_k.reshape(span, width), d_val.reshape(span, w...]
    all_gather x1 -> x0, waiting for transfers between devices: 123 us -> none  [shards(): every_kv = lax.all_gather(own_kv, 'row', axis=0, tiled=True)]
    ppermute x0 -> x49, starting transfers between devices: none -> 73.9 us  [the longest x47 66.9 us: send(): lax.ppermute(pieces[k], axis, way(k))]
    pallas_call x0 -> x9, Pallas kernels: none -> 59.2 us  [the longest x1 21.9 us: backward(): pl.pallas_call(backward_kernel, grid=(PAIRS,), out_shape=[jax.ShapeDtypeS...]
    dot_general x16 -> x3, matrix products: 66.1 us -> 7.41 us  [the longest x2 3.92 us: nn(): return jnp.dot(left, right, preferred_element_type=F32)]
    ppermute x0 -> x49, waiting for transfers between devices: none -> 27.6 us  [the longest x47 27.6 us: send(): lax.ppermute(pieces[k], axis, way(k))]
    psum x1 -> x0, blocking collectives: 23.8 us -> none  [shards(): lax.psum((local_total * factor).astype(jnp.bfloat16), 'col')]
    pmax x1 -> x0, blocking collectives: 23.5 us -> none  [shards(): top = lax.pmax(local_top, 'col')]
  transfers between devices with their start and end apart: 4 -> 49, of which waited for: 4 -> 15; matrix products, arithmetic and copies ran while one was open for 3% -> 15% of each run, Pallas kernels for 0% -> 5%
where the time goes in v1:
time: 199 us; the launch traced here: 197 us
  starting transfers between devices  73.9 us (37%)
  Pallas kernels  59.2 us (30%)
  waiting for transfers between devices  27.6 us (14%)
  local copies, waits for them, and re-layouts  21.9 us (11%)
  matrix products  7.41 us (4%)
  other arithmetic  6.18 us (3%)
    ppermute x47, starting transfers between devices, send(): lax.ppermute(pieces[k], axis, way(k))  66.9 us
    ppermute x47, waiting for transfers between devices, send(): lax.ppermute(pieces[k], axis, way(k))  27.6 us
    pallas_call x1, Pallas kernels, backward(): pl.pallas_call(backward_kernel, grid=(PAIRS,), out_shape=[jax.ShapeDtypeS...  21.9 us
    pallas_call x1, Pallas kernels, forward(): pl.pallas_call(forward_kernel, grid=(PAIRS,), out_shape=(jax.ShapeDtypeSt...  14.2 us
    unnamed x118, local copies, waits for them, and re-layouts  10.5 us
    reshape x4, local copies, waits for them, and re-layouts, widen(): jnp.pad(split, ((0, 0), (0, 0), (0, SLOT - HD)))  8.09 us
    pallas_call x1, Pallas kernels, project(): pl.pallas_call(project_kernel, out_shape=(shape, shape), in_specs=[SCALAR...  6.25 us
    pallas_call x3, Pallas kernels, place(): pl.pallas_call(place_kernel, out_shape=jax.ShapeDtypeStruct((rows, pieces...  5.74 us
  transfers between devices with their start and end apart: 49, of which 15 were waited for; matrix products, arithmetic and copies ran while one was open for 15% of the time, Pallas kernels for 5%

profile of v1, /device:TPU:1, one launch (start us, length us, event | category | flops | bytes accessed | tf_op | source)
XLA Modules:
  0.0 197.4 jit_solution(17129595770231278162)
XLA Ops:
  1.7 4.5 %collective-permute-start = (bf16[48,768]{1,0:T(8,128)(2,1)S(1)}, bf16[48,768]{1,0:T(8,128)(2,1)S(1)}, u32[]{:S(2)}, u32[]{:S(2)}) collective-permute-start(bf16[48,768]{1,0:T(8,128)(2,1)S(1)} %constant_dynamic-slice_fusion), channel_id=1, source_target_pairs={{0,0},{1,8},{2,16},{3,24},{4,32},{5,40},{6,48},{7,56},{8,64},{9,72... | collective-permute-start | bytes 221192 | tf_op jit(solution)/shard_map/ppermute | solution.py:325
  17.6 2.2 %divide_bitcast_fusion.refs_8_ = f32[384,1024]{1,0:T(8,128)} fusion(bf16[768,1024]{0,1:T(8,128)(2,1)S(1)} %bitcast.28, bf16[384,768]{1,0:T(8,128)(2,1)S(1)} %copy-done), kind=kOutput, calls=%fused_computation.2 | convolution fusion | flops 605159424 | bytes 3735552 | tf_op jit(solution)/shard_map/dot_general | solution.py:28
  20.0 3.2 %copy.25.wq_ref = bf16[768,1024]{1,0:T(8,128)(2,1)} copy(bf16[768,1024]{0,1:T(8,128)(2,1)} %bitcast.30) | data formatting | bytes 3145728 | tf_op jit(solution)/shard_map/reshape | solution.py:310
  23.2 3.5 %fusion.dh_ref.refs_9_ = f32[384,1024]{1,0:T(8,128)} fusion(f32[384,1024]{1,0:T(8,128)} %divide_bitcast_fusion.refs_8_, bf16[1024,768]{1,0:T(8,128)(2,1)S(1)} %bitcast.26, bf16[384,768]{1,0:T(8,128)(2,1)S(1)} %copy-done.8, pred[1024]{0:T(1024)(128)(4,1)S(1)} %fusion.5), kind=kOutput, calls=%fused_computation.1 | convolution fusion | flops 604766208 | bytes 5309440 | tf_op jit(solution)/shard_map/dot_general | solution.py:24
  27.1 2.9 %collective-permute-start.1 = (bf16[48,768]{1,0:T(8,128)(2,1)S(1)}, bf16[48,768]{1,0:T(8,128)(2,1)S(1)}, u32[]{:S(2)}, u32[]{:S(2)}) collective-permute-start(bf16[48,768]{1,0:T(8,128)(2,1)S(1)} %collective-permute-done.refs_0_), channel_id=1, source_target_pairs={{0,8},{8,16},{16,24},{24,0},{32,40},{40,48},{48,56},{56,32},{64,72... | collective-permute-start | bytes 221192 | tf_op jit(solution)/shard_map/ppermute | solution.py:305
  30.1 2.7 %collective-permute-start.2 = (bf16[48,768]{1,0:T(8,128)(2,1)S(1)}, bf16[48,768]{1,0:T(8,128)(2,1)S(1)}, u32[]{:S(2)}, u32[]{:S(2)}) collective-permute-start(bf16[48,768]{1,0:T(8,128)(2,1)S(1)} %collective-permute-done.refs_0_), channel_id=1, source_target_pairs={{0,16},{8,24},{16,0},{24,8},{32,48},{40,56},{48,32},{56,40},{64,80... | collective-permute-start | bytes 221192 | tf_op jit(solution)/shard_map/ppermute | solution.py:305
  33.8 3.2 %collective-permute-done.2.refs_2_ = bf16[48,768]{1,0:T(8,128)(2,1)S(1)} collective-permute-done((bf16[48,768]{1,0:T(8,128)(2,1)S(1)}, bf16[48,768]{1,0:T(8,128)(2,1)S(1)}, u32[]{:S(2)}, u32[]{:S(2)}) %collective-permute-start.2) | collective-permute-done | bytes 73760 | tf_op jit(solution)/shard_map/ppermute | solution.py:305
  41.1 3.9 %collective-permute-start.5 = (bf16[192,768]{1,0:T(8,128)(2,1)}, bf16[192,768]{1,0:T(8,128)(2,1)S(1)}, u32[]{:S(2)}, u32[]{:S(2)}) collective-permute-start(bf16[192,768]{1,0:T(8,128)(2,1)} %shard_map.112.refs_0_), channel_id=1, source_target_pairs={{0,64},{8,72},{16,80},{24,88},{32,96},{40,104},{48,112},{56,120},{... | collective-permute-start | bytes 884744 | tf_op jit(solution)/shard_map/ppermute | solution.py:305
  47.5 3.6 %collective-permute-done.4.refs_1_ = bf16[192,768]{1,0:T(8,128)(2,1)S(1)} collective-permute-done((bf16[192,768]{1,0:T(8,128)(2,1)}, bf16[192,768]{1,0:T(8,128)(2,1)S(1)}, u32[]{:S(2)}, u32[]{:S(2)}) %collective-permute-start.4) | collective-permute-done | bytes 294944 | tf_op jit(solution)/shard_map/ppermute | solution.py:305
  51.1 7.2 %collective-permute-done.5.refs_2_ = bf16[192,768]{1,0:T(8,128)(2,1)S(1)} collective-permute-done((bf16[192,768]{1,0:T(8,128)(2,1)}, bf16[192,768]{1,0:T(8,128)(2,1)S(1)}, u32[]{:S(2)}, u32[]{:S(2)}) %collective-permute-start.5) | collective-permute-done | bytes 294944 | tf_op jit(solution)/shard_map/ppermute | solution.py:305
  59.7 6.3 %shard_map.113 = (bf16[768,1024]{1,0:T(8,128)(2,1)}, bf16[768,1024]{1,0:T(8,128)(2,1)}) custom-call(s32[4]{0:T(128)} %fusion.10.at_ref, bf16[192,768]{1,0:T(8,128)(2,1)} %shard_map.112.refs_0_, bf16[192,768]{1,0:T(8,128)(2,1)} %copy-done.9, bf16[192,768]{1,0:T(8,128)(2,1)} %copy-done.10, bf16[192,768]{1,0:T(8,128)(2,1)} %copy-done.11, ...), custom_call_target="tpu_custom_call" | custom-call | tf_op jit(solution)/shard_map/pallas_call | solution.py:102
  67.4 14.2 %shard_map.114 = (bf16[16,384,768]{2,1,0:T(8,128)(2,1)}, f32[384,1024]{1,0:T(8,128)}, f32[48,384]{1,0:T(8,128)}) custom-call(bf16[16,384,768]{2,1,0:T(8,128)(2,1)} %bias_ref.1, bf16[384,1024]{1,0:T(8,128)(2,1)} %fusion.1.q_ref, bf16[768,1024]{1,0:T(8,128)(2,1)} %get-tuple-element.36.k_ref, bf16[768,1024]{1,0:T(8,128)(2,1)} %get-tuple-element.37.v_ref, ...), custom_call_target="tpu_custom_call" | custom-call | flops 4831838208 | bytes 18874368 | tf_op jit(solution)/shard_map/pallas_call | solution.py:144
  84.3 1.9 collective-permute-start.9
  87.2 2.6 %collective-permute-start.11 = (f32[48,384]{1,0:T(8,128)}, f32[48,384]{1,0:T(8,128)S(1)}, u32[]{:S(2)}, u32[]{:S(2)}) collective-permute-start(f32[48,384]{1,0:T(8,128)} %get-tuple-element.38.refs_0_), channel_id=1, source_target_pairs={{0,5},{1,6},{2,7},{3,0},{4,1},{5,2},{6,3},{7,4},{8,13},{9,14},{10,... | collective-permute-start | bytes 221192 | tf_op jit(solution)/shard_map/ppermute | solution.py:305
  95.5 4.2 %shard_map.115 = (bf16[384,1024]{1,0:T(8,128)(2,1)}, bf16[48,1024]{1,0:T(8,128)(2,1)}, bf16[48,1024]{1,0:T(8,128)(2,1)}, bf16[48,1024]{1,0:T(8,128)(2,1)}, bf16[...) custom-call(s32[8]{0:T(128)} %fusion.9.at_ref.cat_ref, ...), custom_call_target="tpu_custom_call" | custom-call | tf_op jit(solution)/shard_map/pallas_call | solution.py:192
  99.8 21.9 %shard_map.118 = (bf16[16,384,768]{2,1,0:T(8,128)(2,1)}, bf16[192,768]{1,0:T(8,128)(2,1)}, bf16[192,768]{1,0:T(8,128)(2,1)}, bf16[192,768]{1,0:T(8,128)(2,1)}, b...) custom-call(s32[4]{0:T(128)} %fusion.13.yat_ref, ...), custom_call_target="tpu_custom_call" | custom-call | flops 9663676416 | bytes 18874368 | tf_op jit(solution)/shard_map/pallas_call | solution.py:248
  121.8 2.1 %collective-permute-start.36 = (bf16[192,768]{1,0:T(8,128)(2,1)}, bf16[192,768]{1,0:T(8,128)(2,1)S(1)}, u32[]{:S(2)}, u32[]{:S(2)}) collective-permute-start(bf16[192,768]{1,0:T(8,128)(2,1)} %get-tuple-element.62), channel_id=1, source_target_pairs={{0,64},{8,72},{16,80},{24,88},{32,96},{40,104},{48,112},{56,120},{... | collective-permute-start | bytes 884744 | tf_op jit(solution)/shard_map/ppermute | solution.py:305
  127.7 4.3 %collective-permute-done.35.refs_1_ = bf16[192,768]{1,0:T(8,128)(2,1)S(1)} collective-permute-done((bf16[192,768]{1,0:T(8,128)(2,1)}, bf16[192,768]{1,0:T(8,128)(2,1)S(1)}, u32[]{:S(2)}, u32[]{:S(2)}) %collective-permute-start.35) | collective-permute-done | bytes 294944 | tf_op jit(solution)/shard_map/ppermute | solution.py:305
  132.0 6.9 %collective-permute-start.34 = (bf16[48,768]{1,0:T(8,128)(2,1)}, bf16[48,768]{1,0:T(8,128)(2,1)S(1)}, u32[]{:S(2)}, u32[]{:S(2)}) collective-permute-start(bf16[48,768]{1,0:T(8,128)(2,1)} %get-tuple-element.59), channel_id=1, source_target_pairs={{0,7},{1,0},{2,1},{3,2},{4,3},{5,4},{6,5},{7,6},{8,15},{9,8},{10,9... | collective-permute-start | bytes 221192 | tf_op jit(solution)/shard_map/ppermute | solution.py:305
  138.9 2.8 %collective-permute-start.33 = (bf16[48,768]{1,0:T(8,128)(2,1)}, bf16[48,768]{1,0:T(8,128)(2,1)S(1)}, u32[]{:S(2)}, u32[]{:S(2)}) collective-permute-start(bf16[48,768]{1,0:T(8,128)(2,1)} %get-tuple-element.58), channel_id=1, source_target_pairs={{0,6},{1,7},{2,0},{3,1},{4,2},{5,3},{6,4},{7,5},{8,14},{9,15},{10,... | collective-permute-start | bytes 221192 | tf_op jit(solution)/shard_map/ppermute | solution.py:305
  142.7 2.2 %shard_map.119 = (bf16[48,768]{1,0:T(8,128)(2,1)}, bf16[48,768]{1,0:T(8,128)(2,1)}, bf16[48,768]{1,0:T(8,128)(2,1)}, bf16[48,768]{1,0:T(8,128)(2,1)}) custom-call(s32[4]{0:T(128)} %fusion.14.at_ref, bf16[192,768]{1,0:T(8,128)(2,1)} %get-tuple-element.60.refs_0_, bf16[192,768]{1,0:T(8,128)(2,1)} %copy-done.13, bf16[192,768]{1,0:T(8,128)(2,1)} %copy-done.14, ...), custom_call_target="tpu_custom_call" | custom-call | tf_op jit(solution)/shard_map/pallas_call | solution.py:272
  147.2 3.7 %collective-permute-start.16 = (bf16[48,1024]{1,0:T(8,128)(2,1)S(1)}, bf16[48,1024]{1,0:T(8,128)(2,1)S(1)}, u32[]{:S(2)}, u32[]{:S(2)}) collective-permute-start(bf16[48,1024]{1,0:T(8,128)(2,1)S(1)} %copy-done.54), channel_id=1, source_target_pairs={{0,3},{1,4},{2,5},{3,6},{4,7},{5,0},{6,1},{7,2},{8,11},{9,12},{10,... | collective-permute-start | bytes 294920 | tf_op jit(solution)/shard_map/ppermute | solution.py:305
  152.6 2.3 %collective-permute-start.19 = (bf16[48,1024]{1,0:T(8,128)(2,1)S(1)}, bf16[48,1024]{1,0:T(8,128)(2,1)S(1)}, u32[]{:S(2)}, u32[]{:S(2)}) collective-permute-start(bf16[48,1024]{1,0:T(8,128)(2,1)S(1)} %copy-done.51), channel_id=1, source_target_pairs={{0,6},{1,7},{2,0},{3,1},{4,2},{5,3},{6,4},{7,5},{8,14},{9,15},{10,... | collective-permute-start | bytes 294920 | tf_op jit(solution)/shard_map/ppermute | solution.py:305
  158.9 1.8 collective-permute-start.30
  161.3 1.9 collective-permute-done.20.refs_7_
  163.2 2.4 %collective-permute-start.41 = (bf16[48,768]{1,0:T(8,128)(2,1)S(1)}, bf16[48,768]{1,0:T(8,128)(2,1)S(1)}, u32[]{:S(2)}, u32[]{:S(2)}) collective-permute-start(bf16[48,768]{1,0:T(8,128)(2,1)S(1)} %add_convert_fusion.1), channel_id=1, source_target_pairs={{0,0},{8,1},{16,2},{24,3},{32,4},{40,5},{48,6},{56,7},{64,8},{72,9... | collective-permute-start | bytes 221192 | tf_op jit(solution)/shard_map/ppermute | solution.py:359
  167.3 4.7 %shard_map.116 = (bf16[48,768]{1,0:T(8,128)(2,1)}, f32[48,768]{1,0:T(8,128)}) custom-call(s32[8]{0:T(128)} %fusion.9.at_ref.cat_ref, bf16[48,1024]{1,0:T(8,128)(2,1)} %get-tuple-element.40.refs_0_, bf16[48,1024]{1,0:T(8,128)(2,1)} %copy-done.16, bf16[48,1024]{1,0:T(8,128)(2,1)} %copy-done.17, bf16[48,1024]{1,0:T(8,128)(2,1)} %copy-done.18, ...), custom_call_target="tpu_custom_call" | custom-call | tf_op jit(solution)/shard_map/pallas_call | solution.py:295
  172.7 4.7 %collective-permute-start.23 = (bf16[48,768]{1,0:T(8,128)(2,1)}, bf16[48,768]{1,0:T(8,128)(2,1)S(1)}, u32[]{:S(2)}, u32[]{:S(2)}) collective-permute-start(bf16[48,768]{1,0:T(8,128)(2,1)} %get-tuple-element.48.refs_0_), channel_id=1, source_target_pairs={{0,3},{1,4},{2,5},{3,6},{4,7},{5,0},{6,1},{7,2},{8,11},{9,12},{10,... | collective-permute-start | bytes 221192 | tf_op jit(solution)/shard_map/ppermute | solution.py:305
  177.4 2.0 %collective-permute-start.25 = (bf16[48,768]{1,0:T(8,128)(2,1)}, bf16[48,768]{1,0:T(8,128)(2,1)S(1)}, u32[]{:S(2)}, u32[]{:S(2)}) collective-permute-start(bf16[48,768]{1,0:T(8,128)(2,1)} %get-tuple-element.48.refs_0_), channel_id=1, source_target_pairs={{0,5},{1,6},{2,7},{3,0},{4,1},{5,2},{6,3},{7,4},{8,13},{9,14},{10,... | collective-permute-start | bytes 221192 | tf_op jit(solution)/shard_map/ppermute | solution.py:305
  184.9 2.5 %collective-permute-start.45 = (bf16[48,768]{1,0:T(8,128)(2,1)S(1)}, bf16[48,768]{1,0:T(8,128)(2,1)S(1)}, u32[]{:S(2)}, u32[]{:S(2)}) collective-permute-start(bf16[48,768]{1,0:T(8,128)(2,1)S(1)} %add_convert_fusion.refs_0_), channel_id=1, source_target_pairs={{0,4},{1,5},{2,6},{3,7},{4,0},{5,1},{6,2},{7,3},{8,12},{9,13},{10,... | collective-permute-start | bytes 221192 | tf_op jit(solution)/shard_map/ppermute | solution.py:305
  190.9 2.0 %shard_map.117 = bf16[384,768]{1,0:T(8,128)(2,1)} custom-call(s32[8]{0:T(128)} %fusion.8.at_ref, bf16[48,768]{1,0:T(8,128)(2,1)} %get-tuple-element.48.refs_0_, bf16[48,768]{1,0:T(8,128)(2,1)} %copy-done.24, bf16[48,768]{1,0:T(8,128)(2,1)} %copy-done.25, bf16[48,768]{1,0:T(8,128)(2,1)} %copy-done.26, bf16[48,768]{1,0:T(8,128)(2,1)} %copy-done.27, ...), custom_call_target="tpu_custom_call" | custom-call | tf_op jit(solution)/shard_map/pallas_call | solution.py:80
  195.4 2.0 %shard_map.120 = bf16[384,768]{1,0:T(8,128)(2,1)} custom-call(s32[8]{0:T(128)} %fusion.8.at_ref, bf16[48,768]{1,0:T(8,128)(2,1)} %copy-done.12, bf16[48,768]{1,0:T(8,128)(2,1)} %copy-done.29, bf16[48,768]{1,0:T(8,128)(2,1)} %copy-done.31, bf16[48,768]{1,0:T(8,128)(2,1)} %copy-done.33, bf16[48,768]{1,0:T(8,128)(2,1)} %copy-done.34, ...), custom_call_target="tpu_custom_call" | custom-call | tf_op jit(solution)/shard_map/pallas_call | solution.py:80
  (222 shorter events, 59.9 us)
Async XLA Ops:
  1.7 25.4 %collective-permute-start = (bf16[48,768]{1,0:T(8,128)(2,1)S(1)}, bf16[48,768]{1,0:T(8,128)(2,1)S(1)}, u32[]{:S(2)}, u32[]{:S(2)}) collective-permute-start(bf16[48,768]{1,0:T(8,128)(2,1)S(1)} %constant_dynamic-slice_fusion), channel_id=1, source_target_pairs={{0,0},{1,8},{2,16},{3,24},{4,32},{5,40},{6,48},{7,56},{8,64},{9,72... | collective-permute-start | bytes 221192 | tf_op jit(solution)/shard_map/ppermute | solution.py:325
  30.1 7.0 %collective-permute-start.2 = (bf16[48,768]{1,0:T(8,128)(2,1)S(1)}, bf16[48,768]{1,0:T(8,128)(2,1)S(1)}, u32[]{:S(2)}, u32[]{:S(2)}) collective-permute-start(bf16[48,768]{1,0:T(8,128)(2,1)S(1)} %collective-permute-done.refs_0_), channel_id=1, source_target_pairs={{0,16},{8,24},{16,0},{24,8},{32,48},{40,56},{48,32},{56,40},{64,80... | collective-permute-start | bytes 221192 | tf_op jit(solution)/shard_map/ppermute | solution.py:305
  40.1 11.0 %collective-permute-start.4 = (bf16[192,768]{1,0:T(8,128)(2,1)}, bf16[192,768]{1,0:T(8,128)(2,1)S(1)}, u32[]{:S(2)}, u32[]{:S(2)}) collective-permute-start(bf16[192,768]{1,0:T(8,128)(2,1)} %shard_map.112.refs_0_), channel_id=1, source_target_pairs={{0,32},{8,40},{16,48},{24,56},{32,64},{40,72},{48,80},{56,88},{64,... | collective-permute-start | bytes 884744 | tf_op jit(solution)/shard_map/ppermute | solution.py:305
  41.1 17.2 %collective-permute-start.5 = (bf16[192,768]{1,0:T(8,128)(2,1)}, bf16[192,768]{1,0:T(8,128)(2,1)S(1)}, u32[]{:S(2)}, u32[]{:S(2)}) collective-permute-start(bf16[192,768]{1,0:T(8,128)(2,1)} %shard_map.112.refs_0_), channel_id=1, source_target_pairs={{0,64},{8,72},{16,80},{24,88},{32,96},{40,104},{48,112},{56,120},{... | collective-permute-start | bytes 884744 | tf_op jit(solution)/shard_map/ppermute | solution.py:305
  45.0 13.3 %collective-permute-start.6 = (bf16[192,768]{1,0:T(8,128)(2,1)}, bf16[192,768]{1,0:T(8,128)(2,1)S(1)}, u32[]{:S(2)}, u32[]{:S(2)}) collective-permute-start(bf16[192,768]{1,0:T(8,128)(2,1)} %shard_map.112.refs_0_), channel_id=1, source_target_pairs={{0,96},{8,104},{16,112},{24,120},{32,0},{40,8},{48,16},{56,24},{64... | collective-permute-start | bytes 884744 | tf_op jit(solution)/shard_map/ppermute | solution.py:305
  81.6 8.2 %collective-permute-start.7 = (f32[48,384]{1,0:T(8,128)}, f32[48,384]{1,0:T(8,128)S(1)}, u32[]{:S(2)}, u32[]{:S(2)}) collective-permute-start(f32[48,384]{1,0:T(8,128)} %get-tuple-element.38.refs_0_), channel_id=1, source_target_pairs={{0,1},{1,2},{2,3},{3,4},{4,5},{5,6},{6,7},{7,0},{8,9},{9,10},{10,1... | collective-permute-start | bytes 221192 | tf_op jit(solution)/shard_map/ppermute | solution.py:305
  84.3 8.5 %collective-permute-start.9 = (f32[48,384]{1,0:T(8,128)}, f32[48,384]{1,0:T(8,128)S(1)}, u32[]{:S(2)}, u32[]{:S(2)}) collective-permute-start(f32[48,384]{1,0:T(8,128)} %get-tuple-element.38.refs_0_), channel_id=1, source_target_pairs={{0,3},{1,4},{2,5},{3,6},{4,7},{5,0},{6,1},{7,2},{8,11},{9,12},{10,... | collective-permute-start | bytes 221192 | tf_op jit(solution)/shard_map/ppermute | solution.py:305
  121.6 10.4 %collective-permute-start.35 = (bf16[192,768]{1,0:T(8,128)(2,1)}, bf16[192,768]{1,0:T(8,128)(2,1)S(1)}, u32[]{:S(2)}, u32[]{:S(2)}) collective-permute-start(bf16[192,768]{1,0:T(8,128)(2,1)} %get-tuple-element.61), channel_id=1, source_target_pairs={{0,32},{8,40},{16,48},{24,56},{32,64},{40,72},{48,80},{56,88},{64,... | collective-permute-start | bytes 884744 | tf_op jit(solution)/shard_map/ppermute | solution.py:305
  121.8 17.0 %collective-permute-start.36 = (bf16[192,768]{1,0:T(8,128)(2,1)}, bf16[192,768]{1,0:T(8,128)(2,1)S(1)}, u32[]{:S(2)}, u32[]{:S(2)}) collective-permute-start(bf16[192,768]{1,0:T(8,128)(2,1)} %get-tuple-element.62), channel_id=1, source_target_pairs={{0,64},{8,72},{16,80},{24,88},{32,96},{40,104},{48,112},{56,120},{... | collective-permute-start | bytes 884744 | tf_op jit(solution)/shard_map/ppermute | solution.py:305
  124.0 17.7 %collective-permute-start.37 = (bf16[192,768]{1,0:T(8,128)(2,1)}, bf16[192,768]{1,0:T(8,128)(2,1)S(1)}, u32[]{:S(2)}, u32[]{:S(2)}) collective-permute-start(bf16[192,768]{1,0:T(8,128)(2,1)} %get-tuple-element.63), channel_id=1, source_target_pairs={{0,96},{8,104},{16,112},{24,120},{32,0},{40,8},{48,16},{56,24},{64... | collective-permute-start | bytes 884744 | tf_op jit(solution)/shard_map/ppermute | solution.py:305
  125.0 22.2 %collective-permute-start.14 = (bf16[48,1024]{1,0:T(8,128)(2,1)S(1)}, bf16[48,1024]{1,0:T(8,128)(2,1)S(1)}, u32[]{:S(2)}, u32[]{:S(2)}) collective-permute-start(bf16[48,1024]{1,0:T(8,128)(2,1)S(1)} %copy-done.56), channel_id=1, source_target_pairs={{0,1},{1,2},{2,3},{3,4},{4,5},{5,6},{6,7},{7,0},{8,9},{9,10},{10,1... | collective-permute-start | bytes 294920 | tf_op jit(solution)/shard_map/ppermute | solution.py:305
  126.8 24.0 %collective-permute-start.15 = (bf16[48,1024]{1,0:T(8,128)(2,1)S(1)}, bf16[48,1024]{1,0:T(8,128)(2,1)S(1)}, u32[]{:S(2)}, u32[]{:S(2)}) collective-permute-start(bf16[48,1024]{1,0:T(8,128)(2,1)S(1)} %copy-done.55), channel_id=1, source_target_pairs={{0,2},{1,3},{2,4},{3,5},{4,6},{5,7},{6,0},{7,1},{8,10},{9,11},{10,... | collective-permute-start | bytes 294920 | tf_op jit(solution)/shard_map/ppermute | solution.py:305
  132.0 12.9 %collective-permute-start.34 = (bf16[48,768]{1,0:T(8,128)(2,1)}, bf16[48,768]{1,0:T(8,128)(2,1)S(1)}, u32[]{:S(2)}, u32[]{:S(2)}) collective-permute-start(bf16[48,768]{1,0:T(8,128)(2,1)} %get-tuple-element.59), channel_id=1, source_target_pairs={{0,7},{1,0},{2,1},{3,2},{4,3},{5,4},{6,5},{7,6},{8,15},{9,8},{10,9... | collective-permute-start | bytes 221192 | tf_op jit(solution)/shard_map/ppermute | solution.py:305
  138.9 7.6 %collective-permute-start.33 = (bf16[48,768]{1,0:T(8,128)(2,1)}, bf16[48,768]{1,0:T(8,128)(2,1)S(1)}, u32[]{:S(2)}, u32[]{:S(2)}) collective-permute-start(bf16[48,768]{1,0:T(8,128)(2,1)} %get-tuple-element.58), channel_id=1, source_target_pairs={{0,6},{1,7},{2,0},{3,1},{4,2},{5,3},{6,4},{7,5},{8,14},{9,15},{10,... | collective-permute-start | bytes 221192 | tf_op jit(solution)/shard_map/ppermute | solution.py:305
  144.9 7.3 %collective-permute-start.40 = (bf16[48,768]{1,0:T(8,128)(2,1)}, bf16[48,768]{1,0:T(8,128)(2,1)S(1)}, u32[]{:S(2)}, u32[]{:S(2)}) collective-permute-start(bf16[48,768]{1,0:T(8,128)(2,1)} %get-tuple-element.67), channel_id=1, source_target_pairs={{0,24},{8,0},{16,8},{24,16},{32,56},{40,32},{48,40},{56,48},{64,88... | collective-permute-start | bytes 221192 | tf_op jit(solution)/shard_map/ppermute | solution.py:305
  147.1 7.7 %collective-permute-start.38 = (bf16[48,768]{1,0:T(8,128)(2,1)}, bf16[48,768]{1,0:T(8,128)(2,1)S(1)}, u32[]{:S(2)}, u32[]{:S(2)}) collective-permute-start(bf16[48,768]{1,0:T(8,128)(2,1)} %get-tuple-element.65), channel_id=1, source_target_pairs={{0,8},{8,16},{16,24},{24,0},{32,40},{40,48},{48,56},{56,32},{64,72... | collective-permute-start | bytes 221192 | tf_op jit(solution)/shard_map/ppermute | solution.py:305
  147.2 11.1 %collective-permute-start.16 = (bf16[48,1024]{1,0:T(8,128)(2,1)S(1)}, bf16[48,1024]{1,0:T(8,128)(2,1)S(1)}, u32[]{:S(2)}, u32[]{:S(2)}) collective-permute-start(bf16[48,1024]{1,0:T(8,128)(2,1)S(1)} %copy-done.54), channel_id=1, source_target_pairs={{0,3},{1,4},{2,5},{3,6},{4,7},{5,0},{6,1},{7,2},{8,11},{9,12},{10,... | collective-permute-start | bytes 294920 | tf_op jit(solution)/shard_map/ppermute | solution.py:305
  150.8 8.0 %collective-permute-start.17 = (bf16[48,1024]{1,0:T(8,128)(2,1)S(1)}, bf16[48,1024]{1,0:T(8,128)(2,1)S(1)}, u32[]{:S(2)}, u32[]{:S(2)}) collective-permute-start(bf16[48,1024]{1,0:T(8,128)(2,1)S(1)} %copy-done.53), channel_id=1, source_target_pairs={{0,4},{1,5},{2,6},{3,7},{4,0},{5,1},{6,2},{7,3},{8,12},{9,13},{10,... | collective-permute-start | bytes 294920 | tf_op jit(solution)/shard_map/ppermute | solution.py:305
  152.2 8.5 %collective-permute-start.18 = (bf16[48,1024]{1,0:T(8,128)(2,1)S(1)}, bf16[48,1024]{1,0:T(8,128)(2,1)S(1)}, u32[]{:S(2)}, u32[]{:S(2)}) collective-permute-start(bf16[48,1024]{1,0:T(8,128)(2,1)S(1)} %copy-done.52), channel_id=1, source_target_pairs={{0,5},{1,6},{2,7},{3,0},{4,1},{5,2},{6,3},{7,4},{8,13},{9,14},{10,... | collective-permute-start | bytes 294920 | tf_op jit(solution)/shard_map/ppermute | solution.py:305
  152.6 8.3 %collective-permute-start.19 = (bf16[48,1024]{1,0:T(8,128)(2,1)S(1)}, bf16[48,1024]{1,0:T(8,128)(2,1)S(1)}, u32[]{:S(2)}, u32[]{:S(2)}) collective-permute-start(bf16[48,1024]{1,0:T(8,128)(2,1)S(1)} %copy-done.51), channel_id=1, source_target_pairs={{0,6},{1,7},{2,0},{3,1},{4,2},{5,3},{6,4},{7,5},{8,14},{9,15},{10,... | collective-permute-start | bytes 294920 | tf_op jit(solution)/shard_map/ppermute | solution.py:305
  154.9 8.3 %collective-permute-start.20 = (bf16[48,1024]{1,0:T(8,128)(2,1)S(1)}, bf16[48,1024]{1,0:T(8,128)(2,1)S(1)}, u32[]{:S(2)}, u32[]{:S(2)}) collective-permute-start(bf16[48,1024]{1,0:T(8,128)(2,1)S(1)} %copy-done.50), channel_id=1, source_target_pairs={{0,7},{1,0},{2,1},{3,2},{4,3},{5,4},{6,5},{7,6},{8,15},{9,8},{10,9... | collective-permute-start | bytes 294920 | tf_op jit(solution)/shard_map/ppermute | solution.py:305
  158.2 13.7 %collective-permute-start.31 = (bf16[48,768]{1,0:T(8,128)(2,1)}, bf16[48,768]{1,0:T(8,128)(2,1)S(1)}, u32[]{:S(2)}, u32[]{:S(2)}) collective-permute-start(bf16[48,768]{1,0:T(8,128)(2,1)} %get-tuple-element.56), channel_id=1, source_target_pairs={{0,4},{1,5},{2,6},{3,7},{4,0},{5,1},{6,2},{7,3},{8,12},{9,13},{10,... | collective-permute-start | bytes 221192 | tf_op jit(solution)/shard_map/ppermute | solution.py:305
  158.9 13.1 %collective-permute-start.30 = (bf16[48,768]{1,0:T(8,128)(2,1)}, bf16[48,768]{1,0:T(8,128)(2,1)S(1)}, u32[]{:S(2)}, u32[]{:S(2)}) collective-permute-start(bf16[48,768]{1,0:T(8,128)(2,1)} %get-tuple-element.55), channel_id=1, source_target_pairs={{0,3},{1,4},{2,5},{3,6},{4,7},{5,0},{6,1},{7,2},{8,11},{9,12},{10,... | collective-permute-start | bytes 221192 | tf_op jit(solution)/shard_map/ppermute | solution.py:305
  160.7 12.0 %collective-permute-start.29 = (bf16[48,768]{1,0:T(8,128)(2,1)}, bf16[48,768]{1,0:T(8,128)(2,1)S(1)}, u32[]{:S(2)}, u32[]{:S(2)}) collective-permute-start(bf16[48,768]{1,0:T(8,128)(2,1)} %get-tuple-element.54), channel_id=1, source_target_pairs={{0,2},{1,3},{2,4},{3,5},{4,6},{5,7},{6,0},{7,1},{8,10},{9,11},{10,... | collective-permute-start | bytes 221192 | tf_op jit(solution)/shard_map/ppermute | solution.py:305
  160.9 16.5 %collective-permute-start.28 = (bf16[48,768]{1,0:T(8,128)(2,1)}, bf16[48,768]{1,0:T(8,128)(2,1)S(1)}, u32[]{:S(2)}, u32[]{:S(2)}) collective-permute-start(bf16[48,768]{1,0:T(8,128)(2,1)} %get-tuple-element.53), channel_id=1, source_target_pairs={{0,1},{1,2},{2,3},{3,4},{4,5},{5,6},{6,7},{7,0},{8,9},{9,10},{10,1... | collective-permute-start | bytes 221192 | tf_op jit(solution)/shard_map/ppermute | solution.py:305
  163.2 14.3 %collective-permute-start.41 = (bf16[48,768]{1,0:T(8,128)(2,1)S(1)}, bf16[48,768]{1,0:T(8,128)(2,1)S(1)}, u32[]{:S(2)}, u32[]{:S(2)}) collective-permute-start(bf16[48,768]{1,0:T(8,128)(2,1)S(1)} %add_convert_fusion.1), channel_id=1, source_target_pairs={{0,0},{8,1},{16,2},{24,3},{32,4},{40,5},{48,6},{56,7},{64,8},{72,9... | collective-permute-start | bytes 221192 | tf_op jit(solution)/shard_map/ppermute | solution.py:359
  172.0 8.6 %collective-permute-start.21 = (bf16[48,768]{1,0:T(8,128)(2,1)}, bf16[48,768]{1,0:T(8,128)(2,1)S(1)}, u32[]{:S(2)}, u32[]{:S(2)}) collective-permute-start(bf16[48,768]{1,0:T(8,128)(2,1)} %get-tuple-element.48.refs_0_), channel_id=1, source_target_pairs={{0,1},{1,2},{2,3},{3,4},{4,5},{5,6},{6,7},{7,0},{8,9},{9,10},{10,1... | collective-permute-start | bytes 221192 | tf_op jit(solution)/shard_map/ppermute | solution.py:305
  172.0 8.7 %collective-permute-start.22 = (bf16[48,768]{1,0:T(8,128)(2,1)}, bf16[48,768]{1,0:T(8,128)(2,1)S(1)}, u32[]{:S(2)}, u32[]{:S(2)}) collective-permute-start(bf16[48,768]{1,0:T(8,128)(2,1)} %get-tuple-element.48.refs_0_), channel_id=1, source_target_pairs={{0,2},{1,3},{2,4},{3,5},{4,6},{5,7},{6,0},{7,1},{8,10},{9,11},{10,... | collective-permute-start | bytes 221192 | tf_op jit(solution)/shard_map/ppermute | solution.py:305
  172.7 9.8 %collective-permute-start.23 = (bf16[48,768]{1,0:T(8,128)(2,1)}, bf16[48,768]{1,0:T(8,128)(2,1)S(1)}, u32[]{:S(2)}, u32[]{:S(2)}) collective-permute-start(bf16[48,768]{1,0:T(8,128)(2,1)} %get-tuple-element.48.refs_0_), channel_id=1, source_target_pairs={{0,3},{1,4},{2,5},{3,6},{4,7},{5,0},{6,1},{7,2},{8,11},{9,12},{10,... | collective-permute-start | bytes 221192 | tf_op jit(solution)/shard_map/ppermute | solution.py:305
  180.7 6.7 %collective-permute-start.27 = (bf16[48,768]{1,0:T(8,128)(2,1)}, bf16[48,768]{1,0:T(8,128)(2,1)S(1)}, u32[]{:S(2)}, u32[]{:S(2)}) collective-permute-start(bf16[48,768]{1,0:T(8,128)(2,1)} %get-tuple-element.48.refs_0_), channel_id=1, source_target_pairs={{0,7},{1,0},{2,1},{3,2},{4,3},{5,4},{6,5},{7,6},{8,15},{9,8},{10,9... | collective-permute-start | bytes 221192 | tf_op jit(solution)/shard_map/ppermute | solution.py:305
  183.9 9.0 %collective-permute-start.44 = (bf16[48,768]{1,0:T(8,128)(2,1)S(1)}, bf16[48,768]{1,0:T(8,128)(2,1)S(1)}, u32[]{:S(2)}, u32[]{:S(2)}) collective-permute-start(bf16[48,768]{1,0:T(8,128)(2,1)S(1)} %add_convert_fusion.refs_0_), channel_id=1, source_target_pairs={{0,3},{1,4},{2,5},{3,6},{4,7},{5,0},{6,1},{7,2},{8,11},{9,12},{10,... | collective-permute-start | bytes 221192 | tf_op jit(solution)/shard_map/ppermute | solution.py:305
  184.9 8.0 %collective-permute-start.45 = (bf16[48,768]{1,0:T(8,128)(2,1)S(1)}, bf16[48,768]{1,0:T(8,128)(2,1)S(1)}, u32[]{:S(2)}, u32[]{:S(2)}) collective-permute-start(bf16[48,768]{1,0:T(8,128)(2,1)S(1)} %add_convert_fusion.refs_0_), channel_id=1, source_target_pairs={{0,4},{1,5},{2,6},{3,7},{4,0},{5,1},{6,2},{7,3},{8,12},{9,13},{10,... | collective-permute-start | bytes 221192 | tf_op jit(solution)/shard_map/ppermute | solution.py:305
  (74 other events, 730.8 us)

commit v2 on v0

v2 whole, which is shorter than its diff:
```python
import functools
import math

import jax
import jax.numpy as jnp
from jax import lax
from jax.experimental import pallas as pl
from jax.experimental.pallas import tpu as pltpu
from jax.sharding import PartitionSpec as P

HEADS = 16
HD = 48
EXTRA = 16
SLOT = HD + EXTRA
LOG2E = math.log2(math.e)
LN2 = math.log(2.0)
ROWS, COLS, SIDE = 16, 8, 4
VMEM = 56 * 1024 * 1024
F32, BF16 = jnp.float32, jnp.bfloat16


def dot(left, right, dims):
    return lax.dot_general(left, right, (dims, ((), ())), preferred_element_type=F32)


def nn(left, right):
    return dot(left, right, ((1,), (0,)))


def nt(left, right):
    return dot(left, right, ((1,), (1,)))


def tn(left, right):
    return dot(left, right, ((0,), (0,)))


def along_z(k):
    return [(z * 2 + core, (z + k) % SIDE * 2 + core) for z in range(SIDE) for core in range(2)]


def other_core():
    return [(c, c ^ 1) for c in range(COLS)]


def home_to_block():
    half = ROWS // 2
    return [
        (row * COLS + col, ((row % 2) * half + col) * COLS + row // 2)
        for row in range(ROWS)
        for col in range(COLS)
    ]


def params(**more):
    return pltpu.CompilerParams(vmem_limit_bytes=VMEM, **more)


def whole(count):
    return [pl.BlockSpec(memory_space=pltpu.VMEM)] * count


SCALAR = pl.BlockSpec(memory_space=pltpu.SMEM)
HBM = pl.BlockSpec(memory_space=pl.ANY)


def array(shape, dtype):
    return jax.ShapeDtypeStruct(shape, dtype)


def rows_at(start, size):
    return pl.ds(pl.multiple_of(start, 16), size)


def place_kernel(first, at_ref, *refs):
    *pieces, out = refs
    for k, piece in enumerate(pieces):
        out[rows_at(at_ref[first + k], piece.shape[0]), :] = piece[...]


def place(at, first, pieces):
    rows = sum(p.shape[0] for p in pieces)
    return pl.pallas_call(
        functools.partial(place_kernel, first),
        out_shape=array((rows, pieces[0].shape[1]), pieces[0].dtype),
        in_specs=[SCALAR] + whole(len(pieces)),
        out_specs=whole(1)[0],
        compiler_params=params(),
    )(at, *pieces)


def copier(sems):
    count = iter(range(sems.shape[0]))

    def start(source, target):
        copy = pltpu.make_async_copy(source, target, sems.at[next(count)])
        copy.start()
        return copy

    return start


GROUP = 4


def forward_kernel(*refs):
    tokens_hbm, bias_hbm, q_hbm, w_hbm, mask_hbm, row_hbm, dh_hbm, expo_hbm, kv_hbm, num_hbm, stats_ref = refs[:11]
    tokens, w_ref, q_ref, mask_ref, row_ref, dh_ref, bias_ref, kv_ref, expo_ref, num_ref, tops, sems = refs[11:]
    start = copier(sems)
    rows, width = q_ref.shape[1], w_ref.shape[1]
    early = [start(tokens_hbm, tokens), start(w_hbm, w_ref)]
    late = [start(a, b) for a, b in ((q_hbm, q_ref), (mask_hbm, mask_ref), (row_hbm, row_ref), (dh_hbm, dh_ref))]
    bias_in = [start(bias_hbm.at[h], bias_ref.at[h]) for h in range(HEADS)]
    for copy in early:
        copy.wait()
    out = []
    for part in range(4):
        span = slice(part * width // 2, (part + 1) * width // 2)
        kv_ref[span, :] = nt(w_ref[span, :], tokens[...]).astype(BF16)
        out.append(start(kv_ref.at[span], kv_hbm.at[span]))
    tops[...] = jnp.zeros_like(tops)
    for copy in late:
        copy.wait()
    ones_k = jnp.ones((EXTRA, tokens.shape[0]), BF16)
    ones_q = jnp.ones((EXTRA, rows), BF16)
    live, dead = mask_ref[:HD, :], mask_ref[HD:, :]

    def head(h):
        mine = slice(h * HD, (h + 1) * HD)
        keys = jnp.concatenate([kv_ref[mine, :] * live, dead], axis=0)
        query = jnp.concatenate([q_ref[mine, :], ones_q], axis=0)
        scores = tn(query, keys) + bias_ref[h].astype(F32) * row_ref[0:1, :]
        top = jnp.max(scores, axis=-1, keepdims=True)
        expo = jnp.exp2(scores - top).astype(BF16)
        expo_ref[h] = expo
        values = jnp.concatenate([kv_ref[width + h * HD : width + (h + 1) * HD, :], ones_k], axis=0)
        out = nt(values, expo)
        num = out[:HD]
        num_ref[mine, :] = num
        stats_ref[h : h + 1, :] = out[HD : HD + 1]
        stats_ref[2 * HEADS + h : 2 * HEADS + h + 1, :] = jnp.sum(num * dh_ref[mine, :].astype(F32), axis=0, keepdims=True)
        lane = lax.broadcasted_iota(jnp.int32, tops.shape, 1)
        tops[...] = jnp.where(lane == h, top, tops[...])

    for g in range(0, HEADS, GROUP):
        for h in range(g, g + GROUP):
            bias_in[h].wait()
        for h in range(g, g + GROUP):
            head(h)
        out.append(start(expo_ref.at[pl.ds(g, GROUP)], expo_hbm.at[pl.ds(g, GROUP)]))
        span = pl.ds(g * HD, GROUP * HD)
        out.append(start(num_ref.at[span], num_hbm.at[span]))

    stats_ref[HEADS : 2 * HEADS, :] = tops[...].T[:HEADS, :]
    for copy in out:
        copy.wait()


def forward(tokens, bias, q, w, mask, row, dh):
    rows, span = bias.shape[1:]
    width = w.shape[1]
    return pl.pallas_call(
        forward_kernel,
        out_shape=(
            array(bias.shape, BF16),
            array((2 * width, span), BF16),
            array((width, rows), F32),
            array((3 * HEADS, rows), F32),
        ),
        in_specs=[HBM] * 7,
        out_specs=(HBM, HBM, HBM, *whole(1)),
        scratch_shapes=[
            pltpu.VMEM((span, width), BF16),
            pltpu.VMEM(w.shape, BF16),
            pltpu.VMEM(q.shape, BF16),
            pltpu.VMEM(mask.shape, BF16),
            pltpu.VMEM(row.shape, F32),
            pltpu.VMEM(dh.shape, BF16),
            pltpu.VMEM(bias.shape, BF16),
            pltpu.VMEM((2 * width, span), BF16),
            pltpu.VMEM(bias.shape, BF16),
            pltpu.VMEM((width, rows), F32),
            pltpu.VMEM((rows, 128), F32),
            pltpu.SemaphoreType.DMA((64,)),
        ],
        compiler_params=params(),
        cost_estimate=pl.CostEstimate(flops=4 * HEADS * rows * span * 256, bytes_accessed=4 * HEADS * rows * span, transcendentals=HEADS * rows * span),
    )(tokens, bias, q, w, mask, row, dh)


def merge(stats):
    top = functools.reduce(jnp.maximum, [s[HEADS : 2 * HEADS, :] for s in stats])
    total, inner = jnp.zeros_like(top), jnp.zeros_like(top)
    for s in stats:
        weight = jnp.exp2(s[HEADS : 2 * HEADS, :] - top)
        total += weight * s[:HEADS, :]
        inner += weight * s[2 * HEADS :, :]
    return total, top, inner


def merge_kernel(left_ref, right_ref, out_ref):
    for n, part in enumerate(merge([left_ref[...], right_ref[...]])):
        out_ref[n * HEADS : (n + 1) * HEADS, :] = part


def merge_pair(left, right):
    return pl.pallas_call(
        merge_kernel,
        out_shape=array(left.shape, F32),
        in_specs=whole(2),
        out_specs=whole(1)[0],
        compiler_params=params(),
    )(left, right)


def combine_kernel(*refs):
    stats, (own_ref, num_ref, dh_ref, dhf_ref, out_ref) = refs[:SIDE], refs[SIDE:]
    total, top, inner = merge([s[...] for s in stats])
    factor = jnp.exp2(own_ref[HEADS : 2 * HEADS, :] - top) / total
    shift = -factor * (inner / total)
    row = lax.broadcasted_iota(jnp.int32, (EXTRA, shift.shape[1]), 0)
    for h in range(HEADS):
        span = slice(h * HD, (h + 1) * HD)
        scale = factor[h : h + 1, :]
        dhf_ref[h * SLOT : h * SLOT + HD, :] = (dh_ref[span, :].astype(F32) * scale).astype(BF16)
        out_ref[span, :] = num_ref[span, :] * scale
        rest, rows = shift[h : h + 1, :], 0.0
        for n in range(3):
            part = rest.astype(BF16).astype(F32)
            rest = rest - part
            rows = jnp.where(row == n, part, rows)
        dhf_ref[h * SLOT + HD : (h + 1) * SLOT, :] = rows.astype(BF16)


def combine(stats, own, num, dh):
    width, rows = num.shape
    return pl.pallas_call(
        combine_kernel,
        out_shape=(array((HEADS * SLOT, rows), BF16), array((width, rows), F32)),
        in_specs=whole(SIDE + 3),
        out_specs=tuple(whole(2)),
        compiler_params=params(),
    )(*stats, own, num, dh)


def backward_kernel(expo_hbm, dhf_hbm, q_hbm, kv_hbm, w_hbm, dbias_hbm, dq_hbm, sent_ref, *refs):
    expo_ref, dhf_ref, q_ref, kv_ref, w_ref, dbias_ref, dq_ref, dkv, sems = refs
    start = copier(sems)
    width = q_ref.shape[0]
    early = [start(a, b) for a, b in ((dhf_hbm, dhf_ref), (kv_hbm, kv_ref), (q_hbm, q_ref))]
    expo_in = [start(expo_hbm.at[h], expo_ref.at[h]) for h in range(HEADS)]
    late = start(w_hbm, w_ref)
    for copy in early:
        copy.wait()
    ones_k = jnp.ones((EXTRA, kv_ref.shape[1]), BF16)

    def head(h):
        mine, other = slice(h * HD, (h + 1) * HD), slice(width + h * HD, width + (h + 1) * HD)
        values = jnp.concatenate([kv_ref[other, :], ones_k], axis=0)
        expo = expo_ref[h]
        d_score = (expo.astype(F32) * tn(dhf_ref[h * SLOT : (h + 1) * SLOT, :], values)).astype(BF16)
        dbias_ref[h] = d_score
        dq_ref[mine, :] = (nt(kv_ref[mine, :], d_score) * (1.0 / math.sqrt(HD))).astype(BF16)
        dkv[mine, :] = (nn(q_ref[mine, :], d_score) * LN2).astype(BF16)
        dkv[other, :] = nn(dhf_ref[h * SLOT : h * SLOT + HD, :], expo).astype(BF16)

    out = []
    for g in range(0, HEADS, GROUP):
        for h in range(g, g + GROUP):
            expo_in[h].wait()
        for h in range(g, g + GROUP):
            head(h)
        out.append(start(dbias_ref.at[pl.ds(g, GROUP)], dbias_hbm.at[pl.ds(g, GROUP)]))
    out.append(start(dq_ref, dq_hbm))
    late.wait()
    sent_ref[...] = tn(dkv[...], w_ref[...]).astype(BF16)
    for copy in out:
        copy.wait()


def backward(expo, dhf, q, kv, w):
    rows, span = expo.shape[1:]
    width = q.shape[0]
    return pl.pallas_call(
        backward_kernel,
        out_shape=[array(expo.shape, BF16), array(q.shape, BF16), array((span, width), BF16)],
        in_specs=[HBM] * 5,
        out_specs=[HBM, HBM, *whole(1)],
        scratch_shapes=[
            pltpu.VMEM(expo.shape, BF16),
            pltpu.VMEM(dhf.shape, BF16),
            pltpu.VMEM(q.shape, BF16),
            pltpu.VMEM(kv.shape, BF16),
            pltpu.VMEM(w.shape, BF16),
            pltpu.VMEM(expo.shape, BF16),
            pltpu.VMEM(q.shape, BF16),
            pltpu.VMEM((2 * width, span), BF16),
            pltpu.SemaphoreType.DMA((64,)),
        ],
        compiler_params=params(),
        cost_estimate=pl.CostEstimate(flops=8 * HEADS * rows * span * 256, bytes_accessed=4 * HEADS * rows * span, transcendentals=0),
    )(expo, dhf, q, kv, w)


def prepare_kernel(single_ref, cot_ref, wq_ref, wg_ref, wo_ref, q_ref, dh_ref):
    single = single_ref[...]
    q_ref[...] = (dot(wq_ref[...], single, ((0,), (1,))) * (LOG2E / math.sqrt(HD))).astype(BF16)
    gate = jax.nn.sigmoid(dot(wg_ref[...], single, ((0,), (1,))))
    dh_ref[...] = (nt(wo_ref[...], cot_ref[...]) * gate).astype(BF16)


def prepare(single, cotangent, wq, wg, wo):
    rows, width = single.shape
    return pl.pallas_call(
        prepare_kernel,
        out_shape=(array((width, rows), BF16), array((width, rows), BF16)),
        in_specs=whole(5),
        out_specs=tuple(whole(2)),
        compiler_params=params(),
    )(single, cotangent, wq, wg, wo)


def finish_kernel(*refs):
    parts, (single_ref, cot_ref, wo_ref, wg_ref, att_ref, rest_ref) = refs[:SIDE], refs[SIDE:]
    size = single_ref.shape[0]
    both = functools.reduce(jnp.add, [p[...].astype(F32) for p in parts])
    d_query, out = both[:size], both[size:]
    gate = jax.nn.sigmoid(nn(single_ref[...], wg_ref[...]))
    att_ref[...] = nn((out * gate).astype(BF16), wo_ref[...]).astype(BF16)
    d_gate = (nt(cot_ref[...], wo_ref[...]) * out * gate * (1.0 - gate)).astype(BF16)
    rest_ref[...] = d_query + nt(d_gate, wg_ref[...])


def finish(parts, single, cotangent, wo, wg):
    return pl.pallas_call(
        finish_kernel,
        out_shape=(array(single.shape, BF16), array(single.shape, F32)),
        in_specs=whole(SIDE + 4),
        out_specs=tuple(whole(2)),
        compiler_params=params(),
    )(*parts, single, cotangent, wo, wg)


def query_kernel(first, at_ref, dq_ref, out_ref, w_ref, mine_ref, other_ref, total, turned):
    total[...] = dot(dq_ref[...], w_ref[...], ((0,), (1,)))
    turned[...] = out_ref[...].T
    size = total.shape[0] // COLS
    for n, out in enumerate((mine_ref, other_ref)):
        for k in range(SIDE):
            rows = rows_at(at_ref[first + n * SIDE + k], size)
            out[2 * k * size : (2 * k + 1) * size, :] = total[rows, :].astype(BF16)
            out[(2 * k + 1) * size : (2 * k + 2) * size, :] = turned[rows, :].astype(BF16)


def query(at, first, dq, out, w):
    width, rows = dq.shape
    return pl.pallas_call(
        functools.partial(query_kernel, first),
        out_shape=[array((rows, width), BF16)] * 2,
        in_specs=[SCALAR] + whole(3),
        out_specs=whole(2),
        scratch_shapes=[pltpu.VMEM((rows, width), F32)] * 2,
        compiler_params=params(),
    )(at, dq, out, w)


def split_kernel(left_ref, right_ref, *outs):
    size = outs[0].shape[0]
    for n, out in enumerate(outs):
        rows = slice(n * size, (n + 1) * size)
        out[...] = (left_ref[rows, :].astype(F32) + right_ref[rows, :].astype(F32)).astype(BF16)


def add_split(terms):
    rows, width = terms[0].shape
    return pl.pallas_call(
        split_kernel,
        out_shape=[array((rows // SIDE, width), BF16)] * SIDE,
        in_specs=whole(2),
        out_specs=whole(SIDE),
        compiler_params=params(),
    )(*terms)


def total_kernel(attended_ref, kv_ref, rest_ref, out_ref):
    size = kv_ref.shape[0]
    out_ref[:size, :] = attended_ref[...]
    out_ref[size:, :] = (kv_ref[...].astype(F32) + rest_ref[...]).astype(BF16)


def total(attended, from_kv, rest):
    size, width = attended.shape
    return pl.pallas_call(
        total_kernel,
        out_shape=array((2 * size, width), BF16),
        in_specs=whole(3),
        out_specs=whole(1)[0],
        compiler_params=params(),
    )(attended, from_kv, rest)


def join_kernel(first, at_ref, own_ref, other_ref, *outs):
    size = own_ref.shape[0] // COLS
    mine = at_ref[first]
    for ref, shift in ((own_ref, mine), (other_ref, size - mine)):
        for n, out in enumerate(outs):
            for z in range(SIDE):
                source = slice((2 * z + n) * size, (2 * z + n + 1) * size)
                out[rows_at(2 * z * size + shift, size), :] = ref[source, :]


def join(at, first, own, other):
    rows, width = own.shape
    return pl.pallas_call(
        functools.partial(join_kernel, first),
        out_shape=[array((rows, width), BF16)] * 2,
        in_specs=[SCALAR] + whole(2),
        out_specs=whole(2),
        compiler_params=params(),
    )(at, own, other)


def shards(single, pair_bias, key_live, w_query, w_key, w_value, w_gate, w_out, cotangent):
    rows, width = single.shape
    span = pair_bias.shape[2]
    piece = rows // COLS
    col_index = lax.axis_index("col")
    z, core = col_index // 2, col_index % 2
    steps = jnp.arange(SIDE, dtype=jnp.int32)
    at = jnp.concatenate([
        ((z + steps) % SIDE * 2 + core) * piece,
        ((z + steps) % SIDE * 2 + 1 - core) * piece,
        (z - steps) % SIDE * 2 * piece,
        core[None] * piece,
    ]).astype(jnp.int32)
    both = ("row", "col")

    own = [lax.dynamic_slice_in_dim(a, col_index * piece, piece, 0) for a in (single, cotangent)]
    tokens = lax.ppermute(own[0], both, home_to_block())
    tokens = jnp.broadcast_to(tokens[None], (ROWS, piece, width))
    tokens = lax.all_to_all(tokens, "row", 0, 0).reshape(span, width)

    wkv = jnp.concatenate([w_key, w_value], axis=1).T
    q, dh = prepare(single, cotangent, w_query, w_gate, w_out)
    alive = key_live[None, :] > 0
    row = jnp.broadcast_to(jnp.where(alive, LOG2E, 0.0).astype(F32), (8, span))
    live = jnp.broadcast_to(alive, (HD, span)).astype(BF16)
    rest, spot = jnp.float32(-30000.0 * LOG2E), lax.broadcasted_iota(jnp.int32, (EXTRA, 1), 0)
    fill = jnp.zeros((EXTRA, 1), F32)
    for n in range(3):
        part = rest.astype(BF16).astype(F32)
        rest = rest - part
        fill = jnp.where(spot == n, part, fill)
    dead = jnp.where(alive, 0.0, fill).astype(BF16)

    mask = jnp.concatenate([live, dead], axis=0)
    expo, kv, num, stats = forward(tokens, pair_bias, q, wkv, mask, row, dh)
    chip = merge_pair(stats, lax.ppermute(stats, "col", other_core()))
    every = [chip] + [lax.ppermute(chip, "col", along_z(k)) for k in (1, 3, 2)]
    dhf, out = combine(every, stats, num, dh)
    d_bias, dq, from_kv = backward(expo, dhf, q, kv, wkv)

    from_kv = lax.all_to_all(from_kv.reshape(ROWS, piece, width), "row", 0, 0)
    from_kv = jnp.sum(from_kv.astype(F32), axis=0).astype(BF16)
    from_kv = lax.ppermute(from_kv, both, [(b, a) for a, b in home_to_block()])

    mine, other = query(at, 0, dq, out, w_query)
    other = lax.ppermute(other, "col", other_core())
    parts = add_split([mine, other])
    parts = [parts[0]] + [lax.ppermute(parts[k], "col", along_z(k)) for k in (1, 3, 2)]
    attended, rest = finish(parts, *own, w_out, w_gate)
    ends = total(attended, from_kv, rest)
    ends = place(at, 8, [ends] + [lax.ppermute(ends, "col", along_z(k)) for k in (1, 2, 3)])
    attended, d_single = join(at, 12, ends, lax.ppermute(ends, "col", other_core()))
    return (attended, d_bias, d_single)


def solution(mesh):
    placed = (
        P("row", None),
        P(None, "row", "col"),
        P("col"),
        P(),
        P(),
        P(),
        P(),
        P(),
        P("row", None),
    )
    return jax.shard_map(
        shards,
        mesh=mesh,
        in_specs=placed,
        out_specs=(P("row", None), P(None, "row", "col"), P("row", None)),
        check_vma=False,
    )
```

time: 465 us -> 148 us (0.32)
  waiting for transfers between devices: 296 us -> 23.3 us
  matrix products: 66.1 us -> 0 us
  Pallas kernels: 0 us -> 58.2 us
  starting transfers between devices: 0.16 us -> 49.7 us
  blocking collectives: 47.3 us -> 0 us
  other arithmetic: 17.1 us -> 3.14 us
  between operations: 14.2 us -> 0.83 us
  local copies, waits for them, and re-layouts: 22.1 us -> 12.2 us
    psum x3 -> x0, waiting for transfers between devices: 173 us -> none  [the longest x1 83.3 us: shards(): lax.psum(jnp.concatenate([d_k.reshape(span, width), d_val.reshape(span, w...]
    all_gather x1 -> x0, waiting for transfers between devices: 123 us -> none  [shards(): every_kv = lax.all_gather(own_kv, 'row', axis=0, tiled=True)]
    dot_general x16 -> x0, matrix products: 66.1 us -> none  [the longest x1 11.3 us: shards(): jnp.einsum('ihd,jhd->hij', q_heads, k_heads, preferred_element_type=jnp.f...]
    pallas_call x0 -> x11, Pallas kernels: none -> 58.2 us  [the longest x1 16.8 us: forward(): pl.pallas_call(forward_kernel, out_shape=(array(bias.shape, BF16), array(...]
    ppermute x0 -> x14, starting transfers between devices: none -> 35.9 us  [the longest x3 7.06 us: shards(): every = [chip] + [lax.ppermute(chip, 'col', along_z(k)) for k in (1, 3, 2)]]
    psum x1 -> x0, blocking collectives: 23.8 us -> none  [shards(): lax.psum((local_total * factor).astype(jnp.bfloat16), 'col')]
    pmax x1 -> x0, blocking collectives: 23.5 us -> none  [shards(): top = lax.pmax(local_top, 'col')]
    ppermute x0 -> x14, waiting for transfers between devices: none -> 15.2 us  [the longest x3 4.78 us: shards(): lax.ppermute(ends, 'col', along_z(k))]
  transfers between devices with their start and end apart: 4 -> 16, of which waited for: 4 -> 10; matrix products, arithmetic and copies ran while one was open for 3% -> 4% of each run, Pallas kernels for 0% -> 10%
where the time goes in v2:
time: 148 us; the launch traced here: 147 us
  Pallas kernels  58.2 us (39%)
  starting transfers between devices  49.7 us (34%)
  waiting for transfers between devices  23.3 us (16%)
  local copies, waits for them, and re-layouts  12.2 us (8%)
  other arithmetic  3.14 us (2%)
    pallas_call x1, Pallas kernels, forward(): pl.pallas_call(forward_kernel, out_shape=(array(bias.shape, BF16), array(...  16.8 us
    pallas_call x1, Pallas kernels, backward(): pl.pallas_call(backward_kernel, out_shape=[array(expo.shape, BF16), array...  16 us
    all_to_all x1, starting transfers between devices, shards(): tokens = lax.all_to_all(tokens, 'row', 0, 0).reshape(span, width)  10 us
    unnamed x36, local copies, waits for them, and re-layouts  8.14 us
    ppermute x3, starting transfers between devices, shards(): every = [chip] + [lax.ppermute(chip, 'col', along_z(k)) for k in (1, 3, 2)]  7.06 us
    all_to_all x1, waiting for transfers between devices, shards(): tokens = lax.all_to_all(tokens, 'row', 0, 0).reshape(span, width)  6.93 us
    ppermute x3, starting transfers between devices, shards(): lax.ppermute(ends, 'col', along_z(k))  6.91 us
    ppermute x1, starting transfers between devices, shards(): from_kv = lax.ppermute(from_kv, both, [(b, a) for a, b in home_to_block()])  5.42 us
  transfers between devices with their start and end apart: 16, of which 10 were waited for; matrix products, arithmetic and copies ran while one was open for 4% of the time, Pallas kernels for 10%

profile of v2, /device:TPU:1, one launch (start us, length us, event | category | flops | bytes accessed | tf_op | source)
XLA Modules:
  0.0 147.3 jit_solution(4509114331909191449)
XLA Ops:
  2.2 4.5 %collective-permute-start = (bf16[48,768]{1,0:T(8,128)(2,1)S(1)}, bf16[48,768]{1,0:T(8,128)(2,1)S(1)}, u32[]{:S(2)}, u32[]{:S(2)}) collective-permute-start(bf16[48,768]{1,0:T(8,128)(2,1)S(1)} %constant_dynamic-slice_fusion.1.refs_4_), channel_id=1, source_target_pairs={{0,0},{1,8},{2,16},{3,24},{4,32},{5,40},{6,48},{7,56},{8,64},{9,72... | collective-permute-start | bytes 221192 | tf_op jit(solution)/shard_map/ppermute | solution.py:439
  6.7 3.6 %collective-permute-done = bf16[48,768]{1,0:T(8,128)(2,1)S(1)} collective-permute-done((bf16[48,768]{1,0:T(8,128)(2,1)S(1)}, bf16[48,768]{1,0:T(8,128)(2,1)S(1)}, u32[]{:S(2)}, u32[]{:S(2)}) %collective-permute-start) | collective-permute-done | bytes 73760 | tf_op jit(solution)/shard_map/ppermute | solution.py:439
  11.3 10.0 %all-to-all-start = ((bf16[16,48,768]{2,1,0:T(8,128)(2,1)}), bf16[16,48,768]{2,1,0:T(8,128)(2,1)}, u32[]{:S(2)}, u32[]{:S(2)}) async-start(bf16[16,48,768]{2,1,0:T(8,128)(2,1)} %broadcast_in_dim.56), calls=%async_computation | async-start | bytes 2359296 | tf_op jit(solution)/shard_map/all_to_all | solution.py:441
  23.3 5.2 %shard_map.112 = (bf16[768,384]{1,0:T(8,128)(2,1)}, bf16[768,384]{1,0:T(8,128)(2,1)}) custom-call(bf16[384,768]{1,0:T(8,128)(2,1)} %single_ref.1, bf16[384,768]{1,0:T(8,128)(2,1)} %cot_ref.1, bf16[768,768]{1,0:T(8,128)(2,1)} %w_ref.1, bf16[768,768]{1,0:T(8,128)(2,1)} %refs_7_.1, bf16[768,768]{1,0:T(8,128)(2,1)} %refs_6_.1), custom_call_target="tpu_custom_call" | custom-call | tf_op jit(solution)/shard_map/pallas_call | solution.py:314
  29.3 1.5 %maximum_bitcast_fusion.refs_3_.w_hbm = bf16[1536,768]{1,0:T(8,128)(2,1)} fusion(bf16[768,768]{0,1:T(8,128)(2,1)S(1)} %copy.13, bf16[768,768]{0,1:T(8,128)(2,1)S(1)} %copy.12), kind=kLoop, calls=%fused_computation | loop fusion | flops 4718592 | bytes 4718592 | tf_op jit(solution)/shard_map/transpose | solution.py:443
  30.8 6.9 %all-to-all-done = bf16[16,48,768]{2,1,0:T(8,128)(2,1)} async-done(((bf16[16,48,768]{2,1,0:T(8,128)(2,1)}), bf16[16,48,768]{2,1,0:T(8,128)(2,1)}, u32[]{:S(2)}, u32[]{:S(2)}) %all-to-all-start) | async-done | bytes 1179680 | tf_op jit(solution)/shard_map/all_to_all | solution.py:441
  38.3 16.8 %shard_map.113 = (bf16[16,384,768]{2,1,0:T(8,128)(2,1)}, bf16[1536,768]{1,0:T(8,128)(2,1)}, f32[768,384]{1,0:T(8,128)}, f32[48,384]{1,0:T(8,128)}) custom-call(bf16[768,768]{1,0:T(8,128)(2,1)} %bitcast.1.refs_0_, bf16[16,384,768]{2,1,0:T(8,128)(2,1)} %refs_1_.1, bf16[768,384]{1,0:T(8,128)(2,1)} %get-tuple-element.24.refs_2_.q_hbm, ...), custom_call_target="tpu_custom_call" | custom-call | flops 4831838208 | bytes 18874368 | tf_op jit(solution)/shard_map/pallas_call | solution.py:162
  55.1 3.7 %collective-permute-start.1 = (f32[48,384]{1,0:T(8,128)}, f32[48,384]{1,0:T(8,128)S(1)}, u32[]{:S(2)}, u32[]{:S(2)}) collective-permute-start(f32[48,384]{1,0:T(8,128)} %get-tuple-element.27.left_ref.refs_4_), channel_id=1, source_target_pairs={{0,1},{1,0},{2,3},{3,2},{4,5},{5,4},{6,7},{7,6},{8,9},{9,8},{10,11... | collective-permute-start | bytes 221192 | tf_op jit(solution)/shard_map/ppermute | solution.py:458
  60.5 1.6 %shard_map.114.refs_0_ = f32[48,384]{1,0:T(8,128)} custom-call(f32[48,384]{1,0:T(8,128)} %get-tuple-element.27.left_ref.refs_4_, f32[48,384]{1,0:T(8,128)} %copy-done.15), custom_call_target="tpu_custom_call" | custom-call | tf_op jit(solution)/shard_map/pallas_call | solution.py:207
  62.1 2.1 %collective-permute-start.2 = (f32[48,384]{1,0:T(8,128)}, f32[48,384]{1,0:T(8,128)S(1)}, u32[]{:S(2)}, u32[]{:S(2)}) collective-permute-start(f32[48,384]{1,0:T(8,128)} %shard_map.114.refs_0_), channel_id=1, source_target_pairs={{0,2},{1,3},{2,4},{3,5},{4,6},{5,7},{6,0},{7,1},{8,10},{9,11},{10,... | collective-permute-start | bytes 221192 | tf_op jit(solution)/shard_map/ppermute | solution.py:459
  65.5 3.7 %collective-permute-start.4 = (f32[48,384]{1,0:T(8,128)}, f32[48,384]{1,0:T(8,128)S(1)}, u32[]{:S(2)}, u32[]{:S(2)}) collective-permute-start(f32[48,384]{1,0:T(8,128)} %shard_map.114.refs_0_), channel_id=1, source_target_pairs={{0,4},{1,5},{2,6},{3,7},{4,0},{5,1},{6,2},{7,3},{8,12},{9,13},{10,... | collective-permute-start | bytes 221192 | tf_op jit(solution)/shard_map/ppermute | solution.py:459
  69.4 1.9 %collective-permute-done.4.refs_3_ = f32[48,384]{1,0:T(8,128)S(1)} collective-permute-done((f32[48,384]{1,0:T(8,128)}, f32[48,384]{1,0:T(8,128)S(1)}, u32[]{:S(2)}, u32[]{:S(2)}) %collective-permute-start.4) | collective-permute-done | bytes 73760 | tf_op jit(solution)/shard_map/ppermute | solution.py:459
  71.9 3.1 %shard_map.115 = (bf16[1024,384]{1,0:T(8,128)(2,1)}, f32[768,384]{1,0:T(8,128)}) custom-call(f32[48,384]{1,0:T(8,128)} %shard_map.114.refs_0_, f32[48,384]{1,0:T(8,128)} %copy-done.11, f32[48,384]{1,0:T(8,128)} %copy-done.12, f32[48,384]{1,0:T(8,128)} %copy-done.13, f32[48,384]{1,0:T(8,128)} %get-tuple-element.27.left_ref.refs_4_, ...), custom_call_target="tpu_custom_call" | custom-call | tf_op jit(solution)/shard_map/pallas_call | solution.py:237
  75.0 16.0 %shard_map.116 = (bf16[16,384,768]{2,1,0:T(8,128)(2,1)}, bf16[768,384]{1,0:T(8,128)(2,1)}, bf16[768,768]{1,0:T(8,128)(2,1)}) custom-call(bf16[16,384,768]{2,1,0:T(8,128)(2,1)} %get-tuple-element.26.expo_hbm, bf16[1024,384]{1,0:T(8,128)(2,1)} %get-tuple-element.29.dhf_hbm, bf16[768,384]{1,0:T(8,128)(2,1)} %get-tuple-element.24.refs_2_.q_hbm, ...), custom_call_target="tpu_custom_call" | custom-call | flops 9663676416 | bytes 18874368 | tf_op jit(solution)/shard_map/pallas_call | solution.py:284
  91.0 3.7 %all-to-all-start.1 = ((bf16[16,48,768]{2,1,0:T(8,128)(2,1)}), bf16[16,48,768]{2,1,0:T(8,128)(2,1)S(1)}, u32[]{:S(2)}, u32[]{:S(2)}) async-start(bf16[16,48,768]{2,1,0:T(8,128)(2,1)} %bitcast.5), calls=%async_computation.1 | async-start | bytes 2359296 | tf_op jit(solution)/shard_map/all_to_all | solution.py:463
  95.5 3.5 %shard_map.117 = (bf16[384,768]{1,0:T(8,128)(2,1)}, bf16[384,768]{1,0:T(8,128)(2,1)}) custom-call(s32[13]{0:T(128)} %pad_add_fusion.at_ref, bf16[768,384]{1,0:T(8,128)(2,1)} %get-tuple-element.31.dq_ref, f32[768,384]{1,0:T(8,128)} %get-tuple-element.32.out_ref, bf16[768,768]{1,0:T(8,128)(2,1)} %w_ref.1), custom_call_target="tpu_custom_call" | custom-call | tf_op jit(solution)/shard_map/pallas_call | solution.py:357
  99.0 1.7 %collective-permute-start.5 = (bf16[384,768]{1,0:T(8,128)(2,1)}, bf16[384,768]{1,0:T(8,128)(2,1)S(1)}, u32[]{:S(2)}, u32[]{:S(2)}) collective-permute-start(bf16[384,768]{1,0:T(8,128)(2,1)} %get-tuple-element.34), channel_id=1, source_target_pairs={{0,1},{1,0},{2,3},{3,2},{4,5},{5,4},{6,7},{7,6},{8,9},{9,8},{10,11... | collective-permute-start | bytes 1769480 | tf_op jit(solution)/shard_map/ppermute | solution.py:468
  100.8 1.8 %collective-permute-done.5.right_ref = bf16[384,768]{1,0:T(8,128)(2,1)S(1)} collective-permute-done((bf16[384,768]{1,0:T(8,128)(2,1)}, bf16[384,768]{1,0:T(8,128)(2,1)S(1)}, u32[]{:S(2)}, u32[]{:S(2)}) %collective-permute-start.5) | collective-permute-done | bytes 589856 | tf_op jit(solution)/shard_map/ppermute | solution.py:468
  103.4 2.1 %shard_map.118 = (bf16[96,768]{1,0:T(8,128)(2,1)}, bf16[96,768]{1,0:T(8,128)(2,1)}, bf16[96,768]{1,0:T(8,128)(2,1)}, bf16[96,768]{1,0:T(8,128)(2,1)}) custom-call(bf16[384,768]{1,0:T(8,128)(2,1)} %get-tuple-element.33.left_ref, bf16[384,768]{1,0:T(8,128)(2,1)} %copy-done.2), custom_call_target="tpu_custom_call" | custom-call | tf_op jit(solution)/shard_map/pallas_call | solution.py:376
  106.7 1.5 collective-permute-start.7
  108.2 2.0 %collective-permute-start.8 = (bf16[96,768]{1,0:T(8,128)(2,1)}, bf16[96,768]{1,0:T(8,128)(2,1)S(1)}, u32[]{:S(2)}, u32[]{:S(2)}) collective-permute-start(bf16[96,768]{1,0:T(8,128)(2,1)} %get-tuple-element.38), channel_id=1, source_target_pairs={{0,4},{1,5},{2,6},{3,7},{4,0},{5,1},{6,2},{7,3},{8,12},{9,13},{10,... | collective-permute-start | bytes 442376 | tf_op jit(solution)/shard_map/ppermute | solution.py:470
  111.5 5.4 %collective-permute-start.9 = (bf16[48,768]{1,0:T(8,128)(2,1)S(1)}, bf16[48,768]{1,0:T(8,128)(2,1)S(1)}, u32[]{:S(2)}, u32[]{:S(2)}) collective-permute-start(bf16[48,768]{1,0:T(8,128)(2,1)S(1)} %reduce_sum.12), channel_id=1, source_target_pairs={{0,0},{8,1},{16,2},{24,3},{32,4},{40,5},{48,6},{56,7},{64,8},{72,9... | collective-permute-start | bytes 221192 | tf_op jit(solution)/shard_map/ppermute | solution.py:465
  116.9 1.5 %constant_dynamic-slice_fusion.refs_5_ = bf16[48,768]{1,0:T(8,128)(2,1)} fusion(bf16[384,768]{1,0:T(8,128)(2,1)} %cot_ref.1, s32[]{:T(128)S(6)} %select_n.65), kind=kLoop, calls=%fused_computation.21 | loop fusion | bytes 147460 | tf_op jit(solution)/shard_map/dynamic_slice | solution.py:438
  119.2 3.9 %shard_map.119 = (bf16[48,768]{1,0:T(8,128)(2,1)}, f32[48,768]{1,0:T(8,128)}) custom-call(bf16[96,768]{1,0:T(8,128)(2,1)} %get-tuple-element.35.refs_0_, bf16[96,768]{1,0:T(8,128)(2,1)} %copy-done.5, bf16[96,768]{1,0:T(8,128)(2,1)} %copy-done.6, bf16[96,768]{1,0:T(8,128)(2,1)} %copy-done.7, bf16[48,768]{1,0:T(8,128)(2,1)} %copy-done.4, ...), custom_call_target="tpu_custom_call" | custom-call | tf_op jit(solution)/shard_map/pallas_call | solution.py:335
  123.7 1.7 %shard_map.120.refs_0_ = bf16[96,768]{1,0:T(8,128)(2,1)} custom-call(bf16[48,768]{1,0:T(8,128)(2,1)} %get-tuple-element.39.attended_ref, bf16[48,768]{1,0:T(8,128)(2,1)} %copy-done.14, f32[48,768]{1,0:T(8,128)} %get-tuple-element.41.rest_ref), custom_call_target="tpu_custom_call" | custom-call | tf_op jit(solution)/shard_map/pallas_call | solution.py:393
  125.4 1.8 %collective-permute-start.10 = (bf16[96,768]{1,0:T(8,128)(2,1)}, bf16[96,768]{1,0:T(8,128)(2,1)S(1)}, u32[]{:S(2)}, u32[]{:S(2)}) collective-permute-start(bf16[96,768]{1,0:T(8,128)(2,1)} %shard_map.120.refs_0_), channel_id=1, source_target_pairs={{0,2},{1,3},{2,4},{3,5},{4,6},{5,7},{6,0},{7,1},{8,10},{9,11},{10,... | collective-permute-start | bytes 442376 | tf_op jit(solution)/shard_map/ppermute | solution.py:473
  127.2 3.7 %collective-permute-start.11 = (bf16[96,768]{1,0:T(8,128)(2,1)}, bf16[96,768]{1,0:T(8,128)(2,1)S(1)}, u32[]{:S(2)}, u32[]{:S(2)}) collective-permute-start(bf16[96,768]{1,0:T(8,128)(2,1)} %shard_map.120.refs_0_), channel_id=1, source_target_pairs={{0,4},{1,5},{2,6},{3,7},{4,0},{5,1},{6,2},{7,3},{8,12},{9,13},{10,... | collective-permute-start | bytes 442376 | tf_op jit(solution)/shard_map/ppermute | solution.py:473
  133.0 4.0 %collective-permute-done.11.refs_2_ = bf16[96,768]{1,0:T(8,128)(2,1)S(1)} collective-permute-done((bf16[96,768]{1,0:T(8,128)(2,1)}, bf16[96,768]{1,0:T(8,128)(2,1)S(1)}, u32[]{:S(2)}, u32[]{:S(2)}) %collective-permute-start.11) | collective-permute-done | bytes 147488 | tf_op jit(solution)/shard_map/ppermute | solution.py:473
  138.3 2.0 %shard_map.121.own_ref = bf16[384,768]{1,0:T(8,128)(2,1)} custom-call(s32[13]{0:T(128)} %pad_add_fusion.at_ref, bf16[96,768]{1,0:T(8,128)(2,1)} %shard_map.120.refs_0_, bf16[96,768]{1,0:T(8,128)(2,1)} %copy-done.8, bf16[96,768]{1,0:T(8,128)(2,1)} %copy-done.9, bf16[96,768]{1,0:T(8,128)(2,1)} %copy-done.10), custom_call_target="tpu_custom_call" | custom-call | tf_op jit(solution)/shard_map/pallas_call | solution.py:83
  140.3 2.0 %collective-permute-start.13 = (bf16[384,768]{1,0:T(8,128)(2,1)}, bf16[384,768]{1,0:T(8,128)(2,1)S(1)}, u32[]{:S(2)}, u32[]{:S(2)}) collective-permute-start(bf16[384,768]{1,0:T(8,128)(2,1)} %shard_map.121.own_ref), channel_id=1, source_target_pairs={{0,1},{1,0},{2,3},{3,2},{4,5},{5,4},{6,7},{7,6},{8,9},{9,8},{10,11... | collective-permute-start | bytes 1769480 | tf_op jit(solution)/shard_map/ppermute | solution.py:474
  142.3 1.8 %collective-permute-done.13.other_ref = bf16[384,768]{1,0:T(8,128)(2,1)S(1)} collective-permute-done((bf16[384,768]{1,0:T(8,128)(2,1)}, bf16[384,768]{1,0:T(8,128)(2,1)S(1)}, u32[]{:S(2)}, u32[]{:S(2)}) %collective-permute-start.13) | collective-permute-done | bytes 589856 | tf_op jit(solution)/shard_map/ppermute | solution.py:474
  145.0 2.3 %shard_map.122 = (bf16[384,768]{1,0:T(8,128)(2,1)}, bf16[384,768]{1,0:T(8,128)(2,1)}) custom-call(s32[13]{0:T(128)} %pad_add_fusion.at_ref, bf16[384,768]{1,0:T(8,128)(2,1)} %shard_map.121.own_ref, bf16[384,768]{1,0:T(8,128)(2,1)} %copy-done.3), custom_call_target="tpu_custom_call" | custom-call | tf_op jit(solution)/shard_map/pallas_call | solution.py:414
  (62 shorter events, 19.5 us)
Async XLA Ops:
  1.5 0.6 copy-start.4
  2.2 8.1 %collective-permute-start = (bf16[48,768]{1,0:T(8,128)(2,1)S(1)}, bf16[48,768]{1,0:T(8,128)(2,1)S(1)}, u32[]{:S(2)}, u32[]{:S(2)}) collective-permute-start(bf16[48,768]{1,0:T(8,128)(2,1)S(1)} %constant_dynamic-slice_fusion.1.refs_4_), channel_id=1, source_target_pairs={{0,0},{1,8},{2,16},{3,24},{4,32},{5,40},{6,48},{7,56},{8,64},{9,72... | collective-permute-start | bytes 221192 | tf_op jit(solution)/shard_map/ppermute | solution.py:439
  11.3 10.0 %copy-start.16 = (s32[768]{0:T(1024)S(1)}, s32[768]{0:T(1024)}, u32[]{:S(2)}) copy-start(s32[768]{0:T(1024)} %param.11) | copy-start | bytes 9220
  11.3 10.1 %copy-start = (bf16[768,768]{1,0:T(8,128)(2,1)S(1)}, bf16[768,768]{1,0:T(8,128)(2,1)}, u32[]{:S(2)}) copy-start(bf16[768,768]{1,0:T(8,128)(2,1)} %param.13) | copy-start | bytes 3538948
  11.3 26.4 %all-to-all-start = ((bf16[16,48,768]{2,1,0:T(8,128)(2,1)}), bf16[16,48,768]{2,1,0:T(8,128)(2,1)}, u32[]{:S(2)}, u32[]{:S(2)}) async-start(bf16[16,48,768]{2,1,0:T(8,128)(2,1)} %broadcast_in_dim.56), calls=%async_computation | async-start | bytes 2359296 | tf_op jit(solution)/shard_map/all_to_all | solution.py:441
  21.4 1.3 copy-start.1
  55.1 4.8 %collective-permute-start.1 = (f32[48,384]{1,0:T(8,128)}, f32[48,384]{1,0:T(8,128)S(1)}, u32[]{:S(2)}, u32[]{:S(2)}) collective-permute-start(f32[48,384]{1,0:T(8,128)} %get-tuple-element.27.left_ref.refs_4_), channel_id=1, source_target_pairs={{0,1},{1,0},{2,3},{3,2},{4,5},{5,4},{6,7},{7,6},{8,9},{9,8},{10,11... | collective-permute-start | bytes 221192 | tf_op jit(solution)/shard_map/ppermute | solution.py:458
  59.9 0.6 copy-start.15
  62.1 7.1 %collective-permute-start.2 = (f32[48,384]{1,0:T(8,128)}, f32[48,384]{1,0:T(8,128)S(1)}, u32[]{:S(2)}, u32[]{:S(2)}) collective-permute-start(f32[48,384]{1,0:T(8,128)} %shard_map.114.refs_0_), channel_id=1, source_target_pairs={{0,2},{1,3},{2,4},{3,5},{4,6},{5,7},{6,0},{7,1},{8,10},{9,11},{10,... | collective-permute-start | bytes 221192 | tf_op jit(solution)/shard_map/ppermute | solution.py:459
  64.2 5.1 %collective-permute-start.3 = (f32[48,384]{1,0:T(8,128)}, f32[48,384]{1,0:T(8,128)S(1)}, u32[]{:S(2)}, u32[]{:S(2)}) collective-permute-start(f32[48,384]{1,0:T(8,128)} %shard_map.114.refs_0_), channel_id=1, source_target_pairs={{0,6},{1,7},{2,0},{3,1},{4,2},{5,3},{6,4},{7,5},{8,14},{9,15},{10,... | collective-permute-start | bytes 221192 | tf_op jit(solution)/shard_map/ppermute | solution.py:459
  65.5 5.8 %collective-permute-start.4 = (f32[48,384]{1,0:T(8,128)}, f32[48,384]{1,0:T(8,128)S(1)}, u32[]{:S(2)}, u32[]{:S(2)}) collective-permute-start(f32[48,384]{1,0:T(8,128)} %shard_map.114.refs_0_), channel_id=1, source_target_pairs={{0,4},{1,5},{2,6},{3,7},{4,0},{5,1},{6,2},{7,3},{8,12},{9,13},{10,... | collective-permute-start | bytes 221192 | tf_op jit(solution)/shard_map/ppermute | solution.py:459
  69.2 2.1 %copy-start.11 = (f32[48,384]{1,0:T(8,128)}, f32[48,384]{1,0:T(8,128)S(1)}, u32[]{:S(2)}) copy-start(f32[48,384]{1,0:T(8,128)S(1)} %collective-permute-done.2.refs_1_) | copy-start | bytes 221188
  69.4 1.9 %copy-start.12 = (f32[48,384]{1,0:T(8,128)}, f32[48,384]{1,0:T(8,128)S(1)}, u32[]{:S(2)}) copy-start(f32[48,384]{1,0:T(8,128)S(1)} %collective-permute-done.3.refs_2_) | copy-start | bytes 221188
  71.2 0.7 copy-start.13
  91.0 20.3 %all-to-all-start.1 = ((bf16[16,48,768]{2,1,0:T(8,128)(2,1)}), bf16[16,48,768]{2,1,0:T(8,128)(2,1)S(1)}, u32[]{:S(2)}, u32[]{:S(2)}) async-start(bf16[16,48,768]{2,1,0:T(8,128)(2,1)} %bitcast.5), calls=%async_computation.1 | async-start | bytes 2359296 | tf_op jit(solution)/shard_map/all_to_all | solution.py:463
  99.0 3.6 %collective-permute-start.5 = (bf16[384,768]{1,0:T(8,128)(2,1)}, bf16[384,768]{1,0:T(8,128)(2,1)S(1)}, u32[]{:S(2)}, u32[]{:S(2)}) collective-permute-start(bf16[384,768]{1,0:T(8,128)(2,1)} %get-tuple-element.34), channel_id=1, source_target_pairs={{0,1},{1,0},{2,3},{3,2},{4,5},{5,4},{6,7},{7,6},{8,9},{9,8},{10,11... | collective-permute-start | bytes 1769480 | tf_op jit(solution)/shard_map/ppermute | solution.py:468
  102.6 0.8 copy-start.2
  105.5 12.9 %collective-permute-start.6 = (bf16[96,768]{1,0:T(8,128)(2,1)}, bf16[96,768]{1,0:T(8,128)(2,1)S(1)}, u32[]{:S(2)}, u32[]{:S(2)}) collective-permute-start(bf16[96,768]{1,0:T(8,128)(2,1)} %get-tuple-element.36), channel_id=1, source_target_pairs={{0,2},{1,3},{2,4},{3,5},{4,6},{5,7},{6,0},{7,1},{8,10},{9,11},{10,... | collective-permute-start | bytes 442376 | tf_op jit(solution)/shard_map/ppermute | solution.py:470
  106.7 11.7 %collective-permute-start.7 = (bf16[96,768]{1,0:T(8,128)(2,1)}, bf16[96,768]{1,0:T(8,128)(2,1)S(1)}, u32[]{:S(2)}, u32[]{:S(2)}) collective-permute-start(bf16[96,768]{1,0:T(8,128)(2,1)} %get-tuple-element.37), channel_id=1, source_target_pairs={{0,6},{1,7},{2,0},{3,1},{4,2},{5,3},{6,4},{7,5},{8,14},{9,15},{10,... | collective-permute-start | bytes 442376 | tf_op jit(solution)/shard_map/ppermute | solution.py:470
  108.2 10.2 %collective-permute-start.8 = (bf16[96,768]{1,0:T(8,128)(2,1)}, bf16[96,768]{1,0:T(8,128)(2,1)S(1)}, u32[]{:S(2)}, u32[]{:S(2)}) collective-permute-start(bf16[96,768]{1,0:T(8,128)(2,1)} %get-tuple-element.38), channel_id=1, source_target_pairs={{0,4},{1,5},{2,6},{3,7},{4,0},{5,1},{6,2},{7,3},{8,12},{9,13},{10,... | collective-permute-start | bytes 442376 | tf_op jit(solution)/shard_map/ppermute | solution.py:470
  111.5 11.6 %collective-permute-start.9 = (bf16[48,768]{1,0:T(8,128)(2,1)S(1)}, bf16[48,768]{1,0:T(8,128)(2,1)S(1)}, u32[]{:S(2)}, u32[]{:S(2)}) collective-permute-start(bf16[48,768]{1,0:T(8,128)(2,1)S(1)} %reduce_sum.12), channel_id=1, source_target_pairs={{0,0},{8,1},{16,2},{24,3},{32,4},{40,5},{48,6},{56,7},{64,8},{72,9... | collective-permute-start | bytes 221192 | tf_op jit(solution)/shard_map/ppermute | solution.py:465
  118.4 0.7 copy-start.5
  118.4 0.7 copy-start.6
  118.4 0.7 copy-start.7
  125.4 7.6 %collective-permute-start.10 = (bf16[96,768]{1,0:T(8,128)(2,1)}, bf16[96,768]{1,0:T(8,128)(2,1)S(1)}, u32[]{:S(2)}, u32[]{:S(2)}) collective-permute-start(bf16[96,768]{1,0:T(8,128)(2,1)} %shard_map.120.refs_0_), channel_id=1, source_target_pairs={{0,2},{1,3},{2,4},{3,5},{4,6},{5,7},{6,0},{7,1},{8,10},{9,11},{10,... | collective-permute-start | bytes 442376 | tf_op jit(solution)/shard_map/ppermute | solution.py:473
  127.2 9.9 %collective-permute-start.11 = (bf16[96,768]{1,0:T(8,128)(2,1)}, bf16[96,768]{1,0:T(8,128)(2,1)S(1)}, u32[]{:S(2)}, u32[]{:S(2)}) collective-permute-start(bf16[96,768]{1,0:T(8,128)(2,1)} %shard_map.120.refs_0_), channel_id=1, source_target_pairs={{0,4},{1,5},{2,6},{3,7},{4,0},{5,1},{6,2},{7,3},{8,12},{9,13},{10,... | collective-permute-start | bytes 442376 | tf_op jit(solution)/shard_map/ppermute | solution.py:473
  130.8 6.2 %collective-permute-start.12 = (bf16[96,768]{1,0:T(8,128)(2,1)}, bf16[96,768]{1,0:T(8,128)(2,1)S(1)}, u32[]{:S(2)}, u32[]{:S(2)}) collective-permute-start(bf16[96,768]{1,0:T(8,128)(2,1)} %shard_map.120.refs_0_), channel_id=1, source_target_pairs={{0,6},{1,7},{2,0},{3,1},{4,2},{5,3},{6,4},{7,5},{8,14},{9,15},{10,... | collective-permute-start | bytes 442376 | tf_op jit(solution)/shard_map/ppermute | solution.py:473
  133.0 4.0 %copy-start.8 = (bf16[96,768]{1,0:T(8,128)(2,1)}, bf16[96,768]{1,0:T(8,128)(2,1)S(1)}, u32[]{:S(2)}) copy-start(bf16[96,768]{1,0:T(8,128)(2,1)S(1)} %collective-permute-done.10.refs_1_) | copy-start | bytes 442372
  137.0 0.7 copy-start.9
  137.7 0.7 copy-start.10
  140.3 3.8 %collective-permute-start.13 = (bf16[384,768]{1,0:T(8,128)(2,1)}, bf16[384,768]{1,0:T(8,128)(2,1)S(1)}, u32[]{:S(2)}, u32[]{:S(2)}) collective-permute-start(bf16[384,768]{1,0:T(8,128)(2,1)} %shard_map.121.own_ref), channel_id=1, source_target_pairs={{0,1},{1,0},{2,3},{3,2},{4,5},{5,4},{6,7},{7,6},{8,9},{9,8},{10,11... | collective-permute-start | bytes 1769480 | tf_op jit(solution)/shard_map/ppermute | solution.py:474
  144.1 0.9 copy-start.3
  (1 other events, 0.6 us)

commit v3 on v2

v3 whole, which is shorter than its diff:
```python
import functools
import math

import jax
import jax.numpy as jnp
from jax import lax
from jax.experimental import pallas as pl
from jax.experimental.pallas import tpu as pltpu
from jax.sharding import PartitionSpec as P

HEADS = 16
HD = 48
EXTRA = 16
SLOT = HD + EXTRA
LOG2E = math.log2(math.e)
LN2 = math.log(2.0)
ROWS, COLS, SIDE = 16, 8, 4
VMEM = 56 * 1024 * 1024
F32, BF16 = jnp.float32, jnp.bfloat16


def dot(left, right, dims):
    return lax.dot_general(left, right, (dims, ((), ())), preferred_element_type=F32)


def nn(left, right):
    return dot(left, right, ((1,), (0,)))


def nt(left, right):
    return dot(left, right, ((1,), (1,)))


def tn(left, right):
    return dot(left, right, ((0,), (0,)))


def along_z(k):
    return [(z * 2 + core, (z + k) % SIDE * 2 + core) for z in range(SIDE) for core in range(2)]


def other_core():
    return [(c, c ^ 1) for c in range(COLS)]


def home_of(y, x, z, core):
    turn = (x - 2 * core) % SIDE
    return (turn + 1) % SIDE // 2, (z + 2 - (y - z)) % SIDE * 2 + turn // 2


def home_to_block():
    pairs = []
    for y in range(SIDE):
        for x in range(SIDE):
            for col in range(COLS):
                half, home = home_of(y, x, col // 2, col % 2)
                pairs.append(((2 * col + half) * COLS + home, (y * SIDE + x) * COLS + col))
    return pairs


def params(**more):
    return pltpu.CompilerParams(vmem_limit_bytes=VMEM, **more)


def whole(count):
    return [pl.BlockSpec(memory_space=pltpu.VMEM)] * count


SCALAR = pl.BlockSpec(memory_space=pltpu.SMEM)
HBM = pl.BlockSpec(memory_space=pl.ANY)


def array(shape, dtype):
    return jax.ShapeDtypeStruct(shape, dtype)


def rows_at(start, size):
    return pl.ds(pl.multiple_of(start, 16), size)


def copier(sems):
    count = iter(range(sems.shape[0]))

    def start(source, target):
        copy = pltpu.make_async_copy(source, target, sems.at[next(count)])
        copy.start()
        return copy

    return start


GROUP = 4
CHUNK = 32


def forward_kernel(first, at_ref, *refs):
    tokens_hbm, bias_hbm, q_hbm, w_hbm, mask_hbm, row_hbm, dh_hbm, expo_hbm, kv_hbm, num_hbm, stats_ref = refs[:11]
    tokens, w_ref, q_ref, mask_ref, row_ref, dh_ref, bias_ref, kv_ref, expo_ref, num_ref, tops, score_ref, sems = refs[-13:]
    start = copier(sems)
    rows, width = q_ref.shape[1], w_ref.shape[1]
    early = [start(w_hbm, w_ref)]
    for n in range(ROWS):
        early.append(start(tokens_hbm.at[n], tokens.at[rows_at(at_ref[first + n], tokens_hbm.shape[1])]))
    late = [start(a, b) for a, b in ((q_hbm, q_ref), (mask_hbm, mask_ref), (row_hbm, row_ref), (dh_hbm, dh_ref))]
    bias_in = [start(bias_hbm.at[h], bias_ref.at[h]) for h in range(HEADS)]
    for copy in early:
        copy.wait()
    out = []
    for part in range(4):
        span = slice(part * width // 2, (part + 1) * width // 2)
        kv_ref[span, :] = nt(w_ref[span, :], tokens[...]).astype(BF16)
        out.append(start(kv_ref.at[span], kv_hbm.at[span]))
    tops[...] = jnp.zeros_like(tops)
    for copy in late:
        copy.wait()
    ones_k = jnp.ones((EXTRA, tokens.shape[0]), BF16)
    ones_q = jnp.ones((EXTRA, rows), BF16)
    live, dead = mask_ref[:HD, :], mask_ref[HD:, :]

    def scores_of(h):
        mine = slice(h * HD, (h + 1) * HD)
        keys = jnp.concatenate([kv_ref[mine, :] * live, dead], axis=0)
        query = jnp.concatenate([q_ref[mine, :], ones_q], axis=0)
        score_ref[h % 2] = tn(query, keys)

    def soften(h):
        lane = lax.broadcasted_iota(jnp.int32, (CHUNK, 128), 1)
        for c in range(0, rows, CHUNK):
            part = slice(c, c + CHUNK)
            scores = score_ref[h % 2, part, :] + bias_ref[h, part, :].astype(F32) * row_ref[0:1, :]
            top = jnp.max(scores, axis=-1, keepdims=True)
            expo_ref[h, part, :] = jnp.exp2(scores - top).astype(BF16)
            tops[part, :] = jnp.where(lane == h, top, tops[part, :])

    def weigh(h):
        mine = slice(h * HD, (h + 1) * HD)
        values = jnp.concatenate([kv_ref[width + h * HD : width + (h + 1) * HD, :], ones_k], axis=0)
        sums = nt(values, expo_ref[h])
        num = sums[:HD]
        num_ref[mine, :] = num
        stats_ref[h : h + 1, :] = sums[HD : HD + 1]
        stats_ref[2 * HEADS + h : 2 * HEADS + h + 1, :] = jnp.sum(num * dh_ref[mine, :].astype(F32), axis=0, keepdims=True)

    scores_of(0)
    for h in range(HEADS):
        if h % GROUP == 0:
            for n in range(h, h + GROUP):
                bias_in[n].wait()
        if h + 1 < HEADS:
            scores_of(h + 1)
        if h:
            weigh(h - 1)
        soften(h)
        if h % GROUP == GROUP - 1:
            group = pl.ds(h + 1 - GROUP, GROUP)
            out.append(start(expo_ref.at[group], expo_hbm.at[group]))
    weigh(HEADS - 1)
    out.append(start(num_ref, num_hbm))

    stats_ref[HEADS : 2 * HEADS, :] = tops[...].T[:HEADS, :]
    for copy in out:
        copy.wait()


def forward(at, first, tokens, bias, q, w, mask, row, dh):
    rows, span = bias.shape[1:]
    width = w.shape[1]
    return pl.pallas_call(
        functools.partial(forward_kernel, first),
        out_shape=(
            array(bias.shape, BF16),
            array((2 * width, span), BF16),
            array((width, rows), F32),
            array((3 * HEADS, rows), F32),
        ),
        in_specs=[SCALAR] + [HBM] * 7,
        out_specs=(HBM, HBM, HBM, *whole(1)),
        scratch_shapes=[
            pltpu.VMEM((span, width), BF16),
            pltpu.VMEM(w.shape, BF16),
            pltpu.VMEM(q.shape, BF16),
            pltpu.VMEM(mask.shape, BF16),
            pltpu.VMEM(row.shape, F32),
            pltpu.VMEM(dh.shape, BF16),
            pltpu.VMEM(bias.shape, BF16),
            pltpu.VMEM((2 * width, span), BF16),
            pltpu.VMEM(bias.shape, BF16),
            pltpu.VMEM((width, rows), F32),
            pltpu.VMEM((rows, 128), F32),
            pltpu.VMEM((2, rows, span), F32),
            pltpu.SemaphoreType.DMA((64,)),
        ],
        compiler_params=params(),
        cost_estimate=pl.CostEstimate(flops=4 * HEADS * rows * span * 256, bytes_accessed=4 * HEADS * rows * span, transcendentals=HEADS * rows * span),
    )(at, tokens, bias, q, w, mask, row, dh)


def merge(stats):
    top = functools.reduce(jnp.maximum, [s[HEADS : 2 * HEADS, :] for s in stats])
    total, inner = jnp.zeros_like(top), jnp.zeros_like(top)
    for s in stats:
        weight = jnp.exp2(s[HEADS : 2 * HEADS, :] - top)
        total += weight * s[:HEADS, :]
        inner += weight * s[2 * HEADS :, :]
    return total, top, inner


def merge_kernel(left_ref, right_ref, out_ref):
    for n, part in enumerate(merge([left_ref[...], right_ref[...]])):
        out_ref[n * HEADS : (n + 1) * HEADS, :] = part


def merge_pair(left, right):
    return pl.pallas_call(
        merge_kernel,
        out_shape=array(left.shape, F32),
        in_specs=whole(2),
        out_specs=whole(1)[0],
        compiler_params=params(),
    )(left, right)


def backward_kernel(first, at_ref, *refs):
    stats, refs = refs[: SIDE + 1], refs[SIDE + 1 :]
    num_hbm, dh_hbm, expo_hbm, q_hbm, kv_hbm, w_hbm, dbias_hbm, dq_hbm, sent_hbm, out_hbm = refs[:10]
    num_ref, dh_ref, out_ref, expo_ref, dhf_ref, q_ref, kv_ref, w_ref, dbias_ref, dq_ref, dkv, prod_ref, sums, sems = refs[10:]
    start = copier(sems)
    width = q_ref.shape[0]
    early = [start(a, b) for a, b in ((dh_hbm, dh_ref), (num_hbm, num_ref), (kv_hbm, kv_ref), (q_hbm, q_ref))]
    expo_in = [start(expo_hbm.at[h], expo_ref.at[h]) for h in range(HEADS)]
    late = start(w_hbm, w_ref)
    total, top, inner = merge([s[...] for s in stats[1:]])
    factor = jnp.exp2(stats[0][HEADS : 2 * HEADS, :] - top) / total
    shift = -factor * (inner / total)
    row = lax.broadcasted_iota(jnp.int32, (EXTRA, shift.shape[1]), 0)
    for copy in early:
        copy.wait()
    ones_k = jnp.ones((EXTRA, kv_ref.shape[1]), BF16)

    def combine(h):
        mine, scale = slice(h * HD, (h + 1) * HD), factor[h : h + 1, :]
        dhf_ref[h * SLOT : h * SLOT + HD, :] = (dh_ref[mine, :].astype(F32) * scale).astype(BF16)
        out_ref[mine, :] = num_ref[mine, :] * scale
        rest, rows = shift[h : h + 1, :], 0.0
        for n in range(3):
            part = rest.astype(BF16).astype(F32)
            rest = rest - part
            rows = jnp.where(row == n, part, rows)
        dhf_ref[h * SLOT + HD : (h + 1) * SLOT, :] = rows.astype(BF16)

    def products(h):
        values = jnp.concatenate([kv_ref[width + h * HD : width + (h + 1) * HD, :], ones_k], axis=0)
        prod_ref[h % 2] = tn(dhf_ref[h * SLOT : (h + 1) * SLOT, :], values)

    def scores(h):
        for c in range(0, prod_ref.shape[1], CHUNK):
            part = slice(c, c + CHUNK)
            dbias_ref[h, part, :] = (expo_ref[h, part, :].astype(F32) * prod_ref[h % 2, part, :]).astype(BF16)

    def to_values(h):
        other = slice(width + h * HD, width + (h + 1) * HD)
        dkv[other, :] = nn(dhf_ref[h * SLOT : h * SLOT + HD, :], expo_ref[h]).astype(BF16)

    def to_queries_and_keys(h):
        mine, d_score = slice(h * HD, (h + 1) * HD), dbias_ref[h]
        dq_ref[mine, :] = (nt(kv_ref[mine, :], d_score) * (1.0 / math.sqrt(HD))).astype(BF16)
        dkv[mine, :] = (nn(q_ref[mine, :], d_score) * LN2).astype(BF16)

    out = []
    combine(0)
    products(0)
    for h in range(HEADS):
        if h % GROUP == 0:
            for n in range(h, h + GROUP):
                expo_in[n].wait()
        if h + 1 < HEADS:
            combine(h + 1)
            products(h + 1)
        to_values(h)
        if h:
            to_queries_and_keys(h - 1)
        scores(h)
        if h % GROUP == GROUP - 1:
            group = pl.ds(h + 1 - GROUP, GROUP)
            out.append(start(dbias_ref.at[group], dbias_hbm.at[group]))
    to_queries_and_keys(HEADS - 1)
    out.append(start(dq_ref, dq_hbm))
    out.append(start(out_ref, out_hbm))
    late.wait()
    sums[...] = tn(dkv[...], w_ref[...]).astype(BF16)
    size = sums.shape[0] // ROWS
    for n in range(ROWS):
        out.append(start(sums.at[rows_at(at_ref[first + n], size)], sent_hbm.at[n]))
    for copy in out:
        copy.wait()


def backward(at, first, own, every, num, dh, expo, q, kv, w):
    rows, span = expo.shape[1:]
    width = q.shape[0]
    return pl.pallas_call(
        functools.partial(backward_kernel, first),
        out_shape=[array(expo.shape, BF16), array(q.shape, BF16), array((ROWS, span // ROWS, width), BF16), array(num.shape, F32)],
        in_specs=[SCALAR] + whole(SIDE + 1) + [HBM] * 6,
        out_specs=[HBM] * 4,
        scratch_shapes=[
            pltpu.VMEM(num.shape, F32),
            pltpu.VMEM(dh.shape, BF16),
            pltpu.VMEM(num.shape, F32),
            pltpu.VMEM(expo.shape, BF16),
            pltpu.VMEM((HEADS * SLOT, rows), BF16),
            pltpu.VMEM(q.shape, BF16),
            pltpu.VMEM(kv.shape, BF16),
            pltpu.VMEM(w.shape, BF16),
            pltpu.VMEM(expo.shape, BF16),
            pltpu.VMEM(q.shape, BF16),
            pltpu.VMEM((2 * width, span), BF16),
            pltpu.VMEM((2, rows, span), F32),
            pltpu.VMEM((span, width), BF16),
            pltpu.SemaphoreType.DMA((64,)),
        ],
        compiler_params=params(),
        cost_estimate=pl.CostEstimate(flops=8 * HEADS * rows * span * 256, bytes_accessed=4 * HEADS * rows * span, transcendentals=0),
    )(at, own, *every, num, dh, expo, q, kv, w)


def prepare_kernel(single_ref, cot_ref, own_ref, own_cot_ref, wq_ref, wg_ref, wo_ref, q_ref, dh_ref, gate_ref, dhid_ref):
    single = single_ref[...]
    q_ref[...] = (dot(wq_ref[...], single, ((0,), (1,))) * (LOG2E / math.sqrt(HD))).astype(BF16)
    gate = jax.nn.sigmoid(dot(wg_ref[...], single, ((0,), (1,))))
    dh_ref[...] = (nt(wo_ref[...], cot_ref[...]) * gate).astype(BF16)
    gate_ref[...] = jax.nn.sigmoid(nn(own_ref[...], wg_ref[...]))
    dhid_ref[...] = nt(own_cot_ref[...], wo_ref[...])


def prepare(single, cotangent, own, wq, wg, wo):
    rows, width = single.shape
    return pl.pallas_call(
        prepare_kernel,
        out_shape=[array((width, rows), BF16)] * 2 + [array(own[0].shape, F32)] * 2,
        in_specs=whole(7),
        out_specs=whole(4),
        compiler_params=params(),
    )(single, cotangent, *own, wq, wg, wo)


def finish_kernel(*refs):
    parts, (gate_ref, dhid_ref, wo_ref, wg_ref, out_ref) = refs[:SIDE], refs[SIDE:]
    size = gate_ref.shape[0]
    both = functools.reduce(jnp.add, [p[...].astype(F32) for p in parts])
    d_query, out, gate = both[:size], both[size:], gate_ref[...]
    out_ref[:size, :] = nn((out * gate).astype(BF16), wo_ref[...]).astype(BF16)
    d_gate = (dhid_ref[...] * out * gate * (1.0 - gate)).astype(BF16)
    out_ref[size:, :] = (d_query + nt(d_gate, wg_ref[...])).astype(BF16)


def finish(parts, gate, d_hidden, wo, wg):
    return pl.pallas_call(
        finish_kernel,
        out_shape=array(parts[0].shape, BF16),
        in_specs=whole(SIDE + 4),
        out_specs=whole(1)[0],
        compiler_params=params(),
    )(*parts, gate, d_hidden, wo, wg)


def query_kernel(first, at_ref, dq_ref, out_ref, w_ref, mine_ref, other_ref, total, turned):
    total[...] = dot(dq_ref[...], w_ref[...], ((0,), (1,)))
    turned[...] = out_ref[...].T
    size = total.shape[0] // COLS
    for n, out in enumerate((mine_ref, other_ref)):
        for k in range(SIDE):
            rows = rows_at(at_ref[first + n * SIDE + k], size)
            out[2 * k * size : (2 * k + 1) * size, :] = total[rows, :].astype(BF16)
            out[(2 * k + 1) * size : (2 * k + 2) * size, :] = turned[rows, :].astype(BF16)


def query(at, first, dq, out, w):
    width, rows = dq.shape
    return pl.pallas_call(
        functools.partial(query_kernel, first),
        out_shape=[array((rows, width), BF16)] * 2,
        in_specs=[SCALAR] + whole(3),
        out_specs=whole(2),
        scratch_shapes=[pltpu.VMEM((rows, width), F32)] * 2,
        compiler_params=params(),
    )(at, dq, out, w)


def split_kernel(left_ref, right_ref, *outs):
    size = outs[0].shape[0]
    for n, out in enumerate(outs):
        rows = slice(n * size, (n + 1) * size)
        out[...] = (left_ref[rows, :].astype(F32) + right_ref[rows, :].astype(F32)).astype(BF16)


def add_split(terms):
    rows, width = terms[0].shape
    return pl.pallas_call(
        split_kernel,
        out_shape=[array((rows // SIDE, width), BF16)] * SIDE,
        in_specs=whole(2),
        out_specs=whole(SIDE),
        compiler_params=params(),
    )(*terms)


def total_kernel(kv_ref, ends_ref, out_ref):
    size = kv_ref.shape[0]
    out_ref[:size, :] = ends_ref[:size, :]
    out_ref[size:, :] = (ends_ref[size:, :].astype(F32) + kv_ref[...].astype(F32)).astype(BF16)


def total(from_kv, ends):
    return pl.pallas_call(
        total_kernel,
        out_shape=array(ends.shape, BF16),
        in_specs=whole(2),
        out_specs=whole(1)[0],
        compiler_params=params(),
    )(from_kv, ends)


def join_kernel(first, at_ref, *refs):
    ends, outs = refs[: 2 * SIDE], refs[2 * SIDE :]
    size = ends[0].shape[0] // 2
    core = at_ref[first + SIDE]
    for k, end in enumerate(ends):
        shift = core if k < SIDE else size - core
        for n, out in enumerate(outs):
            out[rows_at(at_ref[first + k % SIDE] + shift, size), :] = end[n * size : (n + 1) * size, :]


def join(at, first, near, far):
    size, width = near[0].shape
    return pl.pallas_call(
        functools.partial(join_kernel, first),
        out_shape=[array((size // 2 * COLS, width), BF16)] * 2,
        in_specs=[SCALAR] + whole(COLS),
        out_specs=whole(2),
        compiler_params=params(),
    )(at, *near, *far)


def shards(single, pair_bias, key_live, w_query, w_key, w_value, w_gate, w_out, cotangent):
    rows, width = single.shape
    span = pair_bias.shape[2]
    piece = rows // COLS
    col_index = lax.axis_index("col")
    z, core = col_index // 2, col_index % 2
    steps = jnp.arange(SIDE, dtype=jnp.int32)
    at = jnp.concatenate([
        ((z + steps) % SIDE * 2 + core) * piece,
        ((z + steps) % SIDE * 2 + 1 - core) * piece,
        (z - steps) % SIDE * 2 * piece,
        core[None] * piece,
        jnp.stack([half * rows + home * piece for y in range(SIDE) for x in range(SIDE) for half, home in [home_of(y, x, z, core)]]),
    ]).astype(jnp.int32)
    both = ("row", "col")

    own = [lax.dynamic_slice_in_dim(a, col_index * piece, piece, 0) for a in (single, cotangent)]
    tokens = lax.ppermute(own[0], both, home_to_block())
    tokens = lax.all_to_all(jnp.broadcast_to(tokens[None], (ROWS, *tokens.shape)), "row", 0, 0)
    wkv = jnp.concatenate([w_key, w_value], axis=1).T
    q, dh, gate, d_hidden = prepare(single, cotangent, own, w_query, w_gate, w_out)
    alive = key_live[None, :] > 0
    row = jnp.broadcast_to(jnp.where(alive, LOG2E, 0.0).astype(F32), (8, span))
    live = jnp.broadcast_to(alive, (HD, span)).astype(BF16)
    rest, spot = jnp.float32(-30000.0 * LOG2E), lax.broadcasted_iota(jnp.int32, (EXTRA, 1), 0)
    fill = jnp.zeros((EXTRA, 1), F32)
    for n in range(3):
        part = rest.astype(BF16).astype(F32)
        rest = rest - part
        fill = jnp.where(spot == n, part, fill)
    dead = jnp.where(alive, 0.0, fill).astype(BF16)

    mask = jnp.concatenate([live, dead], axis=0)
    expo, kv, num, stats = forward(at, 13, tokens, pair_bias, q, wkv, mask, row, dh)
    chip = merge_pair(stats, lax.ppermute(stats, "col", other_core()))
    every = [chip] + [lax.ppermute(chip, "col", along_z(k)) for k in (1, 3, 2)]
    d_bias, dq, from_kv, out = backward(at, 13, stats, every, num, dh, expo, q, kv, wkv)

    from_kv = lax.all_to_all(from_kv, "row", 0, 0)
    mine, other = query(at, 0, dq, out, w_query)
    other = lax.ppermute(other, "col", other_core())
    parts = add_split([mine, other])
    parts = [parts[0]] + [lax.ppermute(parts[k], "col", along_z(k)) for k in (1, 3, 2)]
    ends = finish(parts, gate, d_hidden, w_out, w_gate)
    from_kv = jnp.sum(from_kv.astype(F32), axis=0).astype(BF16)
    from_kv = lax.ppermute(from_kv, both, [(b, a) for a, b in home_to_block()])
    ends = total(from_kv, ends)
    near = [ends] + [lax.ppermute(ends, "col", along_z(k)) for k in (1, 2, 3)]
    far = [lax.ppermute(end, "col", other_core()) for end in near]
    attended, d_single = join(at, 8, near, far)
    return (attended, d_bias, d_single)


def solution(mesh):
    placed = (
        P("row", None),
        P(None, "row", "col"),
        P("col"),
        P(),
        P(),
        P(),
        P(),
        P(),
        P("row", None),
    )
    return jax.shard_map(
        shards,
        mesh=mesh,
        in_specs=placed,
        out_specs=(P("row", None), P(None, "row", "col"), P("row", None)),
        check_vma=False,
    )
```

time: 148 us -> 132 us (0.89)
  Pallas kernels: 58.2 us -> 50.5 us
  starting transfers between devices: 49.7 us -> 43.6 us
  waiting for transfers between devices: 23.3 us -> 21.7 us
  local copies, waits for them, and re-layouts: 12.2 us -> 10.7 us
    pallas_call x8 -> x6, Pallas kernels: 51 us -> 43.3 us  [the longest x1 16 us: backward(): pl.pallas_call(functools.partial(backward_kernel, first), out_shape=[arra...]
    all_to_all x2, starting transfers between devices: 13.7 us -> 10 us  [the longest x1 6.32 us: shards(): lax.all_to_all(jnp.broadcast_to(tokens[None], (ROWS, *tokens.shape)), 'ro...]
    ppermute x3, starting transfers between devices: 7.06 us -> 3.48 us  [shards(): every = [chip] + [lax.ppermute(chip, 'col', along_z(k)) for k in (1, 3, 2)]]
    ppermute x4 -> x7, starting transfers between devices: 8.86 us -> 11.9 us  [the longest x4 6.02 us: shards(): far = [lax.ppermute(end, 'col', other_core()) for end in near]]
    ppermute x1, starting transfers between devices: 5.42 us -> 2.8 us  [shards(): from_kv = lax.ppermute(from_kv, both, [(b, a) for a, b in home_to_block()])]
    ppermute x1, waiting for transfers between devices: 3.55 us -> 1.17 us  [shards(): tokens = lax.ppermute(own[0], both, home_to_block())]
    unnamed x36 -> x40, local copies, waits for them, and re-layouts: 8.14 us -> 5.99 us
    ppermute x1, starting transfers between devices: 4.5 us -> 6.5 us  [shards(): tokens = lax.ppermute(own[0], both, home_to_block())]
  transfers between devices with their start and end apart: 16 -> 19, of which waited for: 10 -> 12; matrix products, arithmetic and copies ran while one was open for 4% -> 5% of each run, Pallas kernels for 10% -> 11%
where the time goes in v3:
time: 132 us; the launch traced here: 131 us
  Pallas kernels  50.5 us (38%)
  starting transfers between devices  43.6 us (33%)
  waiting for transfers between devices  21.7 us (16%)
  local copies, waits for them, and re-layouts  10.7 us (8%)
  other arithmetic  3.14 us (2%)
    pallas_call x1, Pallas kernels, backward(): pl.pallas_call(functools.partial(backward_kernel, first), out_shape=[arra...  16 us
    pallas_call x1, Pallas kernels, forward(): pl.pallas_call(functools.partial(forward_kernel, first), out_shape=(array...  14.4 us
    ppermute x1, starting transfers between devices, shards(): tokens = lax.ppermute(own[0], both, home_to_block())  6.5 us
    all_to_all x1, starting transfers between devices, shards(): lax.all_to_all(jnp.broadcast_to(tokens[None], (ROWS, *tokens.shape)), 'ro...  6.32 us
    ppermute x4, starting transfers between devices, shards(): far = [lax.ppermute(end, 'col', other_core()) for end in near]  6.02 us
    unnamed x40, local copies, waits for them, and re-layouts  5.99 us
    ppermute x3, starting transfers between devices, shards(): near = [ends] + [lax.ppermute(ends, 'col', along_z(k)) for k in (1, 2, 3)]  5.89 us
    pallas_call x1, Pallas kernels, prepare(): pl.pallas_call(prepare_kernel, out_shape=[array((width, rows), BF16)] * 2...  5.52 us
  transfers between devices with their start and end apart: 19, of which 12 were waited for; matrix products, arithmetic and copies ran while one was open for 5% of the time, Pallas kernels for 11%

profile of v3, /device:TPU:1, one launch (start us, length us, event | category | flops | bytes accessed | tf_op | source)
XLA Modules:
  0.0 130.9 jit_solution(14497364746030827048)
XLA Ops:
  1.5 6.5 %collective-permute-start = (bf16[48,768]{1,0:T(8,128)(2,1)S(1)}, bf16[48,768]{1,0:T(8,128)(2,1)S(1)}, u32[]{:S(2)}, u32[]{:S(2)}) collective-permute-start(bf16[48,768]{1,0:T(8,128)(2,1)S(1)} %constant_dynamic-slice_fusion.1.own_ref), channel_id=1, source_target_pairs={{4,0},{29,1},{32,2},{57,3},{68,4},{93,5},{96,6},{121,7},{12,8},{21... | collective-permute-start | bytes 221192 | tf_op jit(solution)/shard_map/ppermute | solution.py:462
  8.7 1.2 collective-permute-done
  9.9 1.1 broadcast_in_dim.56
  11.0 6.3 %all-to-all-start = ((bf16[16,48,768]{2,1,0:T(8,128)(2,1)}), bf16[16,48,768]{2,1,0:T(8,128)(2,1)}, u32[]{:S(2)}, u32[]{:S(2)}) async-start(bf16[16,48,768]{2,1,0:T(8,128)(2,1)} %broadcast_in_dim.56), calls=%async_computation | async-start | bytes 2359296 | tf_op jit(solution)/shard_map/all_to_all | solution.py:463
  19.6 1.5 %constant_dynamic-slice_fusion.own_cot_ref = bf16[48,768]{1,0:T(8,128)(2,1)} fusion(bf16[384,768]{1,0:T(8,128)(2,1)} %cot_ref.1, s32[]{:T(128)S(6)} %select_n.253), kind=kLoop, calls=%fused_computation.20 | loop fusion | bytes 147460 | tf_op jit(solution)/shard_map/dynamic_slice | solution.py:461
  21.1 5.5 %shard_map.112 = (bf16[768,384]{1,0:T(8,128)(2,1)}, bf16[768,384]{1,0:T(8,128)(2,1)}, f32[48,768]{1,0:T(8,128)}, f32[48,768]{1,0:T(8,128)}) custom-call(bf16[384,768]{1,0:T(8,128)(2,1)} %single_ref.1, bf16[384,768]{1,0:T(8,128)(2,1)} %cot_ref.1, bf16[48,768]{1,0:T(8,128)(2,1)} %copy-done.3, bf16[48,768]{1,0:T(8,128)(2,1)} %constant_dynamic-slice_fusion.own_cot_ref, ...), custom_call_target="tpu_custom_call" | custom-call | tf_op jit(solution)/shard_map/pallas_call | solution.py:338
  28.0 1.5 %maximum_bitcast_fusion.refs_3_.refs_10_ = bf16[1536,768]{1,0:T(8,128)(2,1)} fusion(bf16[768,768]{0,1:T(8,128)(2,1)S(1)} %copy.13, bf16[768,768]{0,1:T(8,128)(2,1)S(1)} %copy.12), kind=kLoop, calls=%fused_computation | loop fusion | flops 4718592 | bytes 4718592 | tf_op jit(solution)/shard_map/transpose | solution.py:464
  29.6 4.0 %all-to-all-done.refs_0_ = bf16[16,48,768]{2,1,0:T(8,128)(2,1)} async-done(((bf16[16,48,768]{2,1,0:T(8,128)(2,1)}), bf16[16,48,768]{2,1,0:T(8,128)(2,1)}, u32[]{:S(2)}, u32[]{:S(2)}) %all-to-all-start) | async-done | bytes 1179680 | tf_op jit(solution)/shard_map/all_to_all | solution.py:463
  34.1 14.4 %shard_map.113 = (bf16[16,384,768]{2,1,0:T(8,128)(2,1)}, bf16[1536,768]{1,0:T(8,128)(2,1)}, f32[768,384]{1,0:T(8,128)}, f32[48,384]{1,0:T(8,128)}) custom-call(s32[29]{0:T(128)} %concatenate.9.at_ref, bf16[16,48,768]{2,1,0:T(8,128)(2,1)} %all-to-all-done.refs_0_, bf16[16,384,768]{2,1,0:T(8,128)(2,1)} %refs_1_.1, ...), custom_call_target="tpu_custom_call" | custom-call | flops 4831838208 | bytes 18874368 | tf_op jit(solution)/shard_map/pallas_call | solution.py:168
  48.6 4.2 %collective-permute-start.1 = (f32[48,384]{1,0:T(8,128)}, f32[48,384]{1,0:T(8,128)S(1)}, u32[]{:S(2)}, u32[]{:S(2)}) collective-permute-start(f32[48,384]{1,0:T(8,128)} %get-tuple-element.25.left_ref.refs_0_), channel_id=1, source_target_pairs={{0,1},{1,0},{2,3},{3,2},{4,5},{5,4},{6,7},{7,6},{8,9},{9,8},{10,11... | collective-permute-start | bytes 221192 | tf_op jit(solution)/shard_map/ppermute | solution.py:479
  52.7 1.1 collective-permute-done.1.right_ref
  54.5 1.6 %shard_map.114.refs_1_ = f32[48,384]{1,0:T(8,128)} custom-call(f32[48,384]{1,0:T(8,128)} %get-tuple-element.25.left_ref.refs_0_, f32[48,384]{1,0:T(8,128)} %copy-done.14), custom_call_target="tpu_custom_call" | custom-call | tf_op jit(solution)/shard_map/pallas_call | solution.py:214
  56.1 1.9 %collective-permute-start.4 = (f32[48,384]{1,0:T(8,128)}, f32[48,384]{1,0:T(8,128)S(1)}, u32[]{:S(2)}, u32[]{:S(2)}) collective-permute-start(f32[48,384]{1,0:T(8,128)} %shard_map.114.refs_1_), channel_id=1, source_target_pairs={{0,4},{1,5},{2,6},{3,7},{4,0},{5,1},{6,2},{7,3},{8,12},{9,13},{10,... | collective-permute-start | bytes 221192 | tf_op jit(solution)/shard_map/ppermute | solution.py:480
  59.5 1.4 %collective-permute-done.4.refs_4_ = f32[48,384]{1,0:T(8,128)S(1)} collective-permute-done((f32[48,384]{1,0:T(8,128)}, f32[48,384]{1,0:T(8,128)S(1)}, u32[]{:S(2)}, u32[]{:S(2)}) %collective-permute-start.4) | collective-permute-done | bytes 73760 | tf_op jit(solution)/shard_map/ppermute | solution.py:480
  61.0 2.1 %collective-permute-done.3.refs_3_ = f32[48,384]{1,0:T(8,128)S(1)} collective-permute-done((f32[48,384]{1,0:T(8,128)}, f32[48,384]{1,0:T(8,128)S(1)}, u32[]{:S(2)}, u32[]{:S(2)}) %collective-permute-start.3) | collective-permute-done | bytes 73760 | tf_op jit(solution)/shard_map/ppermute | solution.py:480
  64.2 16.0 %shard_map.115 = (bf16[16,384,768]{2,1,0:T(8,128)(2,1)}, bf16[768,384]{1,0:T(8,128)(2,1)}, bf16[16,48,768]{2,1,0:T(8,128)(2,1)}, f32[768,384]{1,0:T(8,128)}) custom-call(s32[29]{0:T(128)} %concatenate.9.at_ref, f32[48,384]{1,0:T(8,128)} %get-tuple-element.25.left_ref.refs_0_, f32[48,384]{1,0:T(8,128)} %shard_map.114.refs_1_, f32[48,384]{1,0:T(8,128)} %copy-done.18, ...), custom_call_target="tpu_custom_call" | custom-call | flops 9663676416 | bytes 18874368 | tf_op jit(solution)/shard_map/pallas_call | solution.py:301
  80.2 3.7 %all-to-all-start.1 = ((bf16[16,48,768]{2,1,0:T(8,128)(2,1)}), bf16[16,48,768]{2,1,0:T(8,128)(2,1)S(1)}, u32[]{:S(2)}, u32[]{:S(2)}) async-start(bf16[16,48,768]{2,1,0:T(8,128)(2,1)} %get-tuple-element.29), calls=%async_computation.1 | async-start | bytes 2359296 | tf_op jit(solution)/shard_map/all_to_all | solution.py:483
  84.0 3.5 %shard_map.116 = (bf16[384,768]{1,0:T(8,128)(2,1)}, bf16[384,768]{1,0:T(8,128)(2,1)}) custom-call(s32[29]{0:T(128)} %concatenate.9.at_ref, bf16[768,384]{1,0:T(8,128)(2,1)} %get-tuple-element.30.dq_ref, f32[768,384]{1,0:T(8,128)} %get-tuple-element.31.out_ref, bf16[768,768]{1,0:T(8,128)(2,1)} %w_ref.1), custom_call_target="tpu_custom_call" | custom-call | tf_op jit(solution)/shard_map/pallas_call | solution.py:380
  87.5 1.8 %collective-permute-start.6 = (bf16[384,768]{1,0:T(8,128)(2,1)}, bf16[384,768]{1,0:T(8,128)(2,1)S(1)}, u32[]{:S(2)}, u32[]{:S(2)}) collective-permute-start(bf16[384,768]{1,0:T(8,128)(2,1)} %get-tuple-element.33), channel_id=1, source_target_pairs={{0,1},{1,0},{2,3},{3,2},{4,5},{5,4},{6,7},{7,6},{8,9},{9,8},{10,11... | collective-permute-start | bytes 1769480 | tf_op jit(solution)/shard_map/ppermute | solution.py:485
  89.3 1.8 %collective-permute-done.6.right_ref = bf16[384,768]{1,0:T(8,128)(2,1)S(1)} collective-permute-done((bf16[384,768]{1,0:T(8,128)(2,1)}, bf16[384,768]{1,0:T(8,128)(2,1)S(1)}, u32[]{:S(2)}, u32[]{:S(2)}) %collective-permute-start.6) | collective-permute-done | bytes 589856 | tf_op jit(solution)/shard_map/ppermute | solution.py:485
  91.9 2.1 %shard_map.117 = (bf16[96,768]{1,0:T(8,128)(2,1)}, bf16[96,768]{1,0:T(8,128)(2,1)}, bf16[96,768]{1,0:T(8,128)(2,1)}, bf16[96,768]{1,0:T(8,128)(2,1)}) custom-call(bf16[384,768]{1,0:T(8,128)(2,1)} %get-tuple-element.32.left_ref, bf16[384,768]{1,0:T(8,128)(2,1)} %copy-done.2), custom_call_target="tpu_custom_call" | custom-call | tf_op jit(solution)/shard_map/pallas_call | solution.py:399
  94.1 2.7 %collective-permute-start.8 = (bf16[96,768]{1,0:T(8,128)(2,1)}, bf16[96,768]{1,0:T(8,128)(2,1)S(1)}, u32[]{:S(2)}, u32[]{:S(2)}) collective-permute-start(bf16[96,768]{1,0:T(8,128)(2,1)} %get-tuple-element.36), channel_id=1, source_target_pairs={{0,6},{1,7},{2,0},{3,1},{4,2},{5,3},{6,4},{7,5},{8,14},{9,15},{10,... | collective-permute-start | bytes 442376 | tf_op jit(solution)/shard_map/ppermute | solution.py:487
  97.0 3.5 %all-to-all-done.1 = bf16[16,48,768]{2,1,0:T(8,128)(2,1)S(1)} async-done(((bf16[16,48,768]{2,1,0:T(8,128)(2,1)}), bf16[16,48,768]{2,1,0:T(8,128)(2,1)S(1)}, u32[]{:S(2)}, u32[]{:S(2)}) %all-to-all-start.1) | async-done | bytes 1179680 | tf_op jit(solution)/shard_map/all_to_all | solution.py:483
  100.6 2.8 %collective-permute-start.5 = (bf16[48,768]{1,0:T(8,128)(2,1)S(1)}, bf16[48,768]{1,0:T(8,128)(2,1)S(1)}, u32[]{:S(2)}, u32[]{:S(2)}) collective-permute-start(bf16[48,768]{1,0:T(8,128)(2,1)S(1)} %reduce_sum.12), channel_id=1, source_target_pairs={{0,4},{1,29},{2,32},{3,57},{4,68},{5,93},{6,96},{7,121},{8,12},{9,... | collective-permute-start | bytes 221192 | tf_op jit(solution)/shard_map/ppermute | solution.py:490
  104.2 3.3 %shard_map.118.ends_ref = bf16[96,768]{1,0:T(8,128)(2,1)} custom-call(bf16[96,768]{1,0:T(8,128)(2,1)} %get-tuple-element.34.refs_0_, bf16[96,768]{1,0:T(8,128)(2,1)} %copy-done.4, bf16[96,768]{1,0:T(8,128)(2,1)} %copy-done.5, bf16[96,768]{1,0:T(8,128)(2,1)} %copy-done.6, f32[48,768]{1,0:T(8,128)} %get-tuple-element.38.refs_4_, ...), custom_call_target="tpu_custom_call" | custom-call | tf_op jit(solution)/shard_map/pallas_call | solution.py:358
  108.9 1.6 %shard_map.119.refs_0_ = bf16[96,768]{1,0:T(8,128)(2,1)} custom-call(bf16[48,768]{1,0:T(8,128)(2,1)} %copy-done.15, bf16[96,768]{1,0:T(8,128)(2,1)} %shard_map.118.ends_ref), custom_call_target="tpu_custom_call" | custom-call | tf_op jit(solution)/shard_map/pallas_call | solution.py:415
  110.6 5.3 %collective-permute-start.12 = (bf16[96,768]{1,0:T(8,128)(2,1)}, bf16[96,768]{1,0:T(8,128)(2,1)S(1)}, u32[]{:S(2)}, u32[]{:S(2)}) collective-permute-start(bf16[96,768]{1,0:T(8,128)(2,1)} %shard_map.119.refs_0_), channel_id=1, source_target_pairs={{0,6},{1,7},{2,0},{3,1},{4,2},{5,3},{6,4},{7,5},{8,14},{9,15},{10,... | collective-permute-start | bytes 442376 | tf_op jit(solution)/shard_map/ppermute | solution.py:492
  116.5 2.0 %collective-permute-start.13 = (bf16[96,768]{1,0:T(8,128)(2,1)}, bf16[96,768]{1,0:T(8,128)(2,1)S(1)}, u32[]{:S(2)}, u32[]{:S(2)}) collective-permute-start(bf16[96,768]{1,0:T(8,128)(2,1)} %shard_map.119.refs_0_), channel_id=1, source_target_pairs={{0,1},{1,0},{2,3},{3,2},{4,5},{5,4},{6,7},{7,6},{8,9},{9,8},{10,11... | collective-permute-start | bytes 442376 | tf_op jit(solution)/shard_map/ppermute | solution.py:493
  118.5 4.1 %collective-permute-done.12.refs_3_ = bf16[96,768]{1,0:T(8,128)(2,1)S(1)} collective-permute-done((bf16[96,768]{1,0:T(8,128)(2,1)}, bf16[96,768]{1,0:T(8,128)(2,1)S(1)}, u32[]{:S(2)}, u32[]{:S(2)}) %collective-permute-start.12) | collective-permute-done | bytes 147488 | tf_op jit(solution)/shard_map/ppermute | solution.py:492
  123.4 2.1 %collective-permute-start.15 = (bf16[96,768]{1,0:T(8,128)(2,1)S(1)}, bf16[96,768]{1,0:T(8,128)(2,1)S(1)}, u32[]{:S(2)}, u32[]{:S(2)}) collective-permute-start(bf16[96,768]{1,0:T(8,128)(2,1)S(1)} %collective-permute-done.11.refs_2_), channel_id=1, source_target_pairs={{0,1},{1,0},{2,3},{3,2},{4,5},{5,4},{6,7},{7,6},{8,9},{9,8},{10,11... | collective-permute-start | bytes 442376 | tf_op jit(solution)/shard_map/ppermute | solution.py:493
  125.7 1.1 collective-permute-start.14
  128.4 2.4 %shard_map.120 = (bf16[384,768]{1,0:T(8,128)(2,1)}, bf16[384,768]{1,0:T(8,128)(2,1)}) custom-call(s32[29]{0:T(128)} %concatenate.9.at_ref, bf16[96,768]{1,0:T(8,128)(2,1)} %shard_map.119.refs_0_, bf16[96,768]{1,0:T(8,128)(2,1)} %copy-done.9, bf16[96,768]{1,0:T(8,128)(2,1)} %copy-done.8, bf16[96,768]{1,0:T(8,128)(2,1)} %copy-done.7, ...), custom_call_target="tpu_custom_call" | custom-call | tf_op jit(solution)/shard_map/pallas_call | solution.py:436
  (70 shorter events, 15.4 us)
Async XLA Ops:
  1.5 8.4 %copy-start.3 = (bf16[48,768]{1,0:T(8,128)(2,1)}, bf16[48,768]{1,0:T(8,128)(2,1)S(1)}, u32[]{:S(2)}) copy-start(bf16[48,768]{1,0:T(8,128)(2,1)S(1)} %constant_dynamic-slice_fusion.1.own_ref) | copy-start | bytes 221188
  1.5 8.4 %collective-permute-start = (bf16[48,768]{1,0:T(8,128)(2,1)S(1)}, bf16[48,768]{1,0:T(8,128)(2,1)S(1)}, u32[]{:S(2)}, u32[]{:S(2)}) collective-permute-start(bf16[48,768]{1,0:T(8,128)(2,1)S(1)} %constant_dynamic-slice_fusion.1.own_ref), channel_id=1, source_target_pairs={{4,0},{29,1},{32,2},{57,3},{68,4},{93,5},{96,6},{121,7},{12,8},{21... | collective-permute-start | bytes 221192 | tf_op jit(solution)/shard_map/ppermute | solution.py:462
  11.0 6.7 %copy-start = (bf16[768,768]{1,0:T(8,128)(2,1)S(1)}, bf16[768,768]{1,0:T(8,128)(2,1)}, u32[]{:S(2)}) copy-start(bf16[768,768]{1,0:T(8,128)(2,1)} %param.13) | copy-start | bytes 3538948
  11.0 22.5 %all-to-all-start = ((bf16[16,48,768]{2,1,0:T(8,128)(2,1)}), bf16[16,48,768]{2,1,0:T(8,128)(2,1)}, u32[]{:S(2)}, u32[]{:S(2)}) async-start(bf16[16,48,768]{2,1,0:T(8,128)(2,1)} %broadcast_in_dim.56), calls=%async_computation | async-start | bytes 2359296 | tf_op jit(solution)/shard_map/all_to_all | solution.py:463
  17.7 1.3 copy-start.1
  48.6 5.3 %collective-permute-start.1 = (f32[48,384]{1,0:T(8,128)}, f32[48,384]{1,0:T(8,128)S(1)}, u32[]{:S(2)}, u32[]{:S(2)}) collective-permute-start(f32[48,384]{1,0:T(8,128)} %get-tuple-element.25.left_ref.refs_0_), channel_id=1, source_target_pairs={{0,1},{1,0},{2,3},{3,2},{4,5},{5,4},{6,7},{7,6},{8,9},{9,8},{10,11... | collective-permute-start | bytes 221192 | tf_op jit(solution)/shard_map/ppermute | solution.py:479
  56.1 4.9 %collective-permute-start.4 = (f32[48,384]{1,0:T(8,128)}, f32[48,384]{1,0:T(8,128)S(1)}, u32[]{:S(2)}, u32[]{:S(2)}) collective-permute-start(f32[48,384]{1,0:T(8,128)} %shard_map.114.refs_1_), channel_id=1, source_target_pairs={{0,4},{1,5},{2,6},{3,7},{4,0},{5,1},{6,2},{7,3},{8,12},{9,13},{10,... | collective-permute-start | bytes 221192 | tf_op jit(solution)/shard_map/ppermute | solution.py:480
  58.0 5.1 %collective-permute-start.3 = (f32[48,384]{1,0:T(8,128)}, f32[48,384]{1,0:T(8,128)S(1)}, u32[]{:S(2)}, u32[]{:S(2)}) collective-permute-start(f32[48,384]{1,0:T(8,128)} %shard_map.114.refs_1_), channel_id=1, source_target_pairs={{0,6},{1,7},{2,0},{3,1},{4,2},{5,3},{6,4},{7,5},{8,14},{9,15},{10,... | collective-permute-start | bytes 221192 | tf_op jit(solution)/shard_map/ppermute | solution.py:480
  59.0 4.6 %collective-permute-start.2 = (f32[48,384]{1,0:T(8,128)}, f32[48,384]{1,0:T(8,128)S(1)}, u32[]{:S(2)}, u32[]{:S(2)}) collective-permute-start(f32[48,384]{1,0:T(8,128)} %shard_map.114.refs_1_), channel_id=1, source_target_pairs={{0,2},{1,3},{2,4},{3,5},{4,6},{5,7},{6,0},{7,1},{8,10},{9,11},{10,... | collective-permute-start | bytes 221192 | tf_op jit(solution)/shard_map/ppermute | solution.py:480
  61.0 2.6 %copy-start.16 = (f32[48,384]{1,0:T(8,128)}, f32[48,384]{1,0:T(8,128)S(1)}, u32[]{:S(2)}) copy-start(f32[48,384]{1,0:T(8,128)S(1)} %collective-permute-done.4.refs_4_) | copy-start | bytes 221188
  80.2 20.2 %all-to-all-start.1 = ((bf16[16,48,768]{2,1,0:T(8,128)(2,1)}), bf16[16,48,768]{2,1,0:T(8,128)(2,1)S(1)}, u32[]{:S(2)}, u32[]{:S(2)}) async-start(bf16[16,48,768]{2,1,0:T(8,128)(2,1)} %get-tuple-element.29), calls=%async_computation.1 | async-start | bytes 2359296 | tf_op jit(solution)/shard_map/all_to_all | solution.py:483
  87.5 3.6 %collective-permute-start.6 = (bf16[384,768]{1,0:T(8,128)(2,1)}, bf16[384,768]{1,0:T(8,128)(2,1)S(1)}, u32[]{:S(2)}, u32[]{:S(2)}) collective-permute-start(bf16[384,768]{1,0:T(8,128)(2,1)} %get-tuple-element.33), channel_id=1, source_target_pairs={{0,1},{1,0},{2,3},{3,2},{4,5},{5,4},{6,7},{7,6},{8,9},{9,8},{10,11... | collective-permute-start | bytes 1769480 | tf_op jit(solution)/shard_map/ppermute | solution.py:485
  91.1 0.8 copy-start.2
  94.0 9.4 %collective-permute-start.7 = (bf16[96,768]{1,0:T(8,128)(2,1)}, bf16[96,768]{1,0:T(8,128)(2,1)S(1)}, u32[]{:S(2)}, u32[]{:S(2)}) collective-permute-start(bf16[96,768]{1,0:T(8,128)(2,1)} %get-tuple-element.35), channel_id=1, source_target_pairs={{0,2},{1,3},{2,4},{3,5},{4,6},{5,7},{6,0},{7,1},{8,10},{9,11},{10,... | collective-permute-start | bytes 442376 | tf_op jit(solution)/shard_map/ppermute | solution.py:487
  94.1 9.4 %collective-permute-start.8 = (bf16[96,768]{1,0:T(8,128)(2,1)}, bf16[96,768]{1,0:T(8,128)(2,1)S(1)}, u32[]{:S(2)}, u32[]{:S(2)}) collective-permute-start(bf16[96,768]{1,0:T(8,128)(2,1)} %get-tuple-element.36), channel_id=1, source_target_pairs={{0,6},{1,7},{2,0},{3,1},{4,2},{5,3},{6,4},{7,5},{8,14},{9,15},{10,... | collective-permute-start | bytes 442376 | tf_op jit(solution)/shard_map/ppermute | solution.py:487
  96.7 6.7 %collective-permute-start.9 = (bf16[96,768]{1,0:T(8,128)(2,1)}, bf16[96,768]{1,0:T(8,128)(2,1)S(1)}, u32[]{:S(2)}, u32[]{:S(2)}) collective-permute-start(bf16[96,768]{1,0:T(8,128)(2,1)} %get-tuple-element.37), channel_id=1, source_target_pairs={{0,4},{1,5},{2,6},{3,7},{4,0},{5,1},{6,2},{7,3},{8,12},{9,13},{10,... | collective-permute-start | bytes 442376 | tf_op jit(solution)/shard_map/ppermute | solution.py:487
  100.6 7.7 %collective-permute-start.5 = (bf16[48,768]{1,0:T(8,128)(2,1)S(1)}, bf16[48,768]{1,0:T(8,128)(2,1)S(1)}, u32[]{:S(2)}, u32[]{:S(2)}) collective-permute-start(bf16[48,768]{1,0:T(8,128)(2,1)S(1)} %reduce_sum.12), channel_id=1, source_target_pairs={{0,4},{1,29},{2,32},{3,57},{4,68},{5,93},{6,96},{7,121},{8,12},{9,... | collective-permute-start | bytes 221192 | tf_op jit(solution)/shard_map/ppermute | solution.py:490
  103.4 0.7 copy-start.5
  103.5 0.7 copy-start.6
  110.6 12.0 %collective-permute-start.12 = (bf16[96,768]{1,0:T(8,128)(2,1)}, bf16[96,768]{1,0:T(8,128)(2,1)S(1)}, u32[]{:S(2)}, u32[]{:S(2)}) collective-permute-start(bf16[96,768]{1,0:T(8,128)(2,1)} %shard_map.119.refs_0_), channel_id=1, source_target_pairs={{0,6},{1,7},{2,0},{3,1},{4,2},{5,3},{6,4},{7,5},{8,14},{9,15},{10,... | collective-permute-start | bytes 442376 | tf_op jit(solution)/shard_map/ppermute | solution.py:492
  115.9 7.5 %collective-permute-start.11 = (bf16[96,768]{1,0:T(8,128)(2,1)}, bf16[96,768]{1,0:T(8,128)(2,1)S(1)}, u32[]{:S(2)}, u32[]{:S(2)}) collective-permute-start(bf16[96,768]{1,0:T(8,128)(2,1)} %shard_map.119.refs_0_), channel_id=1, source_target_pairs={{0,4},{1,5},{2,6},{3,7},{4,0},{5,1},{6,2},{7,3},{8,12},{9,13},{10,... | collective-permute-start | bytes 442376 | tf_op jit(solution)/shard_map/ppermute | solution.py:492
  115.9 9.8 %collective-permute-start.10 = (bf16[96,768]{1,0:T(8,128)(2,1)}, bf16[96,768]{1,0:T(8,128)(2,1)S(1)}, u32[]{:S(2)}, u32[]{:S(2)}) collective-permute-start(bf16[96,768]{1,0:T(8,128)(2,1)} %shard_map.119.refs_0_), channel_id=1, source_target_pairs={{0,2},{1,3},{2,4},{3,5},{4,6},{5,7},{6,0},{7,1},{8,10},{9,11},{10,... | collective-permute-start | bytes 442376 | tf_op jit(solution)/shard_map/ppermute | solution.py:492
  116.5 10.3 %collective-permute-start.13 = (bf16[96,768]{1,0:T(8,128)(2,1)}, bf16[96,768]{1,0:T(8,128)(2,1)S(1)}, u32[]{:S(2)}, u32[]{:S(2)}) collective-permute-start(bf16[96,768]{1,0:T(8,128)(2,1)} %shard_map.119.refs_0_), channel_id=1, source_target_pairs={{0,1},{1,0},{2,3},{3,2},{4,5},{5,4},{6,7},{7,6},{8,9},{9,8},{10,11... | collective-permute-start | bytes 442376 | tf_op jit(solution)/shard_map/ppermute | solution.py:493
  122.6 5.2 %copy-start.7 = (bf16[96,768]{1,0:T(8,128)(2,1)}, bf16[96,768]{1,0:T(8,128)(2,1)S(1)}, u32[]{:S(2)}) copy-start(bf16[96,768]{1,0:T(8,128)(2,1)S(1)} %collective-permute-done.12.refs_3_) | copy-start | bytes 442372
  122.6 4.2 %collective-permute-start.16 = (bf16[96,768]{1,0:T(8,128)(2,1)S(1)}, bf16[96,768]{1,0:T(8,128)(2,1)S(1)}, u32[]{:S(2)}, u32[]{:S(2)}) collective-permute-start(bf16[96,768]{1,0:T(8,128)(2,1)S(1)} %collective-permute-done.12.refs_3_), channel_id=1, source_target_pairs={{0,1},{1,0},{2,3},{3,2},{4,5},{5,4},{6,7},{7,6},{8,9},{9,8},{10,11... | collective-permute-start | bytes 442376 | tf_op jit(solution)/shard_map/ppermute | solution.py:493
  123.4 4.3 %copy-start.8 = (bf16[96,768]{1,0:T(8,128)(2,1)}, bf16[96,768]{1,0:T(8,128)(2,1)S(1)}, u32[]{:S(2)}) copy-start(bf16[96,768]{1,0:T(8,128)(2,1)S(1)} %collective-permute-done.11.refs_2_) | copy-start | bytes 442372
  123.4 3.3 %collective-permute-start.15 = (bf16[96,768]{1,0:T(8,128)(2,1)S(1)}, bf16[96,768]{1,0:T(8,128)(2,1)S(1)}, u32[]{:S(2)}, u32[]{:S(2)}) collective-permute-start(bf16[96,768]{1,0:T(8,128)(2,1)S(1)} %collective-permute-done.11.refs_2_), channel_id=1, source_target_pairs={{0,1},{1,0},{2,3},{3,2},{4,5},{5,4},{6,7},{7,6},{8,9},{9,8},{10,11... | collective-permute-start | bytes 442376 | tf_op jit(solution)/shard_map/ppermute | solution.py:493
  125.7 2.1 %copy-start.9 = (bf16[96,768]{1,0:T(8,128)(2,1)}, bf16[96,768]{1,0:T(8,128)(2,1)S(1)}, u32[]{:S(2)}) copy-start(bf16[96,768]{1,0:T(8,128)(2,1)S(1)} %collective-permute-done.10.refs_1_) | copy-start | bytes 442372
  125.7 2.1 %collective-permute-start.14 = (bf16[96,768]{1,0:T(8,128)(2,1)S(1)}, bf16[96,768]{1,0:T(8,128)(2,1)S(1)}, u32[]{:S(2)}, u32[]{:S(2)}) collective-permute-start(bf16[96,768]{1,0:T(8,128)(2,1)S(1)} %collective-permute-done.10.refs_1_), channel_id=1, source_target_pairs={{0,1},{1,0},{2,3},{3,2},{4,5},{5,4},{6,7},{7,6},{8,9},{9,8},{10,11... | collective-permute-start | bytes 442376 | tf_op jit(solution)/shard_map/ppermute | solution.py:493
  126.7 1.0 copy-start.10
  126.7 1.0 copy-start.11
  126.8 1.0 copy-start.12
  (6 other events, 3.8 us)

commit v4 on v3

--- a/solution.py
+++ b/solution.py
@@ -15,7 +15,6 @@
 LOG2E = math.log2(math.e)
 LN2 = math.log(2.0)
 ROWS, COLS, SIDE = 16, 8, 4
-VMEM = 56 * 1024 * 1024
 F32, BF16 = jnp.float32, jnp.bfloat16
 
 
@@ -58,8 +57,8 @@
     return pairs
 
 
-def params(**more):
-    return pltpu.CompilerParams(vmem_limit_bytes=VMEM, **more)
+def params(limit=12):
+    return pltpu.CompilerParams(vmem_limit_bytes=limit * 1024 * 1024)
 
 
 def whole(count):
@@ -67,7 +66,7 @@
 
 
 SCALAR = pl.BlockSpec(memory_space=pltpu.SMEM)
-HBM = pl.BlockSpec(memory_space=pl.ANY)
+HBM = pl.BlockSpec(memory_space=pltpu.HBM)
 
 
 def array(shape, dtype):
@@ -94,22 +93,21 @@
 
 
 def forward_kernel(first, at_ref, *refs):
-    tokens_hbm, bias_hbm, q_hbm, w_hbm, mask_hbm, row_hbm, dh_hbm, expo_hbm, kv_hbm, num_hbm, stats_ref = refs[:11]
-    tokens, w_ref, q_ref, mask_ref, row_ref, dh_ref, bias_ref, kv_ref, expo_ref, num_ref, tops, score_ref, sems = refs[-13:]
+    tokens_hbm, bias_hbm, q_hbm, wk_hbm, wv_hbm, mask_hbm, row_hbm, dh_hbm, expo_ref, kv_ref, num_ref, stats_ref = refs[:12]
+    tokens, w_ref, q_ref, mask_ref, row_ref, dh_ref, bias_ref, tops, score_ref, sems = refs[12:]
     start = copier(sems)
-    rows, width = q_ref.shape[1], w_ref.shape[1]
-    early = [start(w_hbm, w_ref)]
+    width, rows = q_ref.shape
+    early = [start(wk_hbm, w_ref.at[0]), start(wv_hbm, w_ref.at[1])]
     for n in range(ROWS):
         early.append(start(tokens_hbm.at[n], tokens.at[rows_at(at_ref[first + n], tokens_hbm.shape[1])]))
     late = [start(a, b) for a, b in ((q_hbm, q_ref), (mask_hbm, mask_ref), (row_hbm, row_ref), (dh_hbm, dh_ref))]
     bias_in = [start(bias_hbm.at[h], bias_ref.at[h]) for h in range(HEADS)]
     for copy in early:
         copy.wait()
-    out = []
     for part in range(4):
         span = slice(part * width // 2, (part + 1) * width // 2)
-        kv_ref[span, :] = nt(w_ref[span, :], tokens[...]).astype(BF16)
-        out.append(start(kv_ref.at[span], kv_hbm.at[span]))
+        columns = slice(part % 2 * width // 2, (part % 2 + 1) * width // 2)
+        kv_ref[span, :] = dot(w_ref[part // 2, :, columns], tokens[...], ((0,), (1,))).astype(BF16)
     tops[...] = jnp.zeros_like(tops)
     for copy in late:
         copy.wait()
@@ -151,48 +149,39 @@
         if h:
             weigh(h - 1)
         soften(h)
-        if h % GROUP == GROUP - 1:
-            group = pl.ds(h + 1 - GROUP, GROUP)
-            out.append(start(expo_ref.at[group], expo_hbm.at[group]))
     weigh(HEADS - 1)
-    out.append(start(num_ref, num_hbm))
 
     stats_ref[HEADS : 2 * HEADS, :] = tops[...].T[:HEADS, :]
-    for copy in out:
-        copy.wait()
-
-
-def forward(at, first, tokens, bias, q, w, mask, row, dh):
+
+
+def forward(at, first, tokens, bias, q, wk, wv, mask, row, dh):
     rows, span = bias.shape[1:]
-    width = w.shape[1]
+    width = wk.shape[0]
     return pl.pallas_call(
         functools.partial(forward_kernel, first),
         out_shape=(
-            array(bias.shape, BF16),
-            array((2 * width, span), BF16),
-            array((width, rows), F32),
+            pltpu.VMEM(bias.shape, BF16),
+            pltpu.VMEM((2 * width, span), BF16),
+            pltpu.VMEM((width, rows), F32),
             array((3 * HEADS, rows), F32),
         ),
-        in_specs=[SCALAR] + [HBM] * 7,
-        out_specs=(HBM, HBM, HBM, *whole(1)),
+        in_specs=[SCALAR] + [HBM] * 8,
+        out_specs=tuple(whole(4)),
         scratch_shapes=[
             pltpu.VMEM((span, width), BF16),
-            pltpu.VMEM(w.shape, BF16),
+            pltpu.VMEM((2, *wk.shape), BF16),
             pltpu.VMEM(q.shape, BF16),
             pltpu.VMEM(mask.shape, BF16),
             pltpu.VMEM(row.shape, F32),
             pltpu.VMEM(dh.shape, BF16),
             pltpu.VMEM(bias.shape, BF16),
-            pltpu.VMEM((2 * width, span), BF16),
-            pltpu.VMEM(bias.shape, BF16),
-            pltpu.VMEM((width, rows), F32),
             pltpu.VMEM((rows, 128), F32),
             pltpu.VMEM((2, rows, span), F32),
             pltpu.SemaphoreType.DMA((64,)),
         ],
-        compiler_params=params(),
+        compiler_params=params(42),
         cost_estimate=pl.CostEstimate(flops=4 * HEADS * rows * span * 256, bytes_accessed=4 * HEADS * rows * span, transcendentals=HEADS * rows * span),
-    )(at, tokens, bias, q, w, mask, row, dh)
+    )(at, tokens, bias, q, wk, wv, mask, row, dh)
 
 
 def merge(stats):
@@ -222,13 +211,12 @@
 
 def backward_kernel(first, at_ref, *refs):
     stats, refs = refs[: SIDE + 1], refs[SIDE + 1 :]
-    num_hbm, dh_hbm, expo_hbm, q_hbm, kv_hbm, w_hbm, dbias_hbm, dq_hbm, sent_hbm, out_hbm = refs[:10]
-    num_ref, dh_ref, out_ref, expo_ref, dhf_ref, q_ref, kv_ref, w_ref, dbias_ref, dq_ref, dkv, prod_ref, sums, sems = refs[10:]
+    num_ref, dh_hbm, expo_ref, q_hbm, kv_ref, wk_hbm, wv_hbm, dbias_hbm, dq_hbm, sent_hbm, out_hbm = refs[:11]
+    dh_ref, out_ref, dhf_ref, q_ref, w_ref, dbias_ref, dq_ref, dkv, prod_ref, sums, sems = refs[11:]
     start = copier(sems)
     width = q_ref.shape[0]
-    early = [start(a, b) for a, b in ((dh_hbm, dh_ref), (num_hbm, num_ref), (kv_hbm, kv_ref), (q_hbm, q_ref))]
-    expo_in = [start(expo_hbm.at[h], expo_ref.at[h]) for h in range(HEADS)]
-    late = start(w_hbm, w_ref)
+    early = [start(a, b) for a, b in ((dh_hbm, dh_ref), (q_hbm, q_ref))]
+    late = [start(wk_hbm, w_ref.at[0]), start(wv_hbm, w_ref.at[1])]
     total, top, inner = merge([s[...] for s in stats[1:]])
     factor = jnp.exp2(stats[0][HEADS : 2 * HEADS, :] - top) / total
     shift = -factor * (inner / total)
@@ -270,9 +258,6 @@
     combine(0)
     products(0)
     for h in range(HEADS):
-        if h % GROUP == 0:
-            for n in range(h, h + GROUP):
-                expo_in[n].wait()
         if h + 1 < HEADS:
             combine(h + 1)
             products(h + 1)
@@ -286,8 +271,10 @@
     to_queries_and_keys(HEADS - 1)
     out.append(start(dq_ref, dq_hbm))
     out.append(start(out_ref, out_hbm))
-    late.wait()
-    sums[...] = tn(dkv[...], w_ref[...]).astype(BF16)
+    for copy in late:
+        copy.wait()
+    to_tokens = dot(dkv[:width, :], w_ref[0], ((0,), (1,))) + dot(dkv[width:, :], w_ref[1], ((0,), (1,)))
+    sums[...] = to_tokens.astype(BF16)
     size = sums.shape[0] // ROWS
     for n in range(ROWS):
         out.append(start(sums.at[rows_at(at_ref[first + n], size)], sent_hbm.at[n]))
@@ -295,23 +282,20 @@
         copy.wait()
 
 
-def backward(at, first, own, every, num, dh, expo, q, kv, w):
+def backward(at, first, own, every, num, dh, expo, q, kv, wk, wv):
     rows, span = expo.shape[1:]
     width = q.shape[0]
     return pl.pallas_call(
         functools.partial(backward_kernel, first),
         out_shape=[array(expo.shape, BF16), array(q.shape, BF16), array((ROWS, span // ROWS, width), BF16), array(num.shape, F32)],
-        in_specs=[SCALAR] + whole(SIDE + 1) + [HBM] * 6,
+        in_specs=[SCALAR] + whole(SIDE + 2) + [HBM] + whole(1) + [HBM] + whole(1) + [HBM] * 2,
         out_specs=[HBM] * 4,
         scratch_shapes=[
-            pltpu.VMEM(num.shape, F32),
             pltpu.VMEM(dh.shape, BF16),
             pltpu.VMEM(num.shape, F32),
-            pltpu.VMEM(expo.shape, BF16),
             pltpu.VMEM((HEADS * SLOT, rows), BF16),
             pltpu.VMEM(q.shape, BF16),
-            pltpu.VMEM(kv.shape, BF16),
-            pltpu.VMEM(w.shape, BF16),
+            pltpu.VMEM((2, *wk.shape), BF16),
             pltpu.VMEM(expo.shape, BF16),
             pltpu.VMEM(q.shape, BF16),
             pltpu.VMEM((2 * width, span), BF16),
@@ -319,9 +303,9 @@
             pltpu.VMEM((span, width), BF16),
             pltpu.SemaphoreType.DMA((64,)),
         ],
-        compiler_params=params(),
+        compiler_params=params(42),
         cost_estimate=pl.CostEstimate(flops=8 * HEADS * rows * span * 256, bytes_accessed=4 * HEADS * rows * span, transcendentals=0),
-    )(at, own, *every, num, dh, expo, q, kv, w)
+    )(at, own, *every, num, dh, expo, q, kv, wk, wv)
 
 
 def prepare_kernel(single_ref, cot_ref, own_ref, own_cot_ref, wq_ref, wg_ref, wo_ref, q_ref, dh_ref, gate_ref, dhid_ref):
@@ -345,21 +329,21 @@
 
 
 def finish_kernel(*refs):
-    parts, (gate_ref, dhid_ref, wo_ref, wg_ref, out_ref) = refs[:SIDE], refs[SIDE:]
+    parts, (gate_ref, dhid_ref, wo_ref, wg_ref, att_ref, rest_ref) = refs[:SIDE], refs[SIDE:]
     size = gate_ref.shape[0]
     both = functools.reduce(jnp.add, [p[...].astype(F32) for p in parts])
     d_query, out, gate = both[:size], both[size:], gate_ref[...]
-    out_ref[:size, :] = nn((out * gate).astype(BF16), wo_ref[...]).astype(BF16)
+    att_ref[...] = nn((out * gate).astype(BF16), wo_ref[...]).astype(BF16)
     d_gate = (dhid_ref[...] * out * gate * (1.0 - gate)).astype(BF16)
-    out_ref[size:, :] = (d_query + nt(d_gate, wg_ref[...])).astype(BF16)
+    rest_ref[...] = d_query + nt(d_gate, wg_ref[...])
 
 
 def finish(parts, gate, d_hidden, wo, wg):
     return pl.pallas_call(
         finish_kernel,
-        out_shape=array(parts[0].shape, BF16),
+        out_shape=[array(gate.shape, BF16), array(gate.shape, F32)],
         in_specs=whole(SIDE + 4),
-        out_specs=whole(1)[0],
+        out_specs=whole(2),
         compiler_params=params(),
     )(*parts, gate, d_hidden, wo, wg)
 
@@ -405,39 +389,38 @@
     )(*terms)
 
 
-def total_kernel(kv_ref, ends_ref, out_ref):
-    size = kv_ref.shape[0]
-    out_ref[:size, :] = ends_ref[:size, :]
-    out_ref[size:, :] = (ends_ref[size:, :].astype(F32) + kv_ref[...].astype(F32)).astype(BF16)
-
-
-def total(from_kv, ends):
+def total_kernel(kv_ref, rest_ref, out_ref):
+    out_ref[...] = (kv_ref[...].astype(F32) + rest_ref[...]).astype(BF16)
+
+
+def total(from_kv, rest):
     return pl.pallas_call(
         total_kernel,
-        out_shape=array(ends.shape, BF16),
+        out_shape=array(from_kv.shape, BF16),
         in_specs=whole(2),
         out_specs=whole(1)[0],
         compiler_params=params(),
-    )(from_kv, ends)
+    )(from_kv, rest)
 
 
 def join_kernel(first, at_ref, *refs):
-    ends, outs = refs[: 2 * SIDE], refs[2 * SIDE :]
-    size = ends[0].shape[0] // 2
+    ends, out = refs[:-1], refs[-1]
+    size = ends[0].shape[0]
     core = at_ref[first + SIDE]
     for k, end in enumerate(ends):
         shift = core if k < SIDE else size - core
-        for n, out in enumerate(outs):
-            out[rows_at(at_ref[first + k % SIDE] + shift, size), :] = end[n * size : (n + 1) * size, :]
-
-
-def join(at, first, near, far):
-    size, width = near[0].shape
+        out[rows_at(at_ref[first + k % SIDE] + shift, size), :] = end[...]
+
+
+def gather_col(at, first, end):
+    near = [end] + [lax.ppermute(end, "col", along_z(k)) for k in (1, 2, 3)]
+    far = [lax.ppermute(end, "col", other_core()) for end in near]
+    size, width = end.shape
     return pl.pallas_call(
         functools.partial(join_kernel, first),
-        out_shape=[array((size // 2 * COLS, width), BF16)] * 2,
+        out_shape=array((size * COLS, width), BF16),
         in_specs=[SCALAR] + whole(COLS),
-        out_specs=whole(2),
+        out_specs=whole(1)[0],
         compiler_params=params(),
     )(at, *near, *far)
 
@@ -461,7 +444,6 @@
     own = [lax.dynamic_slice_in_dim(a, col_index * piece, piece, 0) for a in (single, cotangent)]
     tokens = lax.ppermute(own[0], both, home_to_block())
     tokens = lax.all_to_all(jnp.broadcast_to(tokens[None], (ROWS, *tokens.shape)), "row", 0, 0)
-    wkv = jnp.concatenate([w_key, w_value], axis=1).T
     q, dh, gate, d_hidden = prepare(single, cotangent, own, w_query, w_gate, w_out)
     alive = key_live[None, :] > 0
     row = jnp.broadcast_to(jnp.where(alive, LOG2E, 0.0).astype(F32), (8, span))
@@ -475,23 +457,22 @@
     dead = jnp.where(alive, 0.0, fill).astype(BF16)
 
     mask = jnp.concatenate([live, dead], axis=0)
-    expo, kv, num, stats = forward(at, 13, tokens, pair_bias, q, wkv, mask, row, dh)
+    expo, kv, num, stats = forward(at, 13, tokens, pair_bias, q, w_key, w_value, mask, row, dh)
+    expo, kv, num = (pltpu.with_memory_space_constraint(a, pltpu.VMEM) for a in (expo, kv, num))
     chip = merge_pair(stats, lax.ppermute(stats, "col", other_core()))
     every = [chip] + [lax.ppermute(chip, "col", along_z(k)) for k in (1, 3, 2)]
-    d_bias, dq, from_kv, out = backward(at, 13, stats, every, num, dh, expo, q, kv, wkv)
+    d_bias, dq, from_kv, out = backward(at, 13, stats, every, num, dh, expo, q, kv, w_key, w_value)
 
     from_kv = lax.all_to_all(from_kv, "row", 0, 0)
     mine, other = query(at, 0, dq, out, w_query)
     other = lax.ppermute(other, "col", other_core())
     parts = add_split([mine, other])
     parts = [parts[0]] + [lax.ppermute(parts[k], "col", along_z(k)) for k in (1, 3, 2)]
-    ends = finish(parts, gate, d_hidden, w_out, w_gate)
+    attended, rest = finish(parts, gate, d_hidden, w_out, w_gate)
+    attended = gather_col(at, 8, attended)
     from_kv = jnp.sum(from_kv.astype(F32), axis=0).astype(BF16)
     from_kv = lax.ppermute(from_kv, both, [(b, a) for a, b in home_to_block()])
-    ends = total(from_kv, ends)
-    near = [ends] + [lax.ppermute(ends, "col", along_z(k)) for k in (1, 2, 3)]
-    far = [lax.ppermute(end, "col", other_core()) for end in near]
-    attended, d_single = join(at, 8, near, far)
+    d_single = gather_col(at, 8, total(from_kv, rest))
     return (attended, d_bias, d_single)
 
 

time: 132 us -> 124 us (0.939)
  Pallas kernels: 50.5 us -> 34.3 us
  local copies, waits for them, and re-layouts: 10.7 us -> 15.3 us
  starting transfers between devices: 43.6 us -> 46.6 us
    ppermute x3, waiting for transfers between devices: 0.01 us -> 6.13 us  [shards(): lax.ppermute(parts[k], 'col', along_z(k))]
    pallas_call x4 -> x5, Pallas kernels: 21.8 us -> 16.7 us  [the longest x1 13.2 us: forward(): pl.pallas_call(functools.partial(forward_kernel, first), out_shape=(pltpu...]
    unnamed x40 -> x44, local copies, waits for them, and re-layouts: 5.99 us -> 10.5 us
    all_to_all x1, waiting for transfers between devices: 3.5 us -> 0.01 us  [shards(): from_kv = lax.all_to_all(from_kv, 'row', 0, 0)]
    ppermute x7 -> x14, waiting for transfers between devices: 5.22 us -> 1.97 us  [the longest x6 1.95 us: gather_col(): near = [end] + [lax.ppermute(end, 'col', along_z(k)) for k in (1, 2, 3)]]
    pallas_call x1, Pallas kernels: 5.52 us -> 2.47 us  [prepare(): pl.pallas_call(prepare_kernel, out_shape=[array((width, rows), BF16)] * 2...]
    ppermute x1, starting transfers between devices: 2.8 us -> 5.45 us  [shards(): from_kv = lax.ppermute(from_kv, both, [(b, a) for a, b in home_to_block()])]
    ppermute x1, waiting for transfers between devices: 0.83 us -> 3.31 us  [shards(): from_kv = lax.ppermute(from_kv, both, [(b, a) for a, b in home_to_block()])]
  transfers between devices with their start and end apart: 19 -> 26, of which waited for: 12 -> 11; matrix products, arithmetic and copies ran while one was open for 5% -> 4% of each run, Pallas kernels for 11% -> 5%
where the time goes in v4:
time: 124 us; the launch traced here: 123 us
  starting transfers between devices  46.6 us (38%)
  Pallas kernels  34.3 us (28%)
  waiting for transfers between devices  22.6 us (18%)
  local copies, waits for them, and re-layouts  15.3 us (12%)
  other arithmetic  3.31 us (3%)
  between operations  1.32 us (1%)
    pallas_call x1, Pallas kernels, backward(): pl.pallas_call(functools.partial(backward_kernel, first), out_shape=[arra...  13.7 us
    pallas_call x1, Pallas kernels, forward(): pl.pallas_call(functools.partial(forward_kernel, first), out_shape=(pltpu...  13.2 us
    unnamed x44, local copies, waits for them, and re-layouts  10.5 us
    ppermute x1, starting transfers between devices, shards(): tokens = lax.ppermute(own[0], both, home_to_block())  6.5 us
    all_to_all x1, starting transfers between devices, shards(): lax.all_to_all(jnp.broadcast_to(tokens[None], (ROWS, *tokens.shape)), 'ro...  6.32 us
    ppermute x6, starting transfers between devices, gather_col(): near = [end] + [lax.ppermute(end, 'col', along_z(k)) for k in (1, 2, 3)]  6.24 us
    ppermute x3, waiting for transfers between devices, shards(): lax.ppermute(parts[k], 'col', along_z(k))  6.13 us
    ppermute x8, starting transfers between devices, gather_col(): far = [lax.ppermute(end, 'col', other_core()) for end in near]  5.59 us
  transfers between devices with their start and end apart: 26, of which 11 were waited for; matrix products, arithmetic and copies ran while one was open for 4% of the time, Pallas kernels for 5%

profile of v4, /device:TPU:1, one launch (start us, length us, event | category | flops | bytes accessed | tf_op | source)
XLA Modules:
  0.0 123.5 jit_solution(11057286931973672514)
XLA Ops:
  1.5 6.5 %collective-permute-start = (bf16[48,768]{1,0:T(8,128)(2,1)S(1)}, bf16[48,768]{1,0:T(8,128)(2,1)S(1)}, u32[]{:S(2)}, u32[]{:S(2)}) collective-permute-start(bf16[48,768]{1,0:T(8,128)(2,1)S(1)} %constant_dynamic-slice_fusion.1.own_ref), channel_id=1, source_target_pairs={{4,0},{29,1},{32,2},{57,3},{68,4},{93,5},{96,6},{121,7},{12,8},{21... | collective-permute-start | bytes 221192 | tf_op jit(solution)/shard_map/ppermute | solution.py:445
  8.7 1.2 collective-permute-done
  11.0 6.3 %all-to-all-start = ((bf16[16,48,768]{2,1,0:T(8,128)(2,1)}), bf16[16,48,768]{2,1,0:T(8,128)(2,1)}, u32[]{:S(2)}, u32[]{:S(2)}) async-start(bf16[16,48,768]{2,1,0:T(8,128)(2,1)} %broadcast_in_dim.56), calls=%async_computation | async-start | bytes 2359296 | tf_op jit(solution)/shard_map/all_to_all | solution.py:446
  21.7 2.5 %shard_map.112 = (bf16[768,384]{1,0:T(8,128)(2,1)S(1)}, bf16[768,384]{1,0:T(8,128)(2,1)S(1)}, f32[48,768]{1,0:T(8,128)S(1)}, f32[48,768]{1,0:T(8,128)S(1)}) custom-call(bf16[384,768]{1,0:T(8,128)(2,1)S(1)} %copy-done.4, bf16[384,768]{1,0:T(8,128)(2,1)S(1)} %copy-done.5, bf16[48,768]{1,0:T(8,128)(2,1)S(1)} %copy-done.8, ...), custom_call_target="tpu_custom_call" | custom-call | tf_op jit(solution)/shard_map/pallas_call | solution.py:322
  28.3 1.3 %concatenate.6.at_ref = s32[29]{0:T(128)} concatenate(s32[4]{0:T(128)} %add_multiply_fusion, s32[4]{0:T(128)} %get-tuple-element.46, s32[4]{0:T(128)S(1)} %get-tuple-element.45, s32[1]{0:T(128)} %bitcast, s32[1]{0:T(128)} %bitcast.1, s32[1]{0:T(128)} %bitcast.2, s32[1]{0:T(128)} %bitcast.3, s32[1]{0:T(128)} %bitcast.4, s32[1]{0:T(128)} %bitcast.5, s32[1]{0:T(128)} %bitcast.6, ...), dimensions={0} | concatenate | bytes 232 | tf_op jit(solution)/shard_map/concatenate | solution.py:435
  30.4 3.2 %all-to-all-done.refs_0_ = bf16[16,48,768]{2,1,0:T(8,128)(2,1)} async-done(((bf16[16,48,768]{2,1,0:T(8,128)(2,1)}), bf16[16,48,768]{2,1,0:T(8,128)(2,1)}, u32[]{:S(2)}, u32[]{:S(2)}) %all-to-all-start) | async-done | bytes 1179680 | tf_op jit(solution)/shard_map/all_to_all | solution.py:446
  34.1 13.2 %shard_map.113 = (bf16[16,384,768]{2,1,0:T(8,128)(2,1)S(1)}, bf16[1536,768]{1,0:T(8,128)(2,1)S(1)}, f32[768,384]{1,0:T(8,128)S(1)}, f32[48,384]{1,0:T(8,128)}) custom-call(s32[29]{0:T(128)} %concatenate.6.at_ref, bf16[16,48,768]{2,1,0:T(8,128)(2,1)} %all-to-all-done.refs_0_, bf16[16,384,768]{2,1,0:T(8,128)(2,1)} %refs_1_.1, bf16[768,384]{1,0:T(8,128)(2,1)} %copy-done.16, ...), custom_call_target="tpu_custom_call" | custom-call | flops 4831838208 | bytes 18874368 | tf_op jit(solution)/shard_map/pallas_call | solution.py:160
  47.3 4.0 %collective-permute-start.1 = (f32[48,384]{1,0:T(8,128)}, f32[48,384]{1,0:T(8,128)S(1)}, u32[]{:S(2)}, u32[]{:S(2)}) collective-permute-start(f32[48,384]{1,0:T(8,128)} %get-tuple-element.25.left_ref.refs_0_), channel_id=1, source_target_pairs={{0,1},{1,0},{2,3},{3,2},{4,5},{5,4},{6,7},{7,6},{8,9},{9,8},{10,11... | collective-permute-start | bytes 221192 | tf_op jit(solution)/shard_map/ppermute | solution.py:462
  51.3 1.1 collective-permute-done.1.right_ref
  53.4 2.0 %collective-permute-start.4 = (f32[48,384]{1,0:T(8,128)S(1)}, f32[48,384]{1,0:T(8,128)S(1)}, u32[]{:S(2)}, u32[]{:S(2)}) collective-permute-start(f32[48,384]{1,0:T(8,128)S(1)} %shard_map.114.refs_1_), channel_id=1, source_target_pairs={{0,4},{1,5},{2,6},{3,7},{4,0},{5,1},{6,2},{7,3},{8,12},{9,13},{10,... | collective-permute-start | bytes 221192 | tf_op jit(solution)/shard_map/ppermute | solution.py:463
  55.4 1.2 collective-permute-start.3
  56.9 1.3 %collective-permute-done.4.refs_4_ = f32[48,384]{1,0:T(8,128)S(1)} collective-permute-done((f32[48,384]{1,0:T(8,128)S(1)}, f32[48,384]{1,0:T(8,128)S(1)}, u32[]{:S(2)}, u32[]{:S(2)}) %collective-permute-start.4) | collective-permute-done | bytes 73760 | tf_op jit(solution)/shard_map/ppermute | solution.py:463
  58.2 2.1 %collective-permute-done.3.refs_3_ = f32[48,384]{1,0:T(8,128)S(1)} collective-permute-done((f32[48,384]{1,0:T(8,128)S(1)}, f32[48,384]{1,0:T(8,128)S(1)}, u32[]{:S(2)}, u32[]{:S(2)}) %collective-permute-start.3) | collective-permute-done | bytes 73760 | tf_op jit(solution)/shard_map/ppermute | solution.py:463
  61.6 13.7 %shard_map.115 = (bf16[16,384,768]{2,1,0:T(8,128)(2,1)}, bf16[768,384]{1,0:T(8,128)(2,1)}, bf16[16,48,768]{2,1,0:T(8,128)(2,1)}, f32[768,384]{1,0:T(8,128)}) custom-call(s32[29]{0:T(128)} %concatenate.6.at_ref, f32[48,384]{1,0:T(8,128)} %get-tuple-element.25.left_ref.refs_0_, f32[48,384]{1,0:T(8,128)} %copy-done.14, f32[48,384]{1,0:T(8,128)} %copy-done.21, ...), custom_call_target="tpu_custom_call" | custom-call | flops 9663676416 | bytes 18874368 | tf_op jit(solution)/shard_map/pallas_call | solution.py:288
  75.4 4.4 %all-to-all-start.1 = ((bf16[16,48,768]{2,1,0:T(8,128)(2,1)}), bf16[16,48,768]{2,1,0:T(8,128)(2,1)}, u32[]{:S(2)}, u32[]{:S(2)}) async-start(bf16[16,48,768]{2,1,0:T(8,128)(2,1)} %get-tuple-element.41), calls=%async_computation.1 | async-start | bytes 2359296 | tf_op jit(solution)/shard_map/all_to_all | solution.py:466
  79.8 1.3 %copy-done.3 = f32[768,384]{1,0:T(8,128)S(1)} copy-done((f32[768,384]{1,0:T(8,128)S(1)}, f32[768,384]{1,0:T(8,128)}, u32[]{:S(2)}) %copy-start.3) | copy-done | bytes 1179672
  82.1 1.3 %shard_map.116 = (bf16[384,768]{1,0:T(8,128)(2,1)S(1)}, bf16[384,768]{1,0:T(8,128)(2,1)S(1)}) custom-call(s32[29]{0:T(128)S(1)} %copy-done.15, bf16[768,384]{1,0:T(8,128)(2,1)S(1)} %copy-done.6, f32[768,384]{1,0:T(8,128)S(1)} %copy-done.3, bf16[768,768]{1,0:T(8,128)(2,1)S(1)} %copy-done), custom_call_target="tpu_custom_call" | custom-call | tf_op jit(solution)/shard_map/pallas_call | solution.py:364
  83.4 1.9 %collective-permute-start.5 = (bf16[384,768]{1,0:T(8,128)(2,1)S(1)}, bf16[384,768]{1,0:T(8,128)(2,1)S(1)}, u32[]{:S(2)}, u32[]{:S(2)}) collective-permute-start(bf16[384,768]{1,0:T(8,128)(2,1)S(1)} %get-tuple-element.32), channel_id=1, source_target_pairs={{0,1},{1,0},{2,3},{3,2},{4,5},{5,4},{6,7},{7,6},{8,9},{9,8},{10,11... | collective-permute-start | bytes 1769480 | tf_op jit(solution)/shard_map/ppermute | solution.py:468
  85.3 1.6 %collective-permute-done.5.right_ref = bf16[384,768]{1,0:T(8,128)(2,1)S(1)} collective-permute-done((bf16[384,768]{1,0:T(8,128)(2,1)S(1)}, bf16[384,768]{1,0:T(8,128)(2,1)S(1)}, u32[]{:S(2)}, u32[]{:S(2)}) %collective-permute-start.5) | collective-permute-done | bytes 589856 | tf_op jit(solution)/shard_map/ppermute | solution.py:468
  87.2 2.7 %collective-permute-start.7 = (bf16[96,768]{1,0:T(8,128)(2,1)S(1)}, bf16[96,768]{1,0:T(8,128)(2,1)S(1)}, u32[]{:S(2)}, u32[]{:S(2)}) collective-permute-start(bf16[96,768]{1,0:T(8,128)(2,1)S(1)} %get-tuple-element.35), channel_id=1, source_target_pairs={{0,6},{1,7},{2,0},{3,1},{4,2},{5,3},{6,4},{7,5},{8,14},{9,15},{10,... | collective-permute-start | bytes 442376 | tf_op jit(solution)/shard_map/ppermute | solution.py:470
  89.8 3.7 %collective-permute-done.6.refs_1_ = bf16[96,768]{1,0:T(8,128)(2,1)S(1)} collective-permute-done((bf16[96,768]{1,0:T(8,128)(2,1)S(1)}, bf16[96,768]{1,0:T(8,128)(2,1)S(1)}, u32[]{:S(2)}, u32[]{:S(2)}) %collective-permute-start.6) | collective-permute-done | bytes 147488 | tf_op jit(solution)/shard_map/ppermute | solution.py:470
  93.5 2.4 %collective-permute-done.8.refs_3_ = bf16[96,768]{1,0:T(8,128)(2,1)S(1)} collective-permute-done((bf16[96,768]{1,0:T(8,128)(2,1)S(1)}, bf16[96,768]{1,0:T(8,128)(2,1)S(1)}, u32[]{:S(2)}, u32[]{:S(2)}) %collective-permute-start.8) | collective-permute-done | bytes 147488 | tf_op jit(solution)/shard_map/ppermute | solution.py:470
  96.6 3.4 %collective-permute-start.11 = (bf16[48,768]{1,0:T(8,128)(2,1)S(1)}, bf16[48,768]{1,0:T(8,128)(2,1)S(1)}, u32[]{:S(2)}, u32[]{:S(2)}) collective-permute-start(bf16[48,768]{1,0:T(8,128)(2,1)S(1)} %get-tuple-element.39.refs_0_), channel_id=1, source_target_pairs={{0,6},{1,7},{2,0},{3,1},{4,2},{5,3},{6,4},{7,5},{8,14},{9,15},{10,... | collective-permute-start | bytes 221192 | tf_op jit(solution)/shard_map/ppermute | solution.py:416
  100.0 1.4 %reduce_sum.12 = bf16[48,768]{1,0:T(8,128)(2,1)S(1)} reduce(bf16[16,48,768]{2,1,0:T(8,128)(2,1)} %all-to-all-done.1, bf16[]{:T(256)} %constant.304.clone.1), dimensions={0}, to_apply=%region_0.1 | reduce | flops 552960 | bytes 1253378 | tf_op jit(solution)/shard_map/reduce_sum | solution.py:473
  101.4 5.4 %collective-permute-start.16 = (bf16[48,768]{1,0:T(8,128)(2,1)S(1)}, bf16[48,768]{1,0:T(8,128)(2,1)S(1)}, u32[]{:S(2)}, u32[]{:S(2)}) collective-permute-start(bf16[48,768]{1,0:T(8,128)(2,1)S(1)} %reduce_sum.12), channel_id=1, source_target_pairs={{0,4},{1,29},{2,32},{3,57},{4,68},{5,93},{6,96},{7,121},{8,12},{9,... | collective-permute-start | bytes 221192 | tf_op jit(solution)/shard_map/ppermute | solution.py:474
  107.6 3.3 %collective-permute-done.16.kv_ref = bf16[48,768]{1,0:T(8,128)(2,1)S(1)} collective-permute-done((bf16[48,768]{1,0:T(8,128)(2,1)S(1)}, bf16[48,768]{1,0:T(8,128)(2,1)S(1)}, u32[]{:S(2)}, u32[]{:S(2)}) %collective-permute-start.16) | collective-permute-done | bytes 73760 | tf_op jit(solution)/shard_map/ppermute | solution.py:474
  110.9 2.2 %collective-permute-start.19 = (bf16[48,768]{1,0:T(8,128)(2,1)S(1)}, bf16[48,768]{1,0:T(8,128)(2,1)S(1)}, u32[]{:S(2)}, u32[]{:S(2)}) collective-permute-start(bf16[48,768]{1,0:T(8,128)(2,1)S(1)} %shard_map.120.refs_0_), channel_id=1, source_target_pairs={{0,6},{1,7},{2,0},{3,1},{4,2},{5,3},{6,4},{7,5},{8,14},{9,15},{10,... | collective-permute-start | bytes 221192 | tf_op jit(solution)/shard_map/ppermute | solution.py:416
  113.8 2.6 %collective-permute-start.13 = (bf16[48,768]{1,0:T(8,128)(2,1)S(1)}, bf16[48,768]{1,0:T(8,128)(2,1)S(1)}, u32[]{:S(2)}, u32[]{:S(2)}) collective-permute-start(bf16[48,768]{1,0:T(8,128)(2,1)S(1)} %collective-permute-done.9.refs_1_), channel_id=1, source_target_pairs={{0,1},{1,0},{2,3},{3,2},{4,5},{5,4},{6,7},{7,6},{8,9},{9,8},{10,11... | collective-permute-start | bytes 221192 | tf_op jit(solution)/shard_map/ppermute | solution.py:417
  116.9 1.9 %collective-permute-done.18.refs_2_ = bf16[48,768]{1,0:T(8,128)(2,1)S(1)} collective-permute-done((bf16[48,768]{1,0:T(8,128)(2,1)S(1)}, bf16[48,768]{1,0:T(8,128)(2,1)S(1)}, u32[]{:S(2)}, u32[]{:S(2)}) %collective-permute-start.18) | collective-permute-done | bytes 73760 | tf_op jit(solution)/shard_map/ppermute | solution.py:416
  119.4 1.2 collective-permute-start.21
  120.6 1.4 %shard_map.119 = bf16[384,768]{1,0:T(8,128)(2,1)} custom-call(s32[29]{0:T(128)S(1)} %copy-done.15, bf16[48,768]{1,0:T(8,128)(2,1)S(1)} %get-tuple-element.39.refs_0_, bf16[48,768]{1,0:T(8,128)(2,1)S(1)} %collective-permute-done.9.refs_1_, bf16[48,768]{1,0:T(8,128)(2,1)S(1)} %collective-permute-done.10.refs_2_, ...), custom_call_target="tpu_custom_call" | custom-call | tf_op jit(solution)/shard_map/pallas_call | solution.py:419
  122.1 1.4 %shard_map.121 = bf16[384,768]{1,0:T(8,128)(2,1)} custom-call(s32[29]{0:T(128)S(1)} %copy-done.15, bf16[48,768]{1,0:T(8,128)(2,1)S(1)} %shard_map.120.refs_0_, bf16[48,768]{1,0:T(8,128)(2,1)S(1)} %collective-permute-done.17.refs_1_, bf16[48,768]{1,0:T(8,128)(2,1)S(1)} %collective-permute-done.18.refs_2_, ...), custom_call_target="tpu_custom_call" | custom-call | tf_op jit(solution)/shard_map/pallas_call | solution.py:419
  (88 shorter events, 19.1 us)
Async XLA Ops:
  1.5 8.4 %collective-permute-start = (bf16[48,768]{1,0:T(8,128)(2,1)S(1)}, bf16[48,768]{1,0:T(8,128)(2,1)S(1)}, u32[]{:S(2)}, u32[]{:S(2)}) collective-permute-start(bf16[48,768]{1,0:T(8,128)(2,1)S(1)} %constant_dynamic-slice_fusion.1.own_ref), channel_id=1, source_target_pairs={{4,0},{29,1},{32,2},{57,3},{68,4},{93,5},{96,6},{121,7},{12,8},{21... | collective-permute-start | bytes 221192 | tf_op jit(solution)/shard_map/ppermute | solution.py:445
  9.9 8.8 %copy-start.2 = (bf16[768,768]{1,0:T(8,128)(2,1)S(1)}, bf16[768,768]{1,0:T(8,128)(2,1)}, u32[]{:S(2)}) copy-start(bf16[768,768]{1,0:T(8,128)(2,1)} %refs_6_.1) | copy-start | bytes 3538948
  11.0 7.7 %copy-start = (bf16[768,768]{1,0:T(8,128)(2,1)S(1)}, bf16[768,768]{1,0:T(8,128)(2,1)}, u32[]{:S(2)}) copy-start(bf16[768,768]{1,0:T(8,128)(2,1)} %w_ref.1) | copy-start | bytes 3538948
  11.0 7.7 %copy-start.1 = (bf16[768,768]{1,0:T(8,128)(2,1)S(1)}, bf16[768,768]{1,0:T(8,128)(2,1)}, u32[]{:S(2)}) copy-start(bf16[768,768]{1,0:T(8,128)(2,1)} %refs_7_.1) | copy-start | bytes 3538948
  11.0 22.5 %all-to-all-start = ((bf16[16,48,768]{2,1,0:T(8,128)(2,1)}), bf16[16,48,768]{2,1,0:T(8,128)(2,1)}, u32[]{:S(2)}, u32[]{:S(2)}) async-start(bf16[16,48,768]{2,1,0:T(8,128)(2,1)} %broadcast_in_dim.56), calls=%async_computation | async-start | bytes 2359296 | tf_op jit(solution)/shard_map/all_to_all | solution.py:446
  47.3 5.1 %collective-permute-start.1 = (f32[48,384]{1,0:T(8,128)}, f32[48,384]{1,0:T(8,128)S(1)}, u32[]{:S(2)}, u32[]{:S(2)}) collective-permute-start(f32[48,384]{1,0:T(8,128)} %get-tuple-element.25.left_ref.refs_0_), channel_id=1, source_target_pairs={{0,1},{1,0},{2,3},{3,2},{4,5},{5,4},{6,7},{7,6},{8,9},{9,8},{10,11... | collective-permute-start | bytes 221192 | tf_op jit(solution)/shard_map/ppermute | solution.py:462
  53.4 7.6 %copy-start.14 = (f32[48,384]{1,0:T(8,128)}, f32[48,384]{1,0:T(8,128)S(1)}, u32[]{:S(2)}) copy-start(f32[48,384]{1,0:T(8,128)S(1)} %shard_map.114.refs_1_) | copy-start | bytes 221188
  53.4 4.8 %collective-permute-start.4 = (f32[48,384]{1,0:T(8,128)S(1)}, f32[48,384]{1,0:T(8,128)S(1)}, u32[]{:S(2)}, u32[]{:S(2)}) collective-permute-start(f32[48,384]{1,0:T(8,128)S(1)} %shard_map.114.refs_1_), channel_id=1, source_target_pairs={{0,4},{1,5},{2,6},{3,7},{4,0},{5,1},{6,2},{7,3},{8,12},{9,13},{10,... | collective-permute-start | bytes 221192 | tf_op jit(solution)/shard_map/ppermute | solution.py:463
  55.4 4.8 %collective-permute-start.3 = (f32[48,384]{1,0:T(8,128)S(1)}, f32[48,384]{1,0:T(8,128)S(1)}, u32[]{:S(2)}, u32[]{:S(2)}) collective-permute-start(f32[48,384]{1,0:T(8,128)S(1)} %shard_map.114.refs_1_), channel_id=1, source_target_pairs={{0,6},{1,7},{2,0},{3,1},{4,2},{5,3},{6,4},{7,5},{8,14},{9,15},{10,... | collective-permute-start | bytes 221192 | tf_op jit(solution)/shard_map/ppermute | solution.py:463
  56.6 4.4 %collective-permute-start.2 = (f32[48,384]{1,0:T(8,128)S(1)}, f32[48,384]{1,0:T(8,128)S(1)}, u32[]{:S(2)}, u32[]{:S(2)}) collective-permute-start(f32[48,384]{1,0:T(8,128)S(1)} %shard_map.114.refs_1_), channel_id=1, source_target_pairs={{0,2},{1,3},{2,4},{3,5},{4,6},{5,7},{6,0},{7,1},{8,10},{9,11},{10,... | collective-permute-start | bytes 221192 | tf_op jit(solution)/shard_map/ppermute | solution.py:463
  75.4 24.6 %all-to-all-start.1 = ((bf16[16,48,768]{2,1,0:T(8,128)(2,1)}), bf16[16,48,768]{2,1,0:T(8,128)(2,1)}, u32[]{:S(2)}, u32[]{:S(2)}) async-start(bf16[16,48,768]{2,1,0:T(8,128)(2,1)} %get-tuple-element.41), calls=%async_computation.1 | async-start | bytes 2359296 | tf_op jit(solution)/shard_map/all_to_all | solution.py:466
  83.4 12.5 %copy-start.10 = (f32[48,768]{1,0:T(8,128)S(1)}, f32[48,768]{1,0:T(8,128)}, u32[]{:S(2)}) copy-start(f32[48,768]{1,0:T(8,128)} %copy-done.9) | copy-start | bytes 442372
  83.4 12.5 %copy-start.12 = (f32[48,768]{1,0:T(8,128)S(1)}, f32[48,768]{1,0:T(8,128)}, u32[]{:S(2)}) copy-start(f32[48,768]{1,0:T(8,128)} %copy-done.11) | copy-start | bytes 442372
  83.4 3.5 %collective-permute-start.5 = (bf16[384,768]{1,0:T(8,128)(2,1)S(1)}, bf16[384,768]{1,0:T(8,128)(2,1)S(1)}, u32[]{:S(2)}, u32[]{:S(2)}) collective-permute-start(bf16[384,768]{1,0:T(8,128)(2,1)S(1)} %get-tuple-element.32), channel_id=1, source_target_pairs={{0,1},{1,0},{2,3},{3,2},{4,5},{5,4},{6,7},{7,6},{8,9},{9,8},{10,11... | collective-permute-start | bytes 1769480 | tf_op jit(solution)/shard_map/ppermute | solution.py:468
  87.1 6.4 %collective-permute-start.6 = (bf16[96,768]{1,0:T(8,128)(2,1)S(1)}, bf16[96,768]{1,0:T(8,128)(2,1)S(1)}, u32[]{:S(2)}, u32[]{:S(2)}) collective-permute-start(bf16[96,768]{1,0:T(8,128)(2,1)S(1)} %get-tuple-element.34), channel_id=1, source_target_pairs={{0,2},{1,3},{2,4},{3,5},{4,6},{5,7},{6,0},{7,1},{8,10},{9,11},{10,... | collective-permute-start | bytes 442376 | tf_op jit(solution)/shard_map/ppermute | solution.py:470
  87.2 6.4 %collective-permute-start.7 = (bf16[96,768]{1,0:T(8,128)(2,1)S(1)}, bf16[96,768]{1,0:T(8,128)(2,1)S(1)}, u32[]{:S(2)}, u32[]{:S(2)}) collective-permute-start(bf16[96,768]{1,0:T(8,128)(2,1)S(1)} %get-tuple-element.35), channel_id=1, source_target_pairs={{0,6},{1,7},{2,0},{3,1},{4,2},{5,3},{6,4},{7,5},{8,14},{9,15},{10,... | collective-permute-start | bytes 442376 | tf_op jit(solution)/shard_map/ppermute | solution.py:470
  89.8 6.1 %collective-permute-start.8 = (bf16[96,768]{1,0:T(8,128)(2,1)S(1)}, bf16[96,768]{1,0:T(8,128)(2,1)S(1)}, u32[]{:S(2)}, u32[]{:S(2)}) collective-permute-start(bf16[96,768]{1,0:T(8,128)(2,1)S(1)} %get-tuple-element.36), channel_id=1, source_target_pairs={{0,4},{1,5},{2,6},{3,7},{4,0},{5,1},{6,2},{7,3},{8,12},{9,13},{10,... | collective-permute-start | bytes 442376 | tf_op jit(solution)/shard_map/ppermute | solution.py:470
  96.6 10.3 %collective-permute-start.11 = (bf16[48,768]{1,0:T(8,128)(2,1)S(1)}, bf16[48,768]{1,0:T(8,128)(2,1)S(1)}, u32[]{:S(2)}, u32[]{:S(2)}) collective-permute-start(bf16[48,768]{1,0:T(8,128)(2,1)S(1)} %get-tuple-element.39.refs_0_), channel_id=1, source_target_pairs={{0,6},{1,7},{2,0},{3,1},{4,2},{5,3},{6,4},{7,5},{8,14},{9,15},{10,... | collective-permute-start | bytes 221192 | tf_op jit(solution)/shard_map/ppermute | solution.py:416
  100.0 7.4 %collective-permute-start.10 = (bf16[48,768]{1,0:T(8,128)(2,1)S(1)}, bf16[48,768]{1,0:T(8,128)(2,1)S(1)}, u32[]{:S(2)}, u32[]{:S(2)}) collective-permute-start(bf16[48,768]{1,0:T(8,128)(2,1)S(1)} %get-tuple-element.39.refs_0_), channel_id=1, source_target_pairs={{0,4},{1,5},{2,6},{3,7},{4,0},{5,1},{6,2},{7,3},{8,12},{9,13},{10,... | collective-permute-start | bytes 221192 | tf_op jit(solution)/shard_map/ppermute | solution.py:416
  101.4 9.4 %collective-permute-start.16 = (bf16[48,768]{1,0:T(8,128)(2,1)S(1)}, bf16[48,768]{1,0:T(8,128)(2,1)S(1)}, u32[]{:S(2)}, u32[]{:S(2)}) collective-permute-start(bf16[48,768]{1,0:T(8,128)(2,1)S(1)} %reduce_sum.12), channel_id=1, source_target_pairs={{0,4},{1,29},{2,32},{3,57},{4,68},{5,93},{6,96},{7,121},{8,12},{9,... | collective-permute-start | bytes 221192 | tf_op jit(solution)/shard_map/ppermute | solution.py:474
  106.9 6.2 %collective-permute-start.12 = (bf16[48,768]{1,0:T(8,128)(2,1)S(1)}, bf16[48,768]{1,0:T(8,128)(2,1)S(1)}, u32[]{:S(2)}, u32[]{:S(2)}) collective-permute-start(bf16[48,768]{1,0:T(8,128)(2,1)S(1)} %get-tuple-element.39.refs_0_), channel_id=1, source_target_pairs={{0,1},{1,0},{2,3},{3,2},{4,5},{5,4},{6,7},{7,6},{8,9},{9,8},{10,11... | collective-permute-start | bytes 221192 | tf_op jit(solution)/shard_map/ppermute | solution.py:417
  106.9 6.2 %collective-permute-start.9 = (bf16[48,768]{1,0:T(8,128)(2,1)S(1)}, bf16[48,768]{1,0:T(8,128)(2,1)S(1)}, u32[]{:S(2)}, u32[]{:S(2)}) collective-permute-start(bf16[48,768]{1,0:T(8,128)(2,1)S(1)} %get-tuple-element.39.refs_0_), channel_id=1, source_target_pairs={{0,2},{1,3},{2,4},{3,5},{4,6},{5,7},{6,0},{7,1},{8,10},{9,11},{10,... | collective-permute-start | bytes 221192 | tf_op jit(solution)/shard_map/ppermute | solution.py:416
  106.9 6.9 %collective-permute-start.15 = (bf16[48,768]{1,0:T(8,128)(2,1)S(1)}, bf16[48,768]{1,0:T(8,128)(2,1)S(1)}, u32[]{:S(2)}, u32[]{:S(2)}) collective-permute-start(bf16[48,768]{1,0:T(8,128)(2,1)S(1)} %collective-permute-done.11.refs_3_), channel_id=1, source_target_pairs={{0,1},{1,0},{2,3},{3,2},{4,5},{5,4},{6,7},{7,6},{8,9},{9,8},{10,11... | collective-permute-start | bytes 221192 | tf_op jit(solution)/shard_map/ppermute | solution.py:417
  107.4 9.0 %collective-permute-start.14 = (bf16[48,768]{1,0:T(8,128)(2,1)S(1)}, bf16[48,768]{1,0:T(8,128)(2,1)S(1)}, u32[]{:S(2)}, u32[]{:S(2)}) collective-permute-start(bf16[48,768]{1,0:T(8,128)(2,1)S(1)} %collective-permute-done.10.refs_2_), channel_id=1, source_target_pairs={{0,1},{1,0},{2,3},{3,2},{4,5},{5,4},{6,7},{7,6},{8,9},{9,8},{10,11... | collective-permute-start | bytes 221192 | tf_op jit(solution)/shard_map/ppermute | solution.py:417
  110.9 5.6 %collective-permute-start.19 = (bf16[48,768]{1,0:T(8,128)(2,1)S(1)}, bf16[48,768]{1,0:T(8,128)(2,1)S(1)}, u32[]{:S(2)}, u32[]{:S(2)}) collective-permute-start(bf16[48,768]{1,0:T(8,128)(2,1)S(1)} %shard_map.120.refs_0_), channel_id=1, source_target_pairs={{0,6},{1,7},{2,0},{3,1},{4,2},{5,3},{6,4},{7,5},{8,14},{9,15},{10,... | collective-permute-start | bytes 221192 | tf_op jit(solution)/shard_map/ppermute | solution.py:416
  113.1 5.7 %collective-permute-start.18 = (bf16[48,768]{1,0:T(8,128)(2,1)S(1)}, bf16[48,768]{1,0:T(8,128)(2,1)S(1)}, u32[]{:S(2)}, u32[]{:S(2)}) collective-permute-start(bf16[48,768]{1,0:T(8,128)(2,1)S(1)} %shard_map.120.refs_0_), channel_id=1, source_target_pairs={{0,4},{1,5},{2,6},{3,7},{4,0},{5,1},{6,2},{7,3},{8,12},{9,13},{10,... | collective-permute-start | bytes 221192 | tf_op jit(solution)/shard_map/ppermute | solution.py:416
  113.1 6.3 %collective-permute-start.17 = (bf16[48,768]{1,0:T(8,128)(2,1)S(1)}, bf16[48,768]{1,0:T(8,128)(2,1)S(1)}, u32[]{:S(2)}, u32[]{:S(2)}) collective-permute-start(bf16[48,768]{1,0:T(8,128)(2,1)S(1)} %shard_map.120.refs_0_), channel_id=1, source_target_pairs={{0,2},{1,3},{2,4},{3,5},{4,6},{5,7},{6,0},{7,1},{8,10},{9,11},{10,... | collective-permute-start | bytes 221192 | tf_op jit(solution)/shard_map/ppermute | solution.py:416
  113.8 6.9 %collective-permute-start.13 = (bf16[48,768]{1,0:T(8,128)(2,1)S(1)}, bf16[48,768]{1,0:T(8,128)(2,1)S(1)}, u32[]{:S(2)}, u32[]{:S(2)}) collective-permute-start(bf16[48,768]{1,0:T(8,128)(2,1)S(1)} %collective-permute-done.9.refs_1_), channel_id=1, source_target_pairs={{0,1},{1,0},{2,3},{3,2},{4,5},{5,4},{6,7},{7,6},{8,9},{9,8},{10,11... | collective-permute-start | bytes 221192 | tf_op jit(solution)/shard_map/ppermute | solution.py:417
  116.4 5.7 %collective-permute-start.20 = (bf16[48,768]{1,0:T(8,128)(2,1)S(1)}, bf16[48,768]{1,0:T(8,128)(2,1)S(1)}, u32[]{:S(2)}, u32[]{:S(2)}) collective-permute-start(bf16[48,768]{1,0:T(8,128)(2,1)S(1)} %shard_map.120.refs_0_), channel_id=1, source_target_pairs={{0,1},{1,0},{2,3},{3,2},{4,5},{5,4},{6,7},{7,6},{8,9},{9,8},{10,11... | collective-permute-start | bytes 221192 | tf_op jit(solution)/shard_map/ppermute | solution.py:417
  116.5 5.6 %collective-permute-start.23 = (bf16[48,768]{1,0:T(8,128)(2,1)S(1)}, bf16[48,768]{1,0:T(8,128)(2,1)S(1)}, u32[]{:S(2)}, u32[]{:S(2)}) collective-permute-start(bf16[48,768]{1,0:T(8,128)(2,1)S(1)} %collective-permute-done.19.refs_3_), channel_id=1, source_target_pairs={{0,1},{1,0},{2,3},{3,2},{4,5},{5,4},{6,7},{7,6},{8,9},{9,8},{10,11... | collective-permute-start | bytes 221192 | tf_op jit(solution)/shard_map/ppermute | solution.py:417
  118.8 3.2 %collective-permute-start.22 = (bf16[48,768]{1,0:T(8,128)(2,1)S(1)}, bf16[48,768]{1,0:T(8,128)(2,1)S(1)}, u32[]{:S(2)}, u32[]{:S(2)}) collective-permute-start(bf16[48,768]{1,0:T(8,128)(2,1)S(1)} %collective-permute-done.18.refs_2_), channel_id=1, source_target_pairs={{0,1},{1,0},{2,3},{3,2},{4,5},{5,4},{6,7},{7,6},{8,9},{9,8},{10,11... | collective-permute-start | bytes 221192 | tf_op jit(solution)/shard_map/ppermute | solution.py:417
  119.4 2.6 %collective-permute-start.21 = (bf16[48,768]{1,0:T(8,128)(2,1)S(1)}, bf16[48,768]{1,0:T(8,128)(2,1)S(1)}, u32[]{:S(2)}, u32[]{:S(2)}) collective-permute-start(bf16[48,768]{1,0:T(8,128)(2,1)S(1)} %collective-permute-done.17.refs_1_), channel_id=1, source_target_pairs={{0,1},{1,0},{2,3},{3,2},{4,5},{5,4},{6,7},{7,6},{8,9},{9,8},{10,11... | collective-permute-start | bytes 221192 | tf_op jit(solution)/shard_map/ppermute | solution.py:417
  (16 other events, 25.3 us)

commit v5 on v4

--- a/solution.py
+++ b/solution.py
@@ -93,14 +93,14 @@
 
 
 def forward_kernel(first, at_ref, *refs):
-    tokens_hbm, bias_hbm, q_hbm, wk_hbm, wv_hbm, mask_hbm, row_hbm, dh_hbm, expo_ref, kv_ref, num_ref, stats_ref = refs[:12]
-    tokens, w_ref, q_ref, mask_ref, row_ref, dh_ref, bias_ref, tops, score_ref, sems = refs[12:]
+    tokens_hbm, bias_hbm, q_hbm, wk_hbm, wv_hbm, mask_hbm, dh_hbm, expo_ref, kv_ref, num_ref, stats_ref = refs[:11]
+    tokens, w_ref, q_ref, mask_ref, dh_ref, bias_ref, tops, score_ref, sems = refs[11:]
     start = copier(sems)
     width, rows = q_ref.shape
     early = [start(wk_hbm, w_ref.at[0]), start(wv_hbm, w_ref.at[1])]
     for n in range(ROWS):
         early.append(start(tokens_hbm.at[n], tokens.at[rows_at(at_ref[first + n], tokens_hbm.shape[1])]))
-    late = [start(a, b) for a, b in ((q_hbm, q_ref), (mask_hbm, mask_ref), (row_hbm, row_ref), (dh_hbm, dh_ref))]
+    late = [start(a, b) for a, b in ((q_hbm, q_ref), (mask_hbm, mask_ref), (dh_hbm, dh_ref))]
     bias_in = [start(bias_hbm.at[h], bias_ref.at[h]) for h in range(HEADS)]
     for copy in early:
         copy.wait()
@@ -114,6 +114,7 @@
     ones_k = jnp.ones((EXTRA, tokens.shape[0]), BF16)
     ones_q = jnp.ones((EXTRA, rows), BF16)
     live, dead = mask_ref[:HD, :], mask_ref[HD:, :]
+    factor = mask_ref[:EXTRA, :].astype(F32)[0:1, :] * LOG2E
 
     def scores_of(h):
         mine = slice(h * HD, (h + 1) * HD)
@@ -125,7 +126,7 @@
         lane = lax.broadcasted_iota(jnp.int32, (CHUNK, 128), 1)
         for c in range(0, rows, CHUNK):
             part = slice(c, c + CHUNK)
-            scores = score_ref[h % 2, part, :] + bias_ref[h, part, :].astype(F32) * row_ref[0:1, :]
+            scores = score_ref[h % 2, part, :] + bias_ref[h, part, :].astype(F32) * factor
             top = jnp.max(scores, axis=-1, keepdims=True)
             expo_ref[h, part, :] = jnp.exp2(scores - top).astype(BF16)
             tops[part, :] = jnp.where(lane == h, top, tops[part, :])
@@ -154,7 +155,7 @@
     stats_ref[HEADS : 2 * HEADS, :] = tops[...].T[:HEADS, :]
 
 
-def forward(at, first, tokens, bias, q, wk, wv, mask, row, dh):
+def forward(at, first, tokens, bias, q, wk, wv, mask, dh):
     rows, span = bias.shape[1:]
     width = wk.shape[0]
     return pl.pallas_call(
@@ -165,14 +166,13 @@
             pltpu.VMEM((width, rows), F32),
             array((3 * HEADS, rows), F32),
         ),
-        in_specs=[SCALAR] + [HBM] * 8,
+        in_specs=[SCALAR] + [HBM] * 7,
         out_specs=tuple(whole(4)),
         scratch_shapes=[
             pltpu.VMEM((span, width), BF16),
             pltpu.VMEM((2, *wk.shape), BF16),
             pltpu.VMEM(q.shape, BF16),
             pltpu.VMEM(mask.shape, BF16),
-            pltpu.VMEM(row.shape, F32),
             pltpu.VMEM(dh.shape, BF16),
             pltpu.VMEM(bias.shape, BF16),
             pltpu.VMEM((rows, 128), F32),
@@ -181,7 +181,7 @@
         ],
         compiler_params=params(42),
         cost_estimate=pl.CostEstimate(flops=4 * HEADS * rows * span * 256, bytes_accessed=4 * HEADS * rows * span, transcendentals=HEADS * rows * span),
-    )(at, tokens, bias, q, wk, wv, mask, row, dh)
+    )(at, tokens, bias, q, wk, wv, mask, dh)
 
 
 def merge(stats):
@@ -404,25 +404,29 @@
 
 
 def join_kernel(first, at_ref, *refs):
-    ends, out = refs[:-1], refs[-1]
-    size = ends[0].shape[0]
     core = at_ref[first + SIDE]
-    for k, end in enumerate(ends):
-        shift = core if k < SIDE else size - core
-        out[rows_at(at_ref[first + k % SIDE] + shift, size), :] = end[...]
-
-
-def gather_col(at, first, end):
+    for n, out in enumerate(refs[-2:]):
+        ends = refs[n * COLS : (n + 1) * COLS]
+        size = ends[0].shape[0]
+        for k, end in enumerate(ends):
+            shift = core if k < SIDE else size - core
+            out[rows_at(at_ref[first + k % SIDE] + shift, size), :] = end[...]
+
+
+def gather_col(end):
     near = [end] + [lax.ppermute(end, "col", along_z(k)) for k in (1, 2, 3)]
-    far = [lax.ppermute(end, "col", other_core()) for end in near]
-    size, width = end.shape
+    return near + [lax.ppermute(end, "col", other_core()) for end in near]
+
+
+def join(at, first, left, right):
+    size, width = left[0].shape
     return pl.pallas_call(
         functools.partial(join_kernel, first),
-        out_shape=array((size * COLS, width), BF16),
-        in_specs=[SCALAR] + whole(COLS),
-        out_specs=whole(1)[0],
-        compiler_params=params(),
-    )(at, *near, *far)
+        out_shape=[array((size * COLS, width), BF16)] * 2,
+        in_specs=[SCALAR] + whole(2 * COLS),
+        out_specs=whole(2),
+        compiler_params=params(),
+    )(at, *left, *right)
 
 
 def shards(single, pair_bias, key_live, w_query, w_key, w_value, w_gate, w_out, cotangent):
@@ -446,7 +450,6 @@
     tokens = lax.all_to_all(jnp.broadcast_to(tokens[None], (ROWS, *tokens.shape)), "row", 0, 0)
     q, dh, gate, d_hidden = prepare(single, cotangent, own, w_query, w_gate, w_out)
     alive = key_live[None, :] > 0
-    row = jnp.broadcast_to(jnp.where(alive, LOG2E, 0.0).astype(F32), (8, span))
     live = jnp.broadcast_to(alive, (HD, span)).astype(BF16)
     rest, spot = jnp.float32(-30000.0 * LOG2E), lax.broadcasted_iota(jnp.int32, (EXTRA, 1), 0)
     fill = jnp.zeros((EXTRA, 1), F32)
@@ -457,7 +460,7 @@
     dead = jnp.where(alive, 0.0, fill).astype(BF16)
 
     mask = jnp.concatenate([live, dead], axis=0)
-    expo, kv, num, stats = forward(at, 13, tokens, pair_bias, q, w_key, w_value, mask, row, dh)
+    expo, kv, num, stats = forward(at, 13, tokens, pair_bias, q, w_key, w_value, mask, dh)
     expo, kv, num = (pltpu.with_memory_space_constraint(a, pltpu.VMEM) for a in (expo, kv, num))
     chip = merge_pair(stats, lax.ppermute(stats, "col", other_core()))
     every = [chip] + [lax.ppermute(chip, "col", along_z(k)) for k in (1, 3, 2)]
@@ -469,10 +472,11 @@
     parts = add_split([mine, other])
     parts = [parts[0]] + [lax.ppermute(parts[k], "col", along_z(k)) for k in (1, 3, 2)]
     attended, rest = finish(parts, gate, d_hidden, w_out, w_gate)
-    attended = gather_col(at, 8, attended)
+    attended = gather_col(attended)
     from_kv = jnp.sum(from_kv.astype(F32), axis=0).astype(BF16)
     from_kv = lax.ppermute(from_kv, both, [(b, a) for a, b in home_to_block()])
-    d_single = gather_col(at, 8, total(from_kv, rest))
+    d_single = gather_col(total(from_kv, rest))
+    attended, d_single = join(at, 8, attended, d_single)
     return (attended, d_bias, d_single)
 
 

time: 124 us -> 123 us (level)
  waiting for transfers between devices: 22.6 us -> 25.2 us
  Pallas kernels: 34.3 us -> 32.6 us
    all_to_all x1, waiting for transfers between devices: 3.16 us -> 4.87 us  [shards(): lax.all_to_all(jnp.broadcast_to(tokens[None], (ROWS, *tokens.shape)), 'ro...]
    pallas_call x2 -> x1, Pallas kernels: 2.8 us -> 1.63 us  [join(): pl.pallas_call(functools.partial(join_kernel, first), out_shape=[array((s...]
  transfers between devices with their start and end apart: 26 -> 26, of which waited for: 11 -> 12; matrix products, arithmetic and copies ran while one was open for 4% -> 3% of each run, Pallas kernels for 5% -> 4%
where the time goes in v5:
time: 123 us; the launch traced here: 122 us
  starting transfers between devices  46.6 us (38%)
  Pallas kernels  32.6 us (27%)
  waiting for transfers between devices  25.2 us (20%)
  local copies, waits for them, and re-layouts  14.1 us (11%)
  other arithmetic  2.21 us (2%)
  between operations  1.3 us (1%)
    pallas_call x1, Pallas kernels, backward(): pl.pallas_call(functools.partial(backward_kernel, first), out_shape=[arra...  13.6 us
    pallas_call x1, Pallas kernels, forward(): pl.pallas_call(functools.partial(forward_kernel, first), out_shape=(pltpu...  12.7 us
    unnamed x44, local copies, waits for them, and re-layouts  10.5 us
    ppermute x1, starting transfers between devices, shards(): tokens = lax.ppermute(own[0], both, home_to_block())  6.5 us
    all_to_all x1, starting transfers between devices, shards(): lax.all_to_all(jnp.broadcast_to(tokens[None], (ROWS, *tokens.shape)), 'ro...  6.32 us
    ppermute x6, starting transfers between devices, gather_col(): near = [end] + [lax.ppermute(end, 'col', along_z(k)) for k in (1, 2, 3)]  6.25 us
    ppermute x3, waiting for transfers between devices, shards(): lax.ppermute(parts[k], 'col', along_z(k))  6.11 us
    ppermute x8, starting transfers between devices, gather_col(): return near + [lax.ppermute(end, 'col', other_core()) for end in near]  5.58 us
  transfers between devices with their start and end apart: 26, of which 12 were waited for; matrix products, arithmetic and copies ran while one was open for 3% of the time, Pallas kernels for 4%

profile of v5, /device:TPU:1, one launch (start us, length us, event | category | flops | bytes accessed | tf_op | source)
XLA Modules:
  0.0 122.0 jit_solution(12321271335595154686)
XLA Ops:
  1.5 6.5 %collective-permute-start = (bf16[48,768]{1,0:T(8,128)(2,1)S(1)}, bf16[48,768]{1,0:T(8,128)(2,1)S(1)}, u32[]{:S(2)}, u32[]{:S(2)}) collective-permute-start(bf16[48,768]{1,0:T(8,128)(2,1)S(1)} %constant_dynamic-slice_fusion.1.own_ref), channel_id=1, source_target_pairs={{4,0},{29,1},{32,2},{57,3},{68,4},{93,5},{96,6},{121,7},{12,8},{21... | collective-permute-start | bytes 221192 | tf_op jit(solution)/shard_map/ppermute | solution.py:449
  8.7 1.2 %collective-permute-done = bf16[48,768]{1,0:T(8,128)(2,1)S(1)} collective-permute-done((bf16[48,768]{1,0:T(8,128)(2,1)S(1)}, bf16[48,768]{1,0:T(8,128)(2,1)S(1)}, u32[]{:S(2)}, u32[]{:S(2)}) %collective-permute-start) | collective-permute-done | bytes 73760 | tf_op jit(solution)/shard_map/ppermute | solution.py:449
  9.9 1.1 broadcast_in_dim.43
  11.0 6.3 %all-to-all-start = ((bf16[16,48,768]{2,1,0:T(8,128)(2,1)}), bf16[16,48,768]{2,1,0:T(8,128)(2,1)}, u32[]{:S(2)}, u32[]{:S(2)}) async-start(bf16[16,48,768]{2,1,0:T(8,128)(2,1)} %broadcast_in_dim.43), calls=%async_computation | async-start | bytes 2359296 | tf_op jit(solution)/shard_map/all_to_all | solution.py:450
  19.7 1.1 copy-done.5
  21.7 2.5 %shard_map.112 = (bf16[768,384]{1,0:T(8,128)(2,1)S(1)}, bf16[768,384]{1,0:T(8,128)(2,1)S(1)}, f32[48,768]{1,0:T(8,128)S(1)}, f32[48,768]{1,0:T(8,128)S(1)}) custom-call(bf16[384,768]{1,0:T(8,128)(2,1)S(1)} %copy-done.4, bf16[384,768]{1,0:T(8,128)(2,1)S(1)} %copy-done.5, bf16[48,768]{1,0:T(8,128)(2,1)S(1)} %copy-done.8, ...), custom_call_target="tpu_custom_call" | custom-call | tf_op jit(solution)/shard_map/pallas_call | solution.py:322
  28.7 4.9 %all-to-all-done.refs_0_ = bf16[16,48,768]{2,1,0:T(8,128)(2,1)} async-done(((bf16[16,48,768]{2,1,0:T(8,128)(2,1)}), bf16[16,48,768]{2,1,0:T(8,128)(2,1)}, u32[]{:S(2)}, u32[]{:S(2)}) %all-to-all-start) | async-done | bytes 1179680 | tf_op jit(solution)/shard_map/all_to_all | solution.py:450
  33.5 12.7 %shard_map.113 = (bf16[16,384,768]{2,1,0:T(8,128)(2,1)S(1)}, bf16[1536,768]{1,0:T(8,128)(2,1)S(1)}, f32[768,384]{1,0:T(8,128)S(1)}, f32[48,384]{1,0:T(8,128)}) custom-call(s32[29]{0:T(128)} %concatenate.6.at_ref, bf16[16,48,768]{2,1,0:T(8,128)(2,1)} %all-to-all-done.refs_0_, bf16[16,384,768]{2,1,0:T(8,128)(2,1)} %refs_1_.1, bf16[768,384]{1,0:T(8,128)(2,1)} %copy-done.16, ...), custom_call_target="tpu_custom_call" | custom-call | flops 4831838208 | bytes 18874368 | tf_op jit(solution)/shard_map/pallas_call | solution.py:161
  46.3 4.0 %collective-permute-start.1 = (f32[48,384]{1,0:T(8,128)}, f32[48,384]{1,0:T(8,128)S(1)}, u32[]{:S(2)}, u32[]{:S(2)}) collective-permute-start(f32[48,384]{1,0:T(8,128)} %get-tuple-element.27.left_ref.refs_0_), channel_id=1, source_target_pairs={{0,1},{1,0},{2,3},{3,2},{4,5},{5,4},{6,7},{7,6},{8,9},{9,8},{10,11... | collective-permute-start | bytes 221192 | tf_op jit(solution)/shard_map/ppermute | solution.py:465
  50.3 1.1 collective-permute-done.1.right_ref
  52.3 2.0 %collective-permute-start.4 = (f32[48,384]{1,0:T(8,128)S(1)}, f32[48,384]{1,0:T(8,128)S(1)}, u32[]{:S(2)}, u32[]{:S(2)}) collective-permute-start(f32[48,384]{1,0:T(8,128)S(1)} %shard_map.114.refs_1_), channel_id=1, source_target_pairs={{0,4},{1,5},{2,6},{3,7},{4,0},{5,1},{6,2},{7,3},{8,12},{9,13},{10,... | collective-permute-start | bytes 221192 | tf_op jit(solution)/shard_map/ppermute | solution.py:466
  54.4 1.2 collective-permute-start.3
  55.9 1.3 %collective-permute-done.4.refs_4_ = f32[48,384]{1,0:T(8,128)S(1)} collective-permute-done((f32[48,384]{1,0:T(8,128)S(1)}, f32[48,384]{1,0:T(8,128)S(1)}, u32[]{:S(2)}, u32[]{:S(2)}) %collective-permute-start.4) | collective-permute-done | bytes 73760 | tf_op jit(solution)/shard_map/ppermute | solution.py:466
  57.1 2.1 %collective-permute-done.3.refs_3_ = f32[48,384]{1,0:T(8,128)S(1)} collective-permute-done((f32[48,384]{1,0:T(8,128)S(1)}, f32[48,384]{1,0:T(8,128)S(1)}, u32[]{:S(2)}, u32[]{:S(2)}) %collective-permute-start.3) | collective-permute-done | bytes 73760 | tf_op jit(solution)/shard_map/ppermute | solution.py:466
  60.6 13.6 %shard_map.115 = (bf16[16,384,768]{2,1,0:T(8,128)(2,1)}, bf16[768,384]{1,0:T(8,128)(2,1)}, bf16[16,48,768]{2,1,0:T(8,128)(2,1)}, f32[768,384]{1,0:T(8,128)}) custom-call(s32[29]{0:T(128)} %concatenate.6.at_ref, f32[48,384]{1,0:T(8,128)} %get-tuple-element.27.left_ref.refs_0_, f32[48,384]{1,0:T(8,128)} %copy-done.14, f32[48,384]{1,0:T(8,128)} %copy-done.21, ...), custom_call_target="tpu_custom_call" | custom-call | flops 9663676416 | bytes 18874368 | tf_op jit(solution)/shard_map/pallas_call | solution.py:288
  74.3 4.4 %all-to-all-start.1 = ((bf16[16,48,768]{2,1,0:T(8,128)(2,1)}), bf16[16,48,768]{2,1,0:T(8,128)(2,1)}, u32[]{:S(2)}, u32[]{:S(2)}) async-start(bf16[16,48,768]{2,1,0:T(8,128)(2,1)} %get-tuple-element.42), calls=%async_computation.1 | async-start | bytes 2359296 | tf_op jit(solution)/shard_map/all_to_all | solution.py:469
  78.7 1.3 %copy-done.3 = f32[768,384]{1,0:T(8,128)S(1)} copy-done((f32[768,384]{1,0:T(8,128)S(1)}, f32[768,384]{1,0:T(8,128)}, u32[]{:S(2)}) %copy-start.3) | copy-done | bytes 1179672
  81.0 1.3 %shard_map.116 = (bf16[384,768]{1,0:T(8,128)(2,1)S(1)}, bf16[384,768]{1,0:T(8,128)(2,1)S(1)}) custom-call(s32[29]{0:T(128)S(1)} %copy-done.15, bf16[768,384]{1,0:T(8,128)(2,1)S(1)} %copy-done.6, f32[768,384]{1,0:T(8,128)S(1)} %copy-done.3, bf16[768,768]{1,0:T(8,128)(2,1)S(1)} %copy-done), custom_call_target="tpu_custom_call" | custom-call | tf_op jit(solution)/shard_map/pallas_call | solution.py:364
  82.3 1.9 %collective-permute-start.5 = (bf16[384,768]{1,0:T(8,128)(2,1)S(1)}, bf16[384,768]{1,0:T(8,128)(2,1)S(1)}, u32[]{:S(2)}, u32[]{:S(2)}) collective-permute-start(bf16[384,768]{1,0:T(8,128)(2,1)S(1)} %get-tuple-element.34), channel_id=1, source_target_pairs={{0,1},{1,0},{2,3},{3,2},{4,5},{5,4},{6,7},{7,6},{8,9},{9,8},{10,11... | collective-permute-start | bytes 1769480 | tf_op jit(solution)/shard_map/ppermute | solution.py:471
  84.2 1.6 %collective-permute-done.5.right_ref = bf16[384,768]{1,0:T(8,128)(2,1)S(1)} collective-permute-done((bf16[384,768]{1,0:T(8,128)(2,1)S(1)}, bf16[384,768]{1,0:T(8,128)(2,1)S(1)}, u32[]{:S(2)}, u32[]{:S(2)}) %collective-permute-start.5) | collective-permute-done | bytes 589856 | tf_op jit(solution)/shard_map/ppermute | solution.py:471
  86.0 2.7 %collective-permute-start.7 = (bf16[96,768]{1,0:T(8,128)(2,1)S(1)}, bf16[96,768]{1,0:T(8,128)(2,1)S(1)}, u32[]{:S(2)}, u32[]{:S(2)}) collective-permute-start(bf16[96,768]{1,0:T(8,128)(2,1)S(1)} %get-tuple-element.37), channel_id=1, source_target_pairs={{0,6},{1,7},{2,0},{3,1},{4,2},{5,3},{6,4},{7,5},{8,14},{9,15},{10,... | collective-permute-start | bytes 442376 | tf_op jit(solution)/shard_map/ppermute | solution.py:473
  88.7 3.7 %collective-permute-done.6.refs_1_ = bf16[96,768]{1,0:T(8,128)(2,1)S(1)} collective-permute-done((bf16[96,768]{1,0:T(8,128)(2,1)S(1)}, bf16[96,768]{1,0:T(8,128)(2,1)S(1)}, u32[]{:S(2)}, u32[]{:S(2)}) %collective-permute-start.6) | collective-permute-done | bytes 147488 | tf_op jit(solution)/shard_map/ppermute | solution.py:473
  92.4 2.4 %collective-permute-done.8.refs_3_ = bf16[96,768]{1,0:T(8,128)(2,1)S(1)} collective-permute-done((bf16[96,768]{1,0:T(8,128)(2,1)S(1)}, bf16[96,768]{1,0:T(8,128)(2,1)S(1)}, u32[]{:S(2)}, u32[]{:S(2)}) %collective-permute-start.8) | collective-permute-done | bytes 147488 | tf_op jit(solution)/shard_map/ppermute | solution.py:473
  95.5 3.4 %collective-permute-start.11 = (bf16[48,768]{1,0:T(8,128)(2,1)S(1)}, bf16[48,768]{1,0:T(8,128)(2,1)S(1)}, u32[]{:S(2)}, u32[]{:S(2)}) collective-permute-start(bf16[48,768]{1,0:T(8,128)(2,1)S(1)} %get-tuple-element.41.refs_0_), channel_id=1, source_target_pairs={{0,6},{1,7},{2,0},{3,1},{4,2},{5,3},{6,4},{7,5},{8,14},{9,15},{10,... | collective-permute-start | bytes 221192 | tf_op jit(solution)/shard_map/ppermute | solution.py:417
  98.8 1.4 %reduce_sum.12 = bf16[48,768]{1,0:T(8,128)(2,1)S(1)} reduce(bf16[16,48,768]{2,1,0:T(8,128)(2,1)} %all-to-all-done.1, bf16[]{:T(256)} %constant.302.clone.1), dimensions={0}, to_apply=%region_0.1 | reduce | flops 552960 | bytes 1253378 | tf_op jit(solution)/shard_map/reduce_sum | solution.py:476
  100.3 5.5 %collective-permute-start.16 = (bf16[48,768]{1,0:T(8,128)(2,1)S(1)}, bf16[48,768]{1,0:T(8,128)(2,1)S(1)}, u32[]{:S(2)}, u32[]{:S(2)}) collective-permute-start(bf16[48,768]{1,0:T(8,128)(2,1)S(1)} %reduce_sum.12), channel_id=1, source_target_pairs={{0,4},{1,29},{2,32},{3,57},{4,68},{5,93},{6,96},{7,121},{8,12},{9,... | collective-permute-start | bytes 221192 | tf_op jit(solution)/shard_map/ppermute | solution.py:477
  106.4 3.3 %collective-permute-done.16.kv_ref = bf16[48,768]{1,0:T(8,128)(2,1)S(1)} collective-permute-done((bf16[48,768]{1,0:T(8,128)(2,1)S(1)}, bf16[48,768]{1,0:T(8,128)(2,1)S(1)}, u32[]{:S(2)}, u32[]{:S(2)}) %collective-permute-start.16) | collective-permute-done | bytes 73760 | tf_op jit(solution)/shard_map/ppermute | solution.py:477
  109.7 2.2 %collective-permute-start.19 = (bf16[48,768]{1,0:T(8,128)(2,1)S(1)}, bf16[48,768]{1,0:T(8,128)(2,1)S(1)}, u32[]{:S(2)}, u32[]{:S(2)}) collective-permute-start(bf16[48,768]{1,0:T(8,128)(2,1)S(1)} %shard_map.119.refs_8_), channel_id=1, source_target_pairs={{0,6},{1,7},{2,0},{3,1},{4,2},{5,3},{6,4},{7,5},{8,14},{9,15},{10,... | collective-permute-start | bytes 221192 | tf_op jit(solution)/shard_map/ppermute | solution.py:417
  112.6 2.6 %collective-permute-start.13 = (bf16[48,768]{1,0:T(8,128)(2,1)S(1)}, bf16[48,768]{1,0:T(8,128)(2,1)S(1)}, u32[]{:S(2)}, u32[]{:S(2)}) collective-permute-start(bf16[48,768]{1,0:T(8,128)(2,1)S(1)} %collective-permute-done.9.refs_1_), channel_id=1, source_target_pairs={{0,1},{1,0},{2,3},{3,2},{4,5},{5,4},{6,7},{7,6},{8,9},{9,8},{10,11... | collective-permute-start | bytes 221192 | tf_op jit(solution)/shard_map/ppermute | solution.py:418
  115.7 1.9 %collective-permute-done.18.refs_10_ = bf16[48,768]{1,0:T(8,128)(2,1)S(1)} collective-permute-done((bf16[48,768]{1,0:T(8,128)(2,1)S(1)}, bf16[48,768]{1,0:T(8,128)(2,1)S(1)}, u32[]{:S(2)}, u32[]{:S(2)}) %collective-permute-start.18) | collective-permute-done | bytes 73760 | tf_op jit(solution)/shard_map/ppermute | solution.py:417
  118.3 1.2 collective-permute-start.21
  120.4 1.6 %shard_map.120 = (bf16[384,768]{1,0:T(8,128)(2,1)}, bf16[384,768]{1,0:T(8,128)(2,1)}) custom-call(s32[29]{0:T(128)S(1)} %copy-done.15, bf16[48,768]{1,0:T(8,128)(2,1)S(1)} %get-tuple-element.41.refs_0_, bf16[48,768]{1,0:T(8,128)(2,1)S(1)} %collective-permute-done.9.refs_1_, bf16[48,768]{1,0:T(8,128)(2,1)S(1)} %collective-permute-done.10.refs_2_, ...), custom_call_target="tpu_custom_call" | custom-call | tf_op jit(solution)/shard_map/pallas_call | solution.py:423
  (85 shorter events, 16.8 us)
Async XLA Ops:
  1.5 8.4 %collective-permute-start = (bf16[48,768]{1,0:T(8,128)(2,1)S(1)}, bf16[48,768]{1,0:T(8,128)(2,1)S(1)}, u32[]{:S(2)}, u32[]{:S(2)}) collective-permute-start(bf16[48,768]{1,0:T(8,128)(2,1)S(1)} %constant_dynamic-slice_fusion.1.own_ref), channel_id=1, source_target_pairs={{4,0},{29,1},{32,2},{57,3},{68,4},{93,5},{96,6},{121,7},{12,8},{21... | collective-permute-start | bytes 221192 | tf_op jit(solution)/shard_map/ppermute | solution.py:449
  9.9 8.8 %copy-start.2 = (bf16[768,768]{1,0:T(8,128)(2,1)S(1)}, bf16[768,768]{1,0:T(8,128)(2,1)}, u32[]{:S(2)}) copy-start(bf16[768,768]{1,0:T(8,128)(2,1)} %refs_6_.1) | copy-start | bytes 3538948
  11.0 7.7 %copy-start = (bf16[768,768]{1,0:T(8,128)(2,1)S(1)}, bf16[768,768]{1,0:T(8,128)(2,1)}, u32[]{:S(2)}) copy-start(bf16[768,768]{1,0:T(8,128)(2,1)} %w_ref.1) | copy-start | bytes 3538948
  11.0 7.7 %copy-start.1 = (bf16[768,768]{1,0:T(8,128)(2,1)S(1)}, bf16[768,768]{1,0:T(8,128)(2,1)}, u32[]{:S(2)}) copy-start(bf16[768,768]{1,0:T(8,128)(2,1)} %refs_7_.1) | copy-start | bytes 3538948
  11.0 22.5 %all-to-all-start = ((bf16[16,48,768]{2,1,0:T(8,128)(2,1)}), bf16[16,48,768]{2,1,0:T(8,128)(2,1)}, u32[]{:S(2)}, u32[]{:S(2)}) async-start(bf16[16,48,768]{2,1,0:T(8,128)(2,1)} %broadcast_in_dim.43), calls=%async_computation | async-start | bytes 2359296 | tf_op jit(solution)/shard_map/all_to_all | solution.py:450
  46.3 5.1 %collective-permute-start.1 = (f32[48,384]{1,0:T(8,128)}, f32[48,384]{1,0:T(8,128)S(1)}, u32[]{:S(2)}, u32[]{:S(2)}) collective-permute-start(f32[48,384]{1,0:T(8,128)} %get-tuple-element.27.left_ref.refs_0_), channel_id=1, source_target_pairs={{0,1},{1,0},{2,3},{3,2},{4,5},{5,4},{6,7},{7,6},{8,9},{9,8},{10,11... | collective-permute-start | bytes 221192 | tf_op jit(solution)/shard_map/ppermute | solution.py:465
  52.3 7.6 %copy-start.14 = (f32[48,384]{1,0:T(8,128)}, f32[48,384]{1,0:T(8,128)S(1)}, u32[]{:S(2)}) copy-start(f32[48,384]{1,0:T(8,128)S(1)} %shard_map.114.refs_1_) | copy-start | bytes 221188
  52.3 4.8 %collective-permute-start.4 = (f32[48,384]{1,0:T(8,128)S(1)}, f32[48,384]{1,0:T(8,128)S(1)}, u32[]{:S(2)}, u32[]{:S(2)}) collective-permute-start(f32[48,384]{1,0:T(8,128)S(1)} %shard_map.114.refs_1_), channel_id=1, source_target_pairs={{0,4},{1,5},{2,6},{3,7},{4,0},{5,1},{6,2},{7,3},{8,12},{9,13},{10,... | collective-permute-start | bytes 221192 | tf_op jit(solution)/shard_map/ppermute | solution.py:466
  54.4 4.8 %collective-permute-start.3 = (f32[48,384]{1,0:T(8,128)S(1)}, f32[48,384]{1,0:T(8,128)S(1)}, u32[]{:S(2)}, u32[]{:S(2)}) collective-permute-start(f32[48,384]{1,0:T(8,128)S(1)} %shard_map.114.refs_1_), channel_id=1, source_target_pairs={{0,6},{1,7},{2,0},{3,1},{4,2},{5,3},{6,4},{7,5},{8,14},{9,15},{10,... | collective-permute-start | bytes 221192 | tf_op jit(solution)/shard_map/ppermute | solution.py:466
  55.5 4.4 %collective-permute-start.2 = (f32[48,384]{1,0:T(8,128)S(1)}, f32[48,384]{1,0:T(8,128)S(1)}, u32[]{:S(2)}, u32[]{:S(2)}) collective-permute-start(f32[48,384]{1,0:T(8,128)S(1)} %shard_map.114.refs_1_), channel_id=1, source_target_pairs={{0,2},{1,3},{2,4},{3,5},{4,6},{5,7},{6,0},{7,1},{8,10},{9,11},{10,... | collective-permute-start | bytes 221192 | tf_op jit(solution)/shard_map/ppermute | solution.py:466
  74.3 24.6 %all-to-all-start.1 = ((bf16[16,48,768]{2,1,0:T(8,128)(2,1)}), bf16[16,48,768]{2,1,0:T(8,128)(2,1)}, u32[]{:S(2)}, u32[]{:S(2)}) async-start(bf16[16,48,768]{2,1,0:T(8,128)(2,1)} %get-tuple-element.42), calls=%async_computation.1 | async-start | bytes 2359296 | tf_op jit(solution)/shard_map/all_to_all | solution.py:469
  82.3 12.5 %copy-start.10 = (f32[48,768]{1,0:T(8,128)S(1)}, f32[48,768]{1,0:T(8,128)}, u32[]{:S(2)}) copy-start(f32[48,768]{1,0:T(8,128)} %copy-done.9) | copy-start | bytes 442372
  82.3 12.5 %copy-start.12 = (f32[48,768]{1,0:T(8,128)S(1)}, f32[48,768]{1,0:T(8,128)}, u32[]{:S(2)}) copy-start(f32[48,768]{1,0:T(8,128)} %copy-done.11) | copy-start | bytes 442372
  82.3 3.5 %collective-permute-start.5 = (bf16[384,768]{1,0:T(8,128)(2,1)S(1)}, bf16[384,768]{1,0:T(8,128)(2,1)S(1)}, u32[]{:S(2)}, u32[]{:S(2)}) collective-permute-start(bf16[384,768]{1,0:T(8,128)(2,1)S(1)} %get-tuple-element.34), channel_id=1, source_target_pairs={{0,1},{1,0},{2,3},{3,2},{4,5},{5,4},{6,7},{7,6},{8,9},{9,8},{10,11... | collective-permute-start | bytes 1769480 | tf_op jit(solution)/shard_map/ppermute | solution.py:471
  85.9 6.4 %collective-permute-start.6 = (bf16[96,768]{1,0:T(8,128)(2,1)S(1)}, bf16[96,768]{1,0:T(8,128)(2,1)S(1)}, u32[]{:S(2)}, u32[]{:S(2)}) collective-permute-start(bf16[96,768]{1,0:T(8,128)(2,1)S(1)} %get-tuple-element.36), channel_id=1, source_target_pairs={{0,2},{1,3},{2,4},{3,5},{4,6},{5,7},{6,0},{7,1},{8,10},{9,11},{10,... | collective-permute-start | bytes 442376 | tf_op jit(solution)/shard_map/ppermute | solution.py:473
  86.0 6.4 %collective-permute-start.7 = (bf16[96,768]{1,0:T(8,128)(2,1)S(1)}, bf16[96,768]{1,0:T(8,128)(2,1)S(1)}, u32[]{:S(2)}, u32[]{:S(2)}) collective-permute-start(bf16[96,768]{1,0:T(8,128)(2,1)S(1)} %get-tuple-element.37), channel_id=1, source_target_pairs={{0,6},{1,7},{2,0},{3,1},{4,2},{5,3},{6,4},{7,5},{8,14},{9,15},{10,... | collective-permute-start | bytes 442376 | tf_op jit(solution)/shard_map/ppermute | solution.py:473
  88.7 6.1 %collective-permute-start.8 = (bf16[96,768]{1,0:T(8,128)(2,1)S(1)}, bf16[96,768]{1,0:T(8,128)(2,1)S(1)}, u32[]{:S(2)}, u32[]{:S(2)}) collective-permute-start(bf16[96,768]{1,0:T(8,128)(2,1)S(1)} %get-tuple-element.38), channel_id=1, source_target_pairs={{0,4},{1,5},{2,6},{3,7},{4,0},{5,1},{6,2},{7,3},{8,12},{9,13},{10,... | collective-permute-start | bytes 442376 | tf_op jit(solution)/shard_map/ppermute | solution.py:473
  95.5 10.3 %collective-permute-start.11 = (bf16[48,768]{1,0:T(8,128)(2,1)S(1)}, bf16[48,768]{1,0:T(8,128)(2,1)S(1)}, u32[]{:S(2)}, u32[]{:S(2)}) collective-permute-start(bf16[48,768]{1,0:T(8,128)(2,1)S(1)} %get-tuple-element.41.refs_0_), channel_id=1, source_target_pairs={{0,6},{1,7},{2,0},{3,1},{4,2},{5,3},{6,4},{7,5},{8,14},{9,15},{10,... | collective-permute-start | bytes 221192 | tf_op jit(solution)/shard_map/ppermute | solution.py:417
  98.8 7.4 %collective-permute-start.10 = (bf16[48,768]{1,0:T(8,128)(2,1)S(1)}, bf16[48,768]{1,0:T(8,128)(2,1)S(1)}, u32[]{:S(2)}, u32[]{:S(2)}) collective-permute-start(bf16[48,768]{1,0:T(8,128)(2,1)S(1)} %get-tuple-element.41.refs_0_), channel_id=1, source_target_pairs={{0,4},{1,5},{2,6},{3,7},{4,0},{5,1},{6,2},{7,3},{8,12},{9,13},{10,... | collective-permute-start | bytes 221192 | tf_op jit(solution)/shard_map/ppermute | solution.py:417
  100.3 9.4 %collective-permute-start.16 = (bf16[48,768]{1,0:T(8,128)(2,1)S(1)}, bf16[48,768]{1,0:T(8,128)(2,1)S(1)}, u32[]{:S(2)}, u32[]{:S(2)}) collective-permute-start(bf16[48,768]{1,0:T(8,128)(2,1)S(1)} %reduce_sum.12), channel_id=1, source_target_pairs={{0,4},{1,29},{2,32},{3,57},{4,68},{5,93},{6,96},{7,121},{8,12},{9,... | collective-permute-start | bytes 221192 | tf_op jit(solution)/shard_map/ppermute | solution.py:477
  105.7 6.2 %collective-permute-start.12 = (bf16[48,768]{1,0:T(8,128)(2,1)S(1)}, bf16[48,768]{1,0:T(8,128)(2,1)S(1)}, u32[]{:S(2)}, u32[]{:S(2)}) collective-permute-start(bf16[48,768]{1,0:T(8,128)(2,1)S(1)} %get-tuple-element.41.refs_0_), channel_id=1, source_target_pairs={{0,1},{1,0},{2,3},{3,2},{4,5},{5,4},{6,7},{7,6},{8,9},{9,8},{10,11... | collective-permute-start | bytes 221192 | tf_op jit(solution)/shard_map/ppermute | solution.py:418
  105.7 6.2 %collective-permute-start.9 = (bf16[48,768]{1,0:T(8,128)(2,1)S(1)}, bf16[48,768]{1,0:T(8,128)(2,1)S(1)}, u32[]{:S(2)}, u32[]{:S(2)}) collective-permute-start(bf16[48,768]{1,0:T(8,128)(2,1)S(1)} %get-tuple-element.41.refs_0_), channel_id=1, source_target_pairs={{0,2},{1,3},{2,4},{3,5},{4,6},{5,7},{6,0},{7,1},{8,10},{9,11},{10,... | collective-permute-start | bytes 221192 | tf_op jit(solution)/shard_map/ppermute | solution.py:417
  105.7 6.9 %collective-permute-start.15 = (bf16[48,768]{1,0:T(8,128)(2,1)S(1)}, bf16[48,768]{1,0:T(8,128)(2,1)S(1)}, u32[]{:S(2)}, u32[]{:S(2)}) collective-permute-start(bf16[48,768]{1,0:T(8,128)(2,1)S(1)} %collective-permute-done.11.refs_3_), channel_id=1, source_target_pairs={{0,1},{1,0},{2,3},{3,2},{4,5},{5,4},{6,7},{7,6},{8,9},{9,8},{10,11... | collective-permute-start | bytes 221192 | tf_op jit(solution)/shard_map/ppermute | solution.py:418
  106.2 9.0 %collective-permute-start.14 = (bf16[48,768]{1,0:T(8,128)(2,1)S(1)}, bf16[48,768]{1,0:T(8,128)(2,1)S(1)}, u32[]{:S(2)}, u32[]{:S(2)}) collective-permute-start(bf16[48,768]{1,0:T(8,128)(2,1)S(1)} %collective-permute-done.10.refs_2_), channel_id=1, source_target_pairs={{0,1},{1,0},{2,3},{3,2},{4,5},{5,4},{6,7},{7,6},{8,9},{9,8},{10,11... | collective-permute-start | bytes 221192 | tf_op jit(solution)/shard_map/ppermute | solution.py:418
  109.7 5.6 %collective-permute-start.19 = (bf16[48,768]{1,0:T(8,128)(2,1)S(1)}, bf16[48,768]{1,0:T(8,128)(2,1)S(1)}, u32[]{:S(2)}, u32[]{:S(2)}) collective-permute-start(bf16[48,768]{1,0:T(8,128)(2,1)S(1)} %shard_map.119.refs_8_), channel_id=1, source_target_pairs={{0,6},{1,7},{2,0},{3,1},{4,2},{5,3},{6,4},{7,5},{8,14},{9,15},{10,... | collective-permute-start | bytes 221192 | tf_op jit(solution)/shard_map/ppermute | solution.py:417
  111.9 5.7 %collective-permute-start.18 = (bf16[48,768]{1,0:T(8,128)(2,1)S(1)}, bf16[48,768]{1,0:T(8,128)(2,1)S(1)}, u32[]{:S(2)}, u32[]{:S(2)}) collective-permute-start(bf16[48,768]{1,0:T(8,128)(2,1)S(1)} %shard_map.119.refs_8_), channel_id=1, source_target_pairs={{0,4},{1,5},{2,6},{3,7},{4,0},{5,1},{6,2},{7,3},{8,12},{9,13},{10,... | collective-permute-start | bytes 221192 | tf_op jit(solution)/shard_map/ppermute | solution.py:417
  111.9 6.3 %collective-permute-start.17 = (bf16[48,768]{1,0:T(8,128)(2,1)S(1)}, bf16[48,768]{1,0:T(8,128)(2,1)S(1)}, u32[]{:S(2)}, u32[]{:S(2)}) collective-permute-start(bf16[48,768]{1,0:T(8,128)(2,1)S(1)} %shard_map.119.refs_8_), channel_id=1, source_target_pairs={{0,2},{1,3},{2,4},{3,5},{4,6},{5,7},{6,0},{7,1},{8,10},{9,11},{10,... | collective-permute-start | bytes 221192 | tf_op jit(solution)/shard_map/ppermute | solution.py:417
  112.6 6.9 %collective-permute-start.13 = (bf16[48,768]{1,0:T(8,128)(2,1)S(1)}, bf16[48,768]{1,0:T(8,128)(2,1)S(1)}, u32[]{:S(2)}, u32[]{:S(2)}) collective-permute-start(bf16[48,768]{1,0:T(8,128)(2,1)S(1)} %collective-permute-done.9.refs_1_), channel_id=1, source_target_pairs={{0,1},{1,0},{2,3},{3,2},{4,5},{5,4},{6,7},{7,6},{8,9},{9,8},{10,11... | collective-permute-start | bytes 221192 | tf_op jit(solution)/shard_map/ppermute | solution.py:418
  115.2 4.3 %collective-permute-start.20 = (bf16[48,768]{1,0:T(8,128)(2,1)S(1)}, bf16[48,768]{1,0:T(8,128)(2,1)S(1)}, u32[]{:S(2)}, u32[]{:S(2)}) collective-permute-start(bf16[48,768]{1,0:T(8,128)(2,1)S(1)} %shard_map.119.refs_8_), channel_id=1, source_target_pairs={{0,1},{1,0},{2,3},{3,2},{4,5},{5,4},{6,7},{7,6},{8,9},{9,8},{10,11... | collective-permute-start | bytes 221192 | tf_op jit(solution)/shard_map/ppermute | solution.py:418
  115.3 4.2 %collective-permute-start.23 = (bf16[48,768]{1,0:T(8,128)(2,1)S(1)}, bf16[48,768]{1,0:T(8,128)(2,1)S(1)}, u32[]{:S(2)}, u32[]{:S(2)}) collective-permute-start(bf16[48,768]{1,0:T(8,128)(2,1)S(1)} %collective-permute-done.19.refs_11_), channel_id=1, source_target_pairs={{0,1},{1,0},{2,3},{3,2},{4,5},{5,4},{6,7},{7,6},{8,9},{9,8},{10,11... | collective-permute-start | bytes 221192 | tf_op jit(solution)/shard_map/ppermute | solution.py:418
  117.7 1.8 %collective-permute-start.22 = (bf16[48,768]{1,0:T(8,128)(2,1)S(1)}, bf16[48,768]{1,0:T(8,128)(2,1)S(1)}, u32[]{:S(2)}, u32[]{:S(2)}) collective-permute-start(bf16[48,768]{1,0:T(8,128)(2,1)S(1)} %collective-permute-done.18.refs_10_), channel_id=1, source_target_pairs={{0,1},{1,0},{2,3},{3,2},{4,5},{5,4},{6,7},{7,6},{8,9},{9,8},{10,11... | collective-permute-start | bytes 221192 | tf_op jit(solution)/shard_map/ppermute | solution.py:418
  118.3 2.1 %collective-permute-start.21 = (bf16[48,768]{1,0:T(8,128)(2,1)S(1)}, bf16[48,768]{1,0:T(8,128)(2,1)S(1)}, u32[]{:S(2)}, u32[]{:S(2)}) collective-permute-start(bf16[48,768]{1,0:T(8,128)(2,1)S(1)} %collective-permute-done.17.refs_9_), channel_id=1, source_target_pairs={{0,1},{1,0},{2,3},{3,2},{4,5},{5,4},{6,7},{7,6},{8,9},{9,8},{10,11... | collective-permute-start | bytes 221192 | tf_op jit(solution)/shard_map/ppermute | solution.py:418
  (16 other events, 24.7 us)

commit v6 on v5

--- a/solution.py
+++ b/solution.py
@@ -329,7 +329,7 @@
 
 
 def finish_kernel(*refs):
-    parts, (gate_ref, dhid_ref, wo_ref, wg_ref, att_ref, rest_ref) = refs[:SIDE], refs[SIDE:]
+    parts, (gate_ref, dhid_ref, wo_ref, wg_ref, _, att_ref, rest_ref) = refs[:SIDE], refs[SIDE:]
     size = gate_ref.shape[0]
     both = functools.reduce(jnp.add, [p[...].astype(F32) for p in parts])
     d_query, out, gate = both[:size], both[size:], gate_ref[...]
@@ -338,14 +338,14 @@
     rest_ref[...] = d_query + nt(d_gate, wg_ref[...])
 
 
-def finish(parts, gate, d_hidden, wo, wg):
+def finish(parts, gate, d_hidden, wo, wg, after):
     return pl.pallas_call(
         finish_kernel,
         out_shape=[array(gate.shape, BF16), array(gate.shape, F32)],
-        in_specs=whole(SIDE + 4),
+        in_specs=whole(SIDE + 4) + [HBM],
         out_specs=whole(2),
         compiler_params=params(),
-    )(*parts, gate, d_hidden, wo, wg)
+    )(*parts, gate, d_hidden, wo, wg, after)
 
 
 def query_kernel(first, at_ref, dq_ref, out_ref, w_ref, mine_ref, other_ref, total, turned):
@@ -471,9 +471,9 @@
     other = lax.ppermute(other, "col", other_core())
     parts = add_split([mine, other])
     parts = [parts[0]] + [lax.ppermute(parts[k], "col", along_z(k)) for k in (1, 3, 2)]
-    attended, rest = finish(parts, gate, d_hidden, w_out, w_gate)
+    from_kv = jnp.sum(from_kv.astype(F32), axis=0).astype(BF16)
+    attended, rest = finish(parts, gate, d_hidden, w_out, w_gate, from_kv)
     attended = gather_col(attended)
-    from_kv = jnp.sum(from_kv.astype(F32), axis=0).astype(BF16)
     from_kv = lax.ppermute(from_kv, both, [(b, a) for a, b in home_to_block()])
     d_single = gather_col(total(from_kv, rest))
     attended, d_single = join(at, 8, attended, d_single)

time: 123 us -> 124 us (level)
  waiting for transfers between devices: 25.2 us -> 21.6 us
  starting transfers between devices: 46.6 us -> 49.9 us
    ppermute x3, waiting for transfers between devices: 6.11 us -> 0.01 us  [shards(): lax.ppermute(parts[k], 'col', along_z(k))]
    all_to_all x1, waiting for transfers between devices: 0.01 us -> 5.38 us  [shards(): from_kv = lax.all_to_all(from_kv, 'row', 0, 0)]
    ppermute x8, starting transfers between devices: 5.58 us -> 8.89 us  [gather_col(): return near + [lax.ppermute(end, 'col', other_core()) for end in near]]
    ppermute x1, waiting for transfers between devices: 3.31 us -> 0.01 us  [shards(): from_kv = lax.ppermute(from_kv, both, [(b, a) for a, b in home_to_block()])]
    ppermute x1, starting transfers between devices: 5.45 us -> 2.23 us  [shards(): from_kv = lax.ppermute(from_kv, both, [(b, a) for a, b in home_to_block()])]
    ppermute x6, starting transfers between devices: 6.25 us -> 9.43 us  [gather_col(): near = [end] + [lax.ppermute(end, 'col', along_z(k)) for k in (1, 2, 3)]]
    unnamed x44 -> x48, local copies, waits for them, and re-layouts: 10.5 us -> 11.1 us
  transfers between devices with their start and end apart: 26 -> 26, of which waited for: 12 -> 13; matrix products, arithmetic and copies ran while one was open for 3% -> 4% of each run, Pallas kernels for 4% -> 4%
where the time goes in v6:
time: 124 us
  starting transfers between devices  49.9 us (40%)
  Pallas kernels  33.1 us (27%)
  waiting for transfers between devices  21.6 us (17%)
  local copies, waits for them, and re-layouts  14.7 us (12%)
  other arithmetic  2.86 us (2%)
  between operations  1.31 us (1%)
    pallas_call x1, Pallas kernels, backward(): pl.pallas_call(functools.partial(backward_kernel, first), out_shape=[arra...  13.6 us
    pallas_call x1, Pallas kernels, forward(): pl.pallas_call(functools.partial(forward_kernel, first), out_shape=(pltpu...  12.7 us
    unnamed x48, local copies, waits for them, and re-layouts  11.1 us
    ppermute x6, starting transfers between devices, gather_col(): near = [end] + [lax.ppermute(end, 'col', along_z(k)) for k in (1, 2, 3)]  9.43 us
    ppermute x8, starting transfers between devices, gather_col(): return near + [lax.ppermute(end, 'col', other_core()) for end in near]  8.89 us
    ppermute x1, starting transfers between devices, shards(): tokens = lax.ppermute(own[0], both, home_to_block())  6.5 us
    all_to_all x1, starting transfers between devices, shards(): lax.all_to_all(jnp.broadcast_to(tokens[None], (ROWS, *tokens.shape)), 'ro...  6.32 us
    all_to_all x1, waiting for transfers between devices, shards(): from_kv = lax.all_to_all(from_kv, 'row', 0, 0)  5.38 us
  transfers between devices with their start and end apart: 26, of which 13 were waited for; matrix products, arithmetic and copies ran while one was open for 4% of the time, Pallas kernels for 4%

profile of v6, /device:TPU:1, one launch (start us, length us, event | category | flops | bytes accessed | tf_op | source)
XLA Modules:
  0.0 123.5 jit_solution(15253989276468307453)
XLA Ops:
  1.5 6.5 %collective-permute-start = (bf16[48,768]{1,0:T(8,128)(2,1)S(1)}, bf16[48,768]{1,0:T(8,128)(2,1)S(1)}, u32[]{:S(2)}, u32[]{:S(2)}) collective-permute-start(bf16[48,768]{1,0:T(8,128)(2,1)S(1)} %constant_dynamic-slice_fusion.1.own_ref), channel_id=1, source_target_pairs={{4,0},{29,1},{32,2},{57,3},{68,4},{93,5},{96,6},{121,7},{12,8},{21... | collective-permute-start | bytes 221192 | tf_op jit(solution)/shard_map/ppermute | solution.py:449
  8.7 1.2 collective-permute-done
  9.9 1.1 broadcast_in_dim.43
  11.0 6.3 %all-to-all-start = ((bf16[16,48,768]{2,1,0:T(8,128)(2,1)}), bf16[16,48,768]{2,1,0:T(8,128)(2,1)}, u32[]{:S(2)}, u32[]{:S(2)}) async-start(bf16[16,48,768]{2,1,0:T(8,128)(2,1)} %broadcast_in_dim.43), calls=%async_computation | async-start | bytes 2359296 | tf_op jit(solution)/shard_map/all_to_all | solution.py:450
  19.7 1.1 copy-done.5
  21.7 2.5 %shard_map.112 = (bf16[768,384]{1,0:T(8,128)(2,1)S(1)}, bf16[768,384]{1,0:T(8,128)(2,1)S(1)}, f32[48,768]{1,0:T(8,128)S(1)}, f32[48,768]{1,0:T(8,128)S(1)}) custom-call(bf16[384,768]{1,0:T(8,128)(2,1)S(1)} %copy-done.4, bf16[384,768]{1,0:T(8,128)(2,1)S(1)} %copy-done.5, bf16[48,768]{1,0:T(8,128)(2,1)S(1)} %copy-done.8, ...), custom_call_target="tpu_custom_call" | custom-call | tf_op jit(solution)/shard_map/pallas_call | solution.py:322
  28.6 4.9 %all-to-all-done.refs_0_ = bf16[16,48,768]{2,1,0:T(8,128)(2,1)} async-done(((bf16[16,48,768]{2,1,0:T(8,128)(2,1)}), bf16[16,48,768]{2,1,0:T(8,128)(2,1)}, u32[]{:S(2)}, u32[]{:S(2)}) %all-to-all-start) | async-done | bytes 1179680 | tf_op jit(solution)/shard_map/all_to_all | solution.py:450
  33.5 12.7 %shard_map.113 = (bf16[16,384,768]{2,1,0:T(8,128)(2,1)S(1)}, bf16[1536,768]{1,0:T(8,128)(2,1)S(1)}, f32[768,384]{1,0:T(8,128)S(1)}, f32[48,384]{1,0:T(8,128)}) custom-call(s32[29]{0:T(128)} %concatenate.6.at_ref, bf16[16,48,768]{2,1,0:T(8,128)(2,1)} %all-to-all-done.refs_0_, bf16[16,384,768]{2,1,0:T(8,128)(2,1)} %refs_1_.1, bf16[768,384]{1,0:T(8,128)(2,1)} %copy-done.18, ...), custom_call_target="tpu_custom_call" | custom-call | flops 4831838208 | bytes 18874368 | tf_op jit(solution)/shard_map/pallas_call | solution.py:161
  46.3 4.0 %collective-permute-start.1 = (f32[48,384]{1,0:T(8,128)}, f32[48,384]{1,0:T(8,128)S(1)}, u32[]{:S(2)}, u32[]{:S(2)}) collective-permute-start(f32[48,384]{1,0:T(8,128)} %get-tuple-element.27.left_ref.refs_0_), channel_id=1, source_target_pairs={{0,1},{1,0},{2,3},{3,2},{4,5},{5,4},{6,7},{7,6},{8,9},{9,8},{10,11... | collective-permute-start | bytes 221192 | tf_op jit(solution)/shard_map/ppermute | solution.py:465
  50.3 1.1 collective-permute-done.1.right_ref
  52.3 2.0 %collective-permute-start.4 = (f32[48,384]{1,0:T(8,128)S(1)}, f32[48,384]{1,0:T(8,128)S(1)}, u32[]{:S(2)}, u32[]{:S(2)}) collective-permute-start(f32[48,384]{1,0:T(8,128)S(1)} %shard_map.114.refs_1_), channel_id=1, source_target_pairs={{0,4},{1,5},{2,6},{3,7},{4,0},{5,1},{6,2},{7,3},{8,12},{9,13},{10,... | collective-permute-start | bytes 221192 | tf_op jit(solution)/shard_map/ppermute | solution.py:466
  54.4 1.2 collective-permute-start.3
  55.9 1.2 collective-permute-done.4.refs_4_
  57.1 2.1 %collective-permute-done.3.refs_3_ = f32[48,384]{1,0:T(8,128)S(1)} collective-permute-done((f32[48,384]{1,0:T(8,128)S(1)}, f32[48,384]{1,0:T(8,128)S(1)}, u32[]{:S(2)}, u32[]{:S(2)}) %collective-permute-start.3) | collective-permute-done | bytes 73760 | tf_op jit(solution)/shard_map/ppermute | solution.py:466
  60.6 13.6 %shard_map.115 = (bf16[16,384,768]{2,1,0:T(8,128)(2,1)}, bf16[768,384]{1,0:T(8,128)(2,1)}, bf16[16,48,768]{2,1,0:T(8,128)(2,1)}, f32[768,384]{1,0:T(8,128)}) custom-call(s32[29]{0:T(128)} %concatenate.6.at_ref, f32[48,384]{1,0:T(8,128)} %get-tuple-element.27.left_ref.refs_0_, f32[48,384]{1,0:T(8,128)} %copy-done.16, f32[48,384]{1,0:T(8,128)} %copy-done.23, ...), custom_call_target="tpu_custom_call" | custom-call | flops 9663676416 | bytes 18874368 | tf_op jit(solution)/shard_map/pallas_call | solution.py:288
  74.3 4.4 %all-to-all-start.1 = ((bf16[16,48,768]{2,1,0:T(8,128)(2,1)}), bf16[16,48,768]{2,1,0:T(8,128)(2,1)}, u32[]{:S(2)}, u32[]{:S(2)}) async-start(bf16[16,48,768]{2,1,0:T(8,128)(2,1)} %get-tuple-element.41), calls=%async_computation.1 | async-start | bytes 2359296 | tf_op jit(solution)/shard_map/all_to_all | solution.py:469
  78.7 1.3 %copy-done.3 = f32[768,384]{1,0:T(8,128)S(1)} copy-done((f32[768,384]{1,0:T(8,128)S(1)}, f32[768,384]{1,0:T(8,128)}, u32[]{:S(2)}) %copy-start.3) | copy-done | bytes 1179672
  81.0 1.3 %shard_map.116 = (bf16[384,768]{1,0:T(8,128)(2,1)S(1)}, bf16[384,768]{1,0:T(8,128)(2,1)S(1)}) custom-call(s32[29]{0:T(128)S(1)} %copy-done.17, bf16[768,384]{1,0:T(8,128)(2,1)S(1)} %copy-done.6, f32[768,384]{1,0:T(8,128)S(1)} %copy-done.3, bf16[768,768]{1,0:T(8,128)(2,1)S(1)} %copy-done), custom_call_target="tpu_custom_call" | custom-call | tf_op jit(solution)/shard_map/pallas_call | solution.py:364
  82.3 1.9 %collective-permute-start.5 = (bf16[384,768]{1,0:T(8,128)(2,1)S(1)}, bf16[384,768]{1,0:T(8,128)(2,1)S(1)}, u32[]{:S(2)}, u32[]{:S(2)}) collective-permute-start(bf16[384,768]{1,0:T(8,128)(2,1)S(1)} %get-tuple-element.34), channel_id=1, source_target_pairs={{0,1},{1,0},{2,3},{3,2},{4,5},{5,4},{6,7},{7,6},{8,9},{9,8},{10,11... | collective-permute-start | bytes 1769480 | tf_op jit(solution)/shard_map/ppermute | solution.py:471
  84.2 1.6 %collective-permute-done.5.right_ref = bf16[384,768]{1,0:T(8,128)(2,1)S(1)} collective-permute-done((bf16[384,768]{1,0:T(8,128)(2,1)S(1)}, bf16[384,768]{1,0:T(8,128)(2,1)S(1)}, u32[]{:S(2)}, u32[]{:S(2)}) %collective-permute-start.5) | collective-permute-done | bytes 589856 | tf_op jit(solution)/shard_map/ppermute | solution.py:471
  87.2 2.7 %collective-permute-start.7 = (bf16[96,768]{1,0:T(8,128)(2,1)S(1)}, bf16[96,768]{1,0:T(8,128)(2,1)S(1)}, u32[]{:S(2)}, u32[]{:S(2)}) collective-permute-start(bf16[96,768]{1,0:T(8,128)(2,1)S(1)} %get-tuple-element.37), channel_id=1, source_target_pairs={{0,6},{1,7},{2,0},{3,1},{4,2},{5,3},{6,4},{7,5},{8,14},{9,15},{10,... | collective-permute-start | bytes 442376 | tf_op jit(solution)/shard_map/ppermute | solution.py:473
  89.9 5.4 %all-to-all-done.1 = bf16[16,48,768]{2,1,0:T(8,128)(2,1)} async-done(((bf16[16,48,768]{2,1,0:T(8,128)(2,1)}), bf16[16,48,768]{2,1,0:T(8,128)(2,1)}, u32[]{:S(2)}, u32[]{:S(2)}) %all-to-all-start.1) | async-done | bytes 1179680 | tf_op jit(solution)/shard_map/all_to_all | solution.py:469
  95.2 2.1 %reduce_sum.12.refs_8_ = bf16[48,768]{1,0:T(8,128)(2,1)} reduce(bf16[16,48,768]{2,1,0:T(8,128)(2,1)} %all-to-all-done.1, bf16[]{:T(256)} %constant.302.clone.1), dimensions={0}, to_apply=%region_0.1 | reduce | flops 552960 | bytes 1253378 | tf_op jit(solution)/shard_map/reduce_sum | solution.py:474
  97.3 2.2 %collective-permute-start.16 = (bf16[48,768]{1,0:T(8,128)(2,1)}, bf16[48,768]{1,0:T(8,128)(2,1)S(1)}, u32[]{:S(2)}, u32[]{:S(2)}) collective-permute-start(bf16[48,768]{1,0:T(8,128)(2,1)} %reduce_sum.12.refs_8_), channel_id=1, source_target_pairs={{0,4},{1,29},{2,32},{3,57},{4,68},{5,93},{6,96},{7,121},{8,12},{9,... | collective-permute-start | bytes 221192 | tf_op jit(solution)/shard_map/ppermute | solution.py:477
  100.2 2.4 %collective-permute-start.12 = (bf16[48,768]{1,0:T(8,128)(2,1)S(1)}, bf16[48,768]{1,0:T(8,128)(2,1)S(1)}, u32[]{:S(2)}, u32[]{:S(2)}) collective-permute-start(bf16[48,768]{1,0:T(8,128)(2,1)S(1)} %get-tuple-element.42.refs_0_), channel_id=1, source_target_pairs={{0,1},{1,0},{2,3},{3,2},{4,5},{5,4},{6,7},{7,6},{8,9},{9,8},{10,11... | collective-permute-start | bytes 221192 | tf_op jit(solution)/shard_map/ppermute | solution.py:418
  102.6 2.0 %collective-permute-start.11 = (bf16[48,768]{1,0:T(8,128)(2,1)S(1)}, bf16[48,768]{1,0:T(8,128)(2,1)S(1)}, u32[]{:S(2)}, u32[]{:S(2)}) collective-permute-start(bf16[48,768]{1,0:T(8,128)(2,1)S(1)} %get-tuple-element.42.refs_0_), channel_id=1, source_target_pairs={{0,6},{1,7},{2,0},{3,1},{4,2},{5,3},{6,4},{7,5},{8,14},{9,15},{10,... | collective-permute-start | bytes 221192 | tf_op jit(solution)/shard_map/ppermute | solution.py:417
  105.2 1.7 %collective-permute-start.20 = (bf16[48,768]{1,0:T(8,128)(2,1)S(1)}, bf16[48,768]{1,0:T(8,128)(2,1)S(1)}, u32[]{:S(2)}, u32[]{:S(2)}) collective-permute-start(bf16[48,768]{1,0:T(8,128)(2,1)S(1)} %shard_map.119.refs_8_), channel_id=1, source_target_pairs={{0,1},{1,0},{2,3},{3,2},{4,5},{5,4},{6,7},{7,6},{8,9},{9,8},{10,11... | collective-permute-start | bytes 221192 | tf_op jit(solution)/shard_map/ppermute | solution.py:418
  106.9 6.2 %collective-permute-start.19 = (bf16[48,768]{1,0:T(8,128)(2,1)S(1)}, bf16[48,768]{1,0:T(8,128)(2,1)S(1)}, u32[]{:S(2)}, u32[]{:S(2)}) collective-permute-start(bf16[48,768]{1,0:T(8,128)(2,1)S(1)} %shard_map.119.refs_8_), channel_id=1, source_target_pairs={{0,6},{1,7},{2,0},{3,1},{4,2},{5,3},{6,4},{7,5},{8,14},{9,15},{10,... | collective-permute-start | bytes 221192 | tf_op jit(solution)/shard_map/ppermute | solution.py:417
  113.7 1.1 collective-permute-start.15
  114.9 1.3 %collective-permute-done.19.refs_11_ = bf16[48,768]{1,0:T(8,128)(2,1)S(1)} collective-permute-done((bf16[48,768]{1,0:T(8,128)(2,1)S(1)}, bf16[48,768]{1,0:T(8,128)(2,1)S(1)}, u32[]{:S(2)}, u32[]{:S(2)}) %collective-permute-start.19) | collective-permute-done | bytes 73760 | tf_op jit(solution)/shard_map/ppermute | solution.py:417
  117.9 2.2 %collective-permute-start.23 = (bf16[48,768]{1,0:T(8,128)(2,1)S(1)}, bf16[48,768]{1,0:T(8,128)(2,1)S(1)}, u32[]{:S(2)}, u32[]{:S(2)}) collective-permute-start(bf16[48,768]{1,0:T(8,128)(2,1)S(1)} %collective-permute-done.19.refs_11_), channel_id=1, source_target_pairs={{0,1},{1,0},{2,3},{3,2},{4,5},{5,4},{6,7},{7,6},{8,9},{9,8},{10,11... | collective-permute-start | bytes 221192 | tf_op jit(solution)/shard_map/ppermute | solution.py:418
  121.9 1.6 %shard_map.120 = (bf16[384,768]{1,0:T(8,128)(2,1)}, bf16[384,768]{1,0:T(8,128)(2,1)}) custom-call(s32[29]{0:T(128)S(1)} %copy-done.17, bf16[48,768]{1,0:T(8,128)(2,1)S(1)} %get-tuple-element.42.refs_0_, bf16[48,768]{1,0:T(8,128)(2,1)S(1)} %collective-permute-done.9.refs_1_, bf16[48,768]{1,0:T(8,128)(2,1)S(1)} %collective-permute-done.10.refs_2_, ...), custom_call_target="tpu_custom_call" | custom-call | tf_op jit(solution)/shard_map/pallas_call | solution.py:423
  (89 shorter events, 19.4 us)
Async XLA Ops:
  1.5 8.4 %collective-permute-start = (bf16[48,768]{1,0:T(8,128)(2,1)S(1)}, bf16[48,768]{1,0:T(8,128)(2,1)S(1)}, u32[]{:S(2)}, u32[]{:S(2)}) collective-permute-start(bf16[48,768]{1,0:T(8,128)(2,1)S(1)} %constant_dynamic-slice_fusion.1.own_ref), channel_id=1, source_target_pairs={{4,0},{29,1},{32,2},{57,3},{68,4},{93,5},{96,6},{121,7},{12,8},{21... | collective-permute-start | bytes 221192 | tf_op jit(solution)/shard_map/ppermute | solution.py:449
  9.9 8.8 %copy-start.2 = (bf16[768,768]{1,0:T(8,128)(2,1)S(1)}, bf16[768,768]{1,0:T(8,128)(2,1)}, u32[]{:S(2)}) copy-start(bf16[768,768]{1,0:T(8,128)(2,1)} %refs_6_.1) | copy-start | bytes 3538948
  11.0 7.7 %copy-start = (bf16[768,768]{1,0:T(8,128)(2,1)S(1)}, bf16[768,768]{1,0:T(8,128)(2,1)}, u32[]{:S(2)}) copy-start(bf16[768,768]{1,0:T(8,128)(2,1)} %w_ref.1) | copy-start | bytes 3538948
  11.0 7.7 %copy-start.1 = (bf16[768,768]{1,0:T(8,128)(2,1)S(1)}, bf16[768,768]{1,0:T(8,128)(2,1)}, u32[]{:S(2)}) copy-start(bf16[768,768]{1,0:T(8,128)(2,1)} %refs_7_.1) | copy-start | bytes 3538948
  11.0 22.5 %all-to-all-start = ((bf16[16,48,768]{2,1,0:T(8,128)(2,1)}), bf16[16,48,768]{2,1,0:T(8,128)(2,1)}, u32[]{:S(2)}, u32[]{:S(2)}) async-start(bf16[16,48,768]{2,1,0:T(8,128)(2,1)} %broadcast_in_dim.43), calls=%async_computation | async-start | bytes 2359296 | tf_op jit(solution)/shard_map/all_to_all | solution.py:450
  46.3 5.1 %collective-permute-start.1 = (f32[48,384]{1,0:T(8,128)}, f32[48,384]{1,0:T(8,128)S(1)}, u32[]{:S(2)}, u32[]{:S(2)}) collective-permute-start(f32[48,384]{1,0:T(8,128)} %get-tuple-element.27.left_ref.refs_0_), channel_id=1, source_target_pairs={{0,1},{1,0},{2,3},{3,2},{4,5},{5,4},{6,7},{7,6},{8,9},{9,8},{10,11... | collective-permute-start | bytes 221192 | tf_op jit(solution)/shard_map/ppermute | solution.py:465
  52.3 4.8 %collective-permute-start.4 = (f32[48,384]{1,0:T(8,128)S(1)}, f32[48,384]{1,0:T(8,128)S(1)}, u32[]{:S(2)}, u32[]{:S(2)}) collective-permute-start(f32[48,384]{1,0:T(8,128)S(1)} %shard_map.114.refs_1_), channel_id=1, source_target_pairs={{0,4},{1,5},{2,6},{3,7},{4,0},{5,1},{6,2},{7,3},{8,12},{9,13},{10,... | collective-permute-start | bytes 221192 | tf_op jit(solution)/shard_map/ppermute | solution.py:466
  54.4 4.8 %collective-permute-start.3 = (f32[48,384]{1,0:T(8,128)S(1)}, f32[48,384]{1,0:T(8,128)S(1)}, u32[]{:S(2)}, u32[]{:S(2)}) collective-permute-start(f32[48,384]{1,0:T(8,128)S(1)} %shard_map.114.refs_1_), channel_id=1, source_target_pairs={{0,6},{1,7},{2,0},{3,1},{4,2},{5,3},{6,4},{7,5},{8,14},{9,15},{10,... | collective-permute-start | bytes 221192 | tf_op jit(solution)/shard_map/ppermute | solution.py:466
  55.6 4.4 %collective-permute-start.2 = (f32[48,384]{1,0:T(8,128)S(1)}, f32[48,384]{1,0:T(8,128)S(1)}, u32[]{:S(2)}, u32[]{:S(2)}) collective-permute-start(f32[48,384]{1,0:T(8,128)S(1)} %shard_map.114.refs_1_), channel_id=1, source_target_pairs={{0,2},{1,3},{2,4},{3,5},{4,6},{5,7},{6,0},{7,1},{8,10},{9,11},{10,... | collective-permute-start | bytes 221192 | tf_op jit(solution)/shard_map/ppermute | solution.py:466
  74.3 21.0 %all-to-all-start.1 = ((bf16[16,48,768]{2,1,0:T(8,128)(2,1)}), bf16[16,48,768]{2,1,0:T(8,128)(2,1)}, u32[]{:S(2)}, u32[]{:S(2)}) async-start(bf16[16,48,768]{2,1,0:T(8,128)(2,1)} %get-tuple-element.41), calls=%async_computation.1 | async-start | bytes 2359296 | tf_op jit(solution)/shard_map/all_to_all | solution.py:469
  82.3 3.5 %collective-permute-start.5 = (bf16[384,768]{1,0:T(8,128)(2,1)S(1)}, bf16[384,768]{1,0:T(8,128)(2,1)S(1)}, u32[]{:S(2)}, u32[]{:S(2)}) collective-permute-start(bf16[384,768]{1,0:T(8,128)(2,1)S(1)} %get-tuple-element.34), channel_id=1, source_target_pairs={{0,1},{1,0},{2,3},{3,2},{4,5},{5,4},{6,7},{7,6},{8,9},{9,8},{10,11... | collective-permute-start | bytes 1769480 | tf_op jit(solution)/shard_map/ppermute | solution.py:471
  87.2 12.4 %copy-start.10 = (f32[48,768]{1,0:T(8,128)S(1)}, f32[48,768]{1,0:T(8,128)}, u32[]{:S(2)}) copy-start(f32[48,768]{1,0:T(8,128)} %copy-done.9) | copy-start | bytes 442372
  87.2 12.4 %copy-start.12 = (f32[48,768]{1,0:T(8,128)S(1)}, f32[48,768]{1,0:T(8,128)}, u32[]{:S(2)}) copy-start(f32[48,768]{1,0:T(8,128)} %copy-done.11) | copy-start | bytes 442372
  87.2 12.4 %copy-start.14 = (bf16[96,768]{1,0:T(8,128)(2,1)S(1)}, bf16[96,768]{1,0:T(8,128)(2,1)}, u32[]{:S(2)}) copy-start(bf16[96,768]{1,0:T(8,128)(2,1)} %copy-done.13) | copy-start | bytes 442372
  87.2 12.4 %collective-permute-start.6 = (bf16[96,768]{1,0:T(8,128)(2,1)}, bf16[96,768]{1,0:T(8,128)(2,1)S(1)}, u32[]{:S(2)}, u32[]{:S(2)}) collective-permute-start(bf16[96,768]{1,0:T(8,128)(2,1)} %get-tuple-element.36), channel_id=1, source_target_pairs={{0,2},{1,3},{2,4},{3,5},{4,6},{5,7},{6,0},{7,1},{8,10},{9,11},{10,... | collective-permute-start | bytes 442376 | tf_op jit(solution)/shard_map/ppermute | solution.py:473
  87.2 12.4 %collective-permute-start.7 = (bf16[96,768]{1,0:T(8,128)(2,1)S(1)}, bf16[96,768]{1,0:T(8,128)(2,1)S(1)}, u32[]{:S(2)}, u32[]{:S(2)}) collective-permute-start(bf16[96,768]{1,0:T(8,128)(2,1)S(1)} %get-tuple-element.37), channel_id=1, source_target_pairs={{0,6},{1,7},{2,0},{3,1},{4,2},{5,3},{6,4},{7,5},{8,14},{9,15},{10,... | collective-permute-start | bytes 442376 | tf_op jit(solution)/shard_map/ppermute | solution.py:473
  89.9 9.7 %collective-permute-start.8 = (bf16[96,768]{1,0:T(8,128)(2,1)S(1)}, bf16[96,768]{1,0:T(8,128)(2,1)S(1)}, u32[]{:S(2)}, u32[]{:S(2)}) collective-permute-start(bf16[96,768]{1,0:T(8,128)(2,1)S(1)} %get-tuple-element.38), channel_id=1, source_target_pairs={{0,4},{1,5},{2,6},{3,7},{4,0},{5,1},{6,2},{7,3},{8,12},{9,13},{10,... | collective-permute-start | bytes 442376 | tf_op jit(solution)/shard_map/ppermute | solution.py:473
  97.3 7.8 %collective-permute-start.16 = (bf16[48,768]{1,0:T(8,128)(2,1)}, bf16[48,768]{1,0:T(8,128)(2,1)S(1)}, u32[]{:S(2)}, u32[]{:S(2)}) collective-permute-start(bf16[48,768]{1,0:T(8,128)(2,1)} %reduce_sum.12.refs_8_), channel_id=1, source_target_pairs={{0,4},{1,29},{2,32},{3,57},{4,68},{5,93},{6,96},{7,121},{8,12},{9,... | collective-permute-start | bytes 221192 | tf_op jit(solution)/shard_map/ppermute | solution.py:477
  100.2 6.6 %collective-permute-start.12 = (bf16[48,768]{1,0:T(8,128)(2,1)S(1)}, bf16[48,768]{1,0:T(8,128)(2,1)S(1)}, u32[]{:S(2)}, u32[]{:S(2)}) collective-permute-start(bf16[48,768]{1,0:T(8,128)(2,1)S(1)} %get-tuple-element.42.refs_0_), channel_id=1, source_target_pairs={{0,1},{1,0},{2,3},{3,2},{4,5},{5,4},{6,7},{7,6},{8,9},{9,8},{10,11... | collective-permute-start | bytes 221192 | tf_op jit(solution)/shard_map/ppermute | solution.py:418
  102.6 10.5 %collective-permute-start.11 = (bf16[48,768]{1,0:T(8,128)(2,1)S(1)}, bf16[48,768]{1,0:T(8,128)(2,1)S(1)}, u32[]{:S(2)}, u32[]{:S(2)}) collective-permute-start(bf16[48,768]{1,0:T(8,128)(2,1)S(1)} %get-tuple-element.42.refs_0_), channel_id=1, source_target_pairs={{0,6},{1,7},{2,0},{3,1},{4,2},{5,3},{6,4},{7,5},{8,14},{9,15},{10,... | collective-permute-start | bytes 221192 | tf_op jit(solution)/shard_map/ppermute | solution.py:417
  104.6 8.5 %collective-permute-start.10 = (bf16[48,768]{1,0:T(8,128)(2,1)S(1)}, bf16[48,768]{1,0:T(8,128)(2,1)S(1)}, u32[]{:S(2)}, u32[]{:S(2)}) collective-permute-start(bf16[48,768]{1,0:T(8,128)(2,1)S(1)} %get-tuple-element.42.refs_0_), channel_id=1, source_target_pairs={{0,4},{1,5},{2,6},{3,7},{4,0},{5,1},{6,2},{7,3},{8,12},{9,13},{10,... | collective-permute-start | bytes 221192 | tf_op jit(solution)/shard_map/ppermute | solution.py:417
  104.6 9.1 %collective-permute-start.9 = (bf16[48,768]{1,0:T(8,128)(2,1)S(1)}, bf16[48,768]{1,0:T(8,128)(2,1)S(1)}, u32[]{:S(2)}, u32[]{:S(2)}) collective-permute-start(bf16[48,768]{1,0:T(8,128)(2,1)S(1)} %get-tuple-element.42.refs_0_), channel_id=1, source_target_pairs={{0,2},{1,3},{2,4},{3,5},{4,6},{5,7},{6,0},{7,1},{8,10},{9,11},{10,... | collective-permute-start | bytes 221192 | tf_op jit(solution)/shard_map/ppermute | solution.py:417
  105.2 9.6 %collective-permute-start.20 = (bf16[48,768]{1,0:T(8,128)(2,1)S(1)}, bf16[48,768]{1,0:T(8,128)(2,1)S(1)}, u32[]{:S(2)}, u32[]{:S(2)}) collective-permute-start(bf16[48,768]{1,0:T(8,128)(2,1)S(1)} %shard_map.119.refs_8_), channel_id=1, source_target_pairs={{0,1},{1,0},{2,3},{3,2},{4,5},{5,4},{6,7},{7,6},{8,9},{9,8},{10,11... | collective-permute-start | bytes 221192 | tf_op jit(solution)/shard_map/ppermute | solution.py:418
  106.9 9.3 %collective-permute-start.19 = (bf16[48,768]{1,0:T(8,128)(2,1)S(1)}, bf16[48,768]{1,0:T(8,128)(2,1)S(1)}, u32[]{:S(2)}, u32[]{:S(2)}) collective-permute-start(bf16[48,768]{1,0:T(8,128)(2,1)S(1)} %shard_map.119.refs_8_), channel_id=1, source_target_pairs={{0,6},{1,7},{2,0},{3,1},{4,2},{5,3},{6,4},{7,5},{8,14},{9,15},{10,... | collective-permute-start | bytes 221192 | tf_op jit(solution)/shard_map/ppermute | solution.py:417
  113.1 4.8 %collective-permute-start.18 = (bf16[48,768]{1,0:T(8,128)(2,1)S(1)}, bf16[48,768]{1,0:T(8,128)(2,1)S(1)}, u32[]{:S(2)}, u32[]{:S(2)}) collective-permute-start(bf16[48,768]{1,0:T(8,128)(2,1)S(1)} %shard_map.119.refs_8_), channel_id=1, source_target_pairs={{0,4},{1,5},{2,6},{3,7},{4,0},{5,1},{6,2},{7,3},{8,12},{9,13},{10,... | collective-permute-start | bytes 221192 | tf_op jit(solution)/shard_map/ppermute | solution.py:417
  113.1 7.0 %collective-permute-start.17 = (bf16[48,768]{1,0:T(8,128)(2,1)S(1)}, bf16[48,768]{1,0:T(8,128)(2,1)S(1)}, u32[]{:S(2)}, u32[]{:S(2)}) collective-permute-start(bf16[48,768]{1,0:T(8,128)(2,1)S(1)} %shard_map.119.refs_8_), channel_id=1, source_target_pairs={{0,2},{1,3},{2,4},{3,5},{4,6},{5,7},{6,0},{7,1},{8,10},{9,11},{10,... | collective-permute-start | bytes 221192 | tf_op jit(solution)/shard_map/ppermute | solution.py:417
  113.7 6.9 %collective-permute-start.15 = (bf16[48,768]{1,0:T(8,128)(2,1)S(1)}, bf16[48,768]{1,0:T(8,128)(2,1)S(1)}, u32[]{:S(2)}, u32[]{:S(2)}) collective-permute-start(bf16[48,768]{1,0:T(8,128)(2,1)S(1)} %collective-permute-done.11.refs_3_), channel_id=1, source_target_pairs={{0,1},{1,0},{2,3},{3,2},{4,5},{5,4},{6,7},{7,6},{8,9},{9,8},{10,11... | collective-permute-start | bytes 221192 | tf_op jit(solution)/shard_map/ppermute | solution.py:418
  114.8 5.8 %collective-permute-start.14 = (bf16[48,768]{1,0:T(8,128)(2,1)S(1)}, bf16[48,768]{1,0:T(8,128)(2,1)S(1)}, u32[]{:S(2)}, u32[]{:S(2)}) collective-permute-start(bf16[48,768]{1,0:T(8,128)(2,1)S(1)} %collective-permute-done.10.refs_2_), channel_id=1, source_target_pairs={{0,1},{1,0},{2,3},{3,2},{4,5},{5,4},{6,7},{7,6},{8,9},{9,8},{10,11... | collective-permute-start | bytes 221192 | tf_op jit(solution)/shard_map/ppermute | solution.py:418
  116.2 4.4 %collective-permute-start.13 = (bf16[48,768]{1,0:T(8,128)(2,1)S(1)}, bf16[48,768]{1,0:T(8,128)(2,1)S(1)}, u32[]{:S(2)}, u32[]{:S(2)}) collective-permute-start(bf16[48,768]{1,0:T(8,128)(2,1)S(1)} %collective-permute-done.9.refs_1_), channel_id=1, source_target_pairs={{0,1},{1,0},{2,3},{3,2},{4,5},{5,4},{6,7},{7,6},{8,9},{9,8},{10,11... | collective-permute-start | bytes 221192 | tf_op jit(solution)/shard_map/ppermute | solution.py:418
  117.9 3.1 %collective-permute-start.23 = (bf16[48,768]{1,0:T(8,128)(2,1)S(1)}, bf16[48,768]{1,0:T(8,128)(2,1)S(1)}, u32[]{:S(2)}, u32[]{:S(2)}) collective-permute-start(bf16[48,768]{1,0:T(8,128)(2,1)S(1)} %collective-permute-done.19.refs_11_), channel_id=1, source_target_pairs={{0,1},{1,0},{2,3},{3,2},{4,5},{5,4},{6,7},{7,6},{8,9},{9,8},{10,11... | collective-permute-start | bytes 221192 | tf_op jit(solution)/shard_map/ppermute | solution.py:418
  120.1 1.5 %collective-permute-start.22 = (bf16[48,768]{1,0:T(8,128)(2,1)S(1)}, bf16[48,768]{1,0:T(8,128)(2,1)S(1)}, u32[]{:S(2)}, u32[]{:S(2)}) collective-permute-start(bf16[48,768]{1,0:T(8,128)(2,1)S(1)} %collective-permute-done.18.refs_10_), channel_id=1, source_target_pairs={{0,1},{1,0},{2,3},{3,2},{4,5},{5,4},{6,7},{7,6},{8,9},{9,8},{10,11... | collective-permute-start | bytes 221192 | tf_op jit(solution)/shard_map/ppermute | solution.py:418
  120.6 1.3 %collective-permute-start.21 = (bf16[48,768]{1,0:T(8,128)(2,1)S(1)}, bf16[48,768]{1,0:T(8,128)(2,1)S(1)}, u32[]{:S(2)}, u32[]{:S(2)}) collective-permute-start(bf16[48,768]{1,0:T(8,128)(2,1)S(1)} %collective-permute-done.17.refs_9_), channel_id=1, source_target_pairs={{0,1},{1,0},{2,3},{3,2},{4,5},{5,4},{6,7},{7,6},{8,9},{9,8},{10,11... | collective-permute-start | bytes 221192 | tf_op jit(solution)/shard_map/ppermute | solution.py:418
  (18 other events, 33.1 us)
